TPU v7x, 32 devices: a whole 2x2x4 slice. The times are simulated.
32 devices in a mesh: gx: 4 (over y, x), gy: 8 (over z, core).
Axes of the slice: x: 2, y: 2, z: 4, core: 2. Of those that a mesh axis runs over, the one named last changes fastest.
Arguments:
- coarse: bfloat16 [12, 64, 256], P(None, ('gx', 'gy')), may hold values from -6 to 6
- weight_one: bfloat16 [3, 3, 12, 64], replicated, may hold values from -0.625 to 0.625
- weight_two: bfloat16 [3, 3, 64, 64], replicated, may hold values from -0.25 to 0.25
- weight_three: bfloat16 [3, 3, 64, 256], replicated, may hold values from -0.25 to 0.25
- weight_four: bfloat16 [3, 3, 64, 256], replicated, may hold values from -0.25 to 0.25
- weight_five: bfloat16 [3, 3, 64, 12], replicated, may hold values from -0.25 to 0.25
- bias_one: float32 [64], replicated, may hold values from -3 to 3
- bias_two: float32 [64], replicated, may hold values from -3 to 3
- bias_three: float32 [256], replicated, may hold values from -3 to 3
- bias_four: float32 [256], replicated, may hold values from -3 to 3
- bias_five: float32 [12], replicated, may hold values from -3 to 3
- cotangent: bfloat16 [12, 256, 1024], P(None, 'gx', 'gy'), may hold values from -6 to 6
Outputs:
- fine: float32 [12, 256, 1024], P(None, 'gx', 'gy')
- grad_w1: float32 [3, 3, 12, 64], replicated
- grad_w2: float32 [3, 3, 64, 64], replicated
- grad_w3: float32 [3, 3, 64, 256], replicated
- grad_w4: float32 [3, 3, 64, 256], replicated
- grad_w5: float32 [3, 3, 64, 12], replicated
- grad_b1: float32 [64], replicated
- grad_b2: float32 [64], replicated
- grad_b3: float32 [256], replicated
- grad_b4: float32 [256], replicated
- grad_b5: float32 [12], replicated
All inputs are finite; a program needn't handle non-finite values.
Results may differ from a plain program's by a relative error of at most 0.013.
Values may be sent and summed in bfloat16 or wider, within the bound.
No kernel may reach another device: no remote copies, remote signals or barrier semaphores. Data moves between devices by JAX's collectives and lax.ppermute only.
A program may use at most 128 MiB of HBM per device.

v0:
```python
import jax
import jax.numpy as jnp
from jax import lax
from jax.experimental import pallas as pl
from jax.experimental.pallas import tpu as pltpu
from jax.sharding import PartitionSpec as P

BF = jnp.bfloat16
F32 = jnp.float32

ROWS, COLS, PITCH, CHUNKS = 16, 32, 48, 32
CELLS = PITCH * CHUNKS
OWN = PITCH * 8
HALO = 6
FINE_HALO = 12
PACKED = 1408
GROUP0, GROUP5 = 6, 6
N1, N2, N3, N4 = 3, 5, 3, 4
M4, M3, M2, M1 = 4, 3, 4, 3
LIMIT = 12


def dotn(left, right):
    return lax.dot_general(left, right, (((1,), (0,)), ((), ())), preferred_element_type=F32)


def dott(left, right):
    return lax.dot_general(left, right, (((1,), (1,)), ((), ())), preferred_element_type=F32)


def take(ref, start, count, low=0, high=None):
    high = ref.shape[1] if high is None else high
    if not isinstance(start, int):
        start = pl.multiple_of(start, 16)
    return ref[pl.ds(start, count), low:high]


def taps(ref, start, count):
    return jnp.concatenate([take(ref, start + d, count) for d in (-PITCH, 0, PITCH)], axis=1)


def own(ref, low, high, row=0):
    block = ref[OWN + PITCH * row : OWN + PITCH * (row + ROWS), low:high]
    return block.reshape(ROWS, PITCH, high - low)[:, 16:48, :].reshape(ROWS * COLS, high - low)


def roll(value, by):
    return pltpu.roll(value, by % value.shape[0], 0)


def lane_roll(value, by):
    return pltpu.roll(value, by % value.shape[1], 1)


def grouped(first, last, group, work):
    def step(n, _):
        for k in range(group):
            work(first + n * group + k)
        return 0

    lax.fori_loop(0, (last - first) // group, step, 0)


def blocks(first, chunks_each, count, work):
    size = chunks_each * PITCH
    if count == 1:
        work(first * PITCH, size)
        return

    def step(n, _):
        work(pl.multiple_of(first * PITCH + n * size, 16), size)
        return 0

    lax.fori_loop(0, count, step, 0)


def clear_margins(fields):
    for ref, first, last in fields:
        ref[0 : first * PITCH, :] = jnp.zeros((first * PITCH, ref.shape[1]), BF)
        if last < CHUNKS:
            ref[last * PITCH :, :] = jnp.zeros((CELLS - last * PITCH, ref.shape[1]), BF)


def put(ref, start, size, value, low, high):
    ref[pl.ds(start, size), low:high] = value.astype(BF)


def row_of(t):
    return t % 2, PITCH * (t // 2)


def low_half():
    return lax.broadcasted_iota(jnp.int32, (1, 128), 1) < 64


def slope(act):
    act = act.astype(F32)
    return 1.0 - act * act


def split_dot(value, perm):
    high = value.astype(BF)
    rest = value - high.astype(F32)
    middle = rest.astype(BF)
    low = (rest - middle.astype(F32)).astype(BF)
    return (dotn(low, perm) + dotn(middle, perm)) + dotn(high, perm)


def grid(rows, cols):
    return tuple(lax.broadcasted_iota(jnp.int32, (rows, cols), n) for n in (0, 1))


def one_hot(chosen):
    return jnp.where(chosen, 1.0, 0.0).astype(BF)


def select(s0_ref, s5_ref, e_ref, turn3_ref, turn4_ref):
    m, lane = grid(PITCH, 64)
    for s in range(3):
        s0_ref[s * PITCH : (s + 1) * PITCH, :] = one_hot(lane == m + s + jnp.where(m < 8, 1, 9))
    m, lane = grid(PITCH, 160)
    wanted = jnp.where(m < 3, 4 * m + 1, jnp.where(m >= 13, 4 * m - 35, 1000))
    for u in range(6):
        s5_ref[u * PITCH : (u + 1) * PITCH, :] = one_hot(lane == wanted + u)
    cell, lane = grid(512, 512)
    e_ref[...] = one_hot(lane == ((cell >> 5) & 3) * 128 + (cell & 31) * 4 + (cell >> 7))
    new, old = grid(256, 256)
    turn3_ref[...] = one_hot(old == 4 * (new & 63) + 2 * (new >> 7) + 1 - ((new >> 6) & 1))
    turn4_ref[...] = one_hot(old == 4 * (new & 63) + 2 * ((new >> 6) & 1) + (new >> 7))


def small_terms(perms, small, bias_ref, bias5_ref):
    b1_ref, b2_ref, b3_ref, b4_ref, b5_ref = small
    perm3, perm4 = perms

    def wide(value):
        return jnp.broadcast_to(value, (8, value.shape[1]))

    bias_ref[0:8, 0:128] = wide(jnp.concatenate([b1_ref[...]] * 2, axis=1))
    bias_ref[8:16, 0:128] = wide(jnp.concatenate([b2_ref[...]] * 2, axis=1))
    bias_ref[16:24, 0:256] = split_dot(wide(b3_ref[...]), perm3)
    four = split_dot(wide(b4_ref[...]), perm4)
    bias_ref[24:32, :] = jnp.concatenate([four, four], axis=1)
    chans = b5_ref.shape[1]
    five = jnp.concatenate([b5_ref[...], jnp.zeros((1, 128 - chans), F32)], axis=1)
    five = sum(lane_roll(five, 16 * n) for n in range(8))
    bias5_ref[...] = jnp.concatenate([jnp.broadcast_to(five, (128, 128)).T] * 2, axis=0)


def arrange(perms, weights, there, back):
    w1_ref, w2_ref, w3_ref, w4_ref, w5_ref = weights
    k1, k2, k3, k4, k5, k5s = there
    r5, r4, r3, r2 = back
    perm3, perm4 = perms
    chans = w1_ref.shape[2]
    w3p = dotn(w3_ref[...], perm3).astype(BF)
    w4p = dotn(w4_ref[...], perm4).astype(BF)
    for ref in (k1, k2, k3, k4, k5, k5s, r4, r3, r2):
        ref[...] = jnp.zeros(ref.shape, BF)
    for r in range(3):
        for s in range(3):
            at = s * 128 + r * 16
            k1[at : at + chans, :] = jnp.concatenate([w1_ref[r, s]] * 2, axis=1)
        part = w2_ref[r * 192 : (r + 1) * 192, :]
        k2[r * 256 : r * 256 + 192, :] = jnp.concatenate([part, part], axis=1)
        k3[r * 256 : r * 256 + 192, :] = w3p[r * 192 : (r + 1) * 192, :]
        for q in range(2):
            k4[r * 256 + q * 64 : r * 256 + q * 64 + 192, q * 256 : (q + 1) * 256] = w4p[
                r * 192 : (r + 1) * 192, :
            ]
        for s in range(3):
            t = 2 - r
            tap = (3 * r + s) * 64
            block = w3p[tap : tap + 64, :]
            r3[s * 64 : (s + 1) * 64, t * 256 : (t + 1) * 256] = block
            small = w2_ref[tap : tap + 64, :]
            r2[s * 64 : (s + 1) * 64, t * 128 + 64 : t * 128 + 128] = small
            if s == 2:
                r3[192:256, t * 256 : (t + 1) * 256] = block
                r2[192:256, t * 128 + 64 : t * 128 + 128] = small
            block = w4p[tap : tap + 64, :]
            for q in range(2):
                for q_src in range(2):
                    at = t * 512 + q_src * 256
                    if q - q_src + 1 == s:
                        r4[(1 - q) * 64 : (2 - q) * 64, at : at + 256] = block
                    if q_src == 1 - q and s == 2 - 2 * q:
                        r4[128 + (1 - q) * 64 : 128 + (2 - q) * 64, at : at + 256] = block
    gap_rows = jnp.zeros((16 - chans, 64), F32)
    turned = []
    for s in range(3):
        column = []
        for r in (2, 1, 0):
            column += [w5_ref[r, s].astype(F32), gap_rows]
        turned.append(jnp.concatenate(column + [jnp.zeros((80, 64), F32)], axis=0))
    w5 = [value.T for value in turned]
    turned = [value.astype(BF) for value in turned]
    empty = jnp.zeros((64, 64), BF)
    for t in range(6):
        at = 64 if t == 0 else (1536 if t == 5 else 512 + ((t - 1) // 2) * 512 + ((t - 1) % 2) * 64)
        side = 64 if t == 0 else (384 if t == 5 else 128 + ((t - 1) // 2) * 128 + ((t - 1) % 2) * 64)
        for b in range(3):
            p = t - 2 + b
            if not 0 <= p < 4:
                continue
            for src in range(4):
                for q in range(max(src - 1, 0), min(src + 1, 3) + 1):
                    k5[q * 64 + p * 16 : q * 64 + p * 16 + 16, at + src * 128 : at + src * 128 + 64] = (
                        turned[src - q + 1][b * 16 : b * 16 + 16, :]
                    )
        rows = [lane_roll(w5[s], 16 * (t - 2)).astype(BF)[:, :64] for s in (0, 2)]
        k5s[side : side + 64, :] = jnp.concatenate([rows[0], empty], axis=1)
        k5s[512 + side : 512 + side + 64, :] = jnp.concatenate([empty, rows[1]], axis=1)
    for p in range(4):
        for v in range(3):
            r5[p * 64 : (p + 1) * 64, v * 128 : (v + 1) * 128] = lane_roll(w5[2 - v], 16 * p).astype(BF)


def in_plane(extent, pos_ref, mask):
    row0 = pos_ref[0]
    col0 = pos_ref[1]
    m = lax.broadcasted_iota(jnp.int32, (PITCH, 128), 0)
    col = col0 + jnp.where(m < 8, m + 32, m - 16)
    col_ok = jnp.logical_and(col >= 0, col < extent[1])
    for k in range(CHUNKS):
        row = row0 + jnp.where(m < 8, k - 9, k - 8)
        ok = jnp.logical_and(col_ok, jnp.logical_and(row >= 0, row < extent[0]))
        mask[k * PITCH : (k + 1) * PITCH, :] = jnp.where(ok, 1.0, 0.0)


def forward(
    extent,
    pos_ref,
    dx_ref,
    w1_hbm,
    w2_hbm,
    w3_hbm,
    w4_hbm,
    w5_hbm,
    b1_ref,
    b2_ref,
    b3_ref,
    b4_ref,
    b5_ref,
    mask,
    s5_ref,
    turn3_ref,
    turn4_ref,
    r5,
    r4,
    r3,
    r2,
    x0,
    x1,
    x2,
    x3,
    a3,
    a4,
    fine_ref,
    bias_ref,
    bias5_ref,
    s0_ref,
    e_ref,
    k1,
    k2,
    k3,
    k4,
    k5,
    k5s,
    w1_ref,
    w2_ref,
    w3_ref,
    w4_ref,
    w5_ref,
    sems,
):
    copies = [
        pltpu.make_async_copy(src, dst, sems.at[n])
        for n, (src, dst) in enumerate(
            (
                (w1_hbm, w1_ref),
                (w2_hbm, w2_ref),
                (w3_hbm, w3_ref),
                (w4_hbm, w4_ref),
                (w5_hbm, w5_ref),
            )
        )
    ]
    for copy in copies:
        copy.start()
    small = (b1_ref, b2_ref, b3_ref, b4_ref, b5_ref)
    select(s0_ref, s5_ref, e_ref, turn3_ref, turn4_ref)
    in_plane(extent, pos_ref, mask)
    low = low_half()
    clear_margins(((x0, 2, 32), (x1, 3, 30), (x2, 4, 29), (x3, 5, 29), (a4, 5, 29)))

    def coarse_chunk(k):
        lines = dx_ref[pl.ds(k - 2, 3)].reshape(48, 64)
        lines = jnp.concatenate([lines, jnp.zeros((80, 64), BF)], axis=0)
        moved = dott(s0_ref[...], lines).astype(BF)
        for s in range(3):
            x0[pl.ds(pl.multiple_of(k * PITCH, 16), PITCH), s * 128 : (s + 1) * 128] = moved[
                s * PITCH : (s + 1) * PITCH, :
            ]

    grouped(2, 32, GROUP0, coarse_chunk)
    for copy in copies:
        copy.wait()
    perms = (turn3_ref[...].T, turn4_ref[...].T)
    small_terms(perms, small, bias_ref, bias5_ref)
    arrange(
        perms,
        (w1_ref, w2_ref, w3_ref, w4_ref, w5_ref),
        (k1, k2, k3, k4, k5, k5s),
        (r5, r4, r3, r2),
    )

    def narrow(read, weight, bias_at, variants):
        def work(start, size):
            wide = size + 32
            z = dotn(read(start - 16, wide), weight[...])
            z = jnp.tanh(z + bias_ref[8 * bias_at : 8 * bias_at + 1, 0:128])
            z = z * take(mask, start - 16, wide)
            inner = slice(16, 16 + size)
            left = jnp.where(low, roll(z, 1), z)
            put(variants, start, size, left[inner], 0, 128)
            put(variants, start, size, roll(z, -1)[inner], 128, 256)

        return work

    blocks(3, 27 // N1, N1, narrow(lambda at, n: take(x0, at, n), k1, 0, x1))
    blocks(4, 25 // N2, N2, narrow(lambda at, n: taps(x1, at, n), k2, 1, x2))

    def conv_three(start, size):
        wide = size + 32
        z = dotn(taps(x2, start - 16, wide), k3[...])
        z = jnp.tanh(z + bias_ref[16:17, 0:256])
        ok = take(mask, start - 16, wide)
        inner = slice(16, 16 + size)
        for p in range(2):
            half = z[:, p * 128 : (p + 1) * 128] * ok
            left = jnp.where(low, roll(half, 1), half)
            right = jnp.where(low, half, roll(half, -1))
            put(x3, start, size, left[inner], p * 256, p * 256 + 128)
            put(x3, start, size, right[inner], p * 256 + 128, p * 256 + 256)
            put(a3, start, size, half[inner], p * 128, p * 128 + 128)

    blocks(5, 24 // N3, N3, conv_three)

    def conv_four(start, size):
        ok = take(mask, start, size)
        for p in range(2):
            lines = []
            for r in range(3):
                phase, by = row_of(p + r - 1)
                lines.append(take(x3, start + by, size, phase * 256, phase * 256 + 256))
            z = dotn(jnp.concatenate(lines, axis=1), k4[...])
            z = jnp.tanh(z + bias_ref[24:25, 0:512])
            for q in range(4):
                at = p * 512 + q * 128
                put(a4, start, size, z[:, q * 128 : (q + 1) * 128] * ok, at, at + 128)

    blocks(5, 24 // N4, N4, conv_four)

    size = ROWS * PITCH
    wide = size + 32
    at = OWN - 16
    side = []
    for low_lane in (384, 0):
        side.append(take(a4, at - PITCH, wide, 512 + low_lane, 640 + low_lane))
        side.append(take(a4, at, wide, low_lane, low_lane + 128))
        side.append(take(a4, at, wide, 512 + low_lane, 640 + low_lane))
        side.append(take(a4, at + PITCH, wide, low_lane, low_lane + 128))
    side = dotn(jnp.concatenate(side, axis=1), k5s[...])
    side = jnp.where(low, roll(side, 1), roll(side, -1))[16 : 16 + size]
    side = side.reshape(ROWS, PITCH, 128)[:, 16:48, :].reshape(ROWS * COLS, 128).T
    field = jnp.concatenate(
        [own(a4, 512, 1024, -1), own(a4, 0, 1024), own(a4, 0, 512, 1)], axis=1
    )
    z = dott(k5[...], field) + bias5_ref[:, 0:1]
    z = [z[0:64] + side[0:64], z[64:128], z[128:192], z[192:256] + side[64:128]]
    z = jnp.concatenate(
        [jnp.concatenate([z[q][:, g * 128 : (g + 1) * 128] for q in range(4)], axis=1) for g in range(4)],
        axis=0,
    )
    high = z.astype(BF)
    rest = (z - high.astype(F32)).astype(BF)
    z = dotn(rest, e_ref[...]) + dotn(high, e_ref[...])
    for g in range(4):
        for n in range(4):
            for p in range(4):
                fine_ref[16 * g + 4 * n + p] = z[
                    g * 64 + p * 16 : g * 64 + p * 16 + 16, n * 128 : (n + 1) * 128
                ]


def backward(
    scale,
    pos_ref,
    dc_ref,
    mask,
    s5_ref,
    turn3_ref,
    turn4_ref,
    r5,
    r4,
    r3,
    r2,
    x0,
    x1,
    x2,
    x3,
    a3,
    a4,
    keep_ref,
    send_ref,
    c5,
    b4,
    b3,
    b2,
    b1,
    g_ref,
):
    low = low_half()
    clear_margins(((c5, 5, 29), (b4, 5, 29), (b3, 6, 27), (b2, 7, 27)))

    def cot_chunk(k):
        lines = dc_ref[pl.ds(4 * (k - 5), 6)].reshape(96, 160)
        lines = jnp.concatenate([lines, jnp.zeros((32, 160), BF)], axis=0)
        moved = dott(s5_ref[...], lines).astype(BF)
        for u in range(6):
            c5[pl.ds(pl.multiple_of(k * PITCH, 16), PITCH), u * 128 : (u + 1) * 128] = moved[
                u * PITCH : (u + 1) * PITCH, :
            ]

    grouped(5, 29, GROUP5, cot_chunk)

    def back_four(start, size):
        ok = take(mask, start, size)
        for q in range(4):
            z = dott(take(c5, start, size, q * 128, q * 128 + 384), r5[...])
            for p in range(2):
                at = p * 512 + q * 128
                z_p = z[:, p * 128 : (p + 1) * 128] * ok
                put(b4, start, size, z_p * slope(take(a4, start, size, at, at + 128)), at, at + 128)

    blocks(5, 24 // M4, M4, back_four)

    def back_three(start, size):
        wide = size + 32
        ok = take(mask, start, size)
        inner = slice(16, 16 + size)
        for p in range(2):
            lines = []
            for t in range(3):
                phase, by = row_of(p + t - 1)
                lines.append(take(b4, start - 16 + by, wide, phase * 512, phase * 512 + 512))
            z = dott(jnp.concatenate(lines, axis=1), r4[...])
            moved = jnp.where(low, roll(z[:, 128:256], -1), roll(z[:, 128:256], 1))
            z = (z[:, 0:128] + moved)[inner] * ok
            at = p * 128
            put(b3, start, size, z * slope(take(a3, start, size, at, at + 128)), at, at + 128)

    blocks(6, 21 // M3, M3, back_three)

    def back_narrow(src, weight, act, out):
        def work(start, size):
            wide = size + 32
            z = dott(taps(src, start - 16, wide), weight[...])
            pair = jnp.where(low, roll(z[:, 0:128], -1), z[:, 0:128])
            z = pair + lane_roll(pair, 64) + roll(z[:, 128:256], 1)
            z = z[16 : 16 + size] * take(mask, start, size)
            z = jnp.where(low, 0.0, z * slope(take(act, start, size, 0, 128)))
            put(out, start, size, z, 0, 128)

        return work

    blocks(7, 20 // M2, M2, back_narrow(b3, r3, x2, b2))
    blocks(8, 18 // M1, M1, back_narrow(b2, r2, x1, b1))

    g_ref[PACKED - 64 :, :] = jnp.zeros((64, 256), F32)
    g_ref[1152:1344, 192:256] = jnp.zeros((192, 64), F32)

    back = own(b4, 0, 1024)
    sums4 = jnp.sum(back.astype(F32), axis=0, keepdims=True)
    back = back.T
    for r in range(3):
        total = None
        for p in range(2):
            phase, by = row_of(p + r - 1)
            field = own(x3, phase * 256, phase * 256 + 256, by // PITCH)
            term = dotn(back[p * 512 : (p + 1) * 512, :], field)
            total = term if total is None else total + term
        total = total[0:256, 0:192] + total[256:512, 64:256]
        g_ref[r * 192 : (r + 1) * 192, :] = split_dot(total.T * scale, turn4_ref[...])
    sums4 = sums4[:, 0:512] + sums4[:, 512:1024]
    sums4 = sums4[:, 0:256] + sums4[:, 256:512]

    back = own(b3, 0, 256)
    sums3 = jnp.sum(back.astype(F32), axis=0, keepdims=True)
    back = back.T
    for r in range(3):
        total = dotn(back, own(x2, 0, 256, r - 1))[:, 0:192]
        g_ref[576 + r * 192 : 576 + (r + 1) * 192, :] = split_dot(total.T * scale, turn3_ref[...])

    back = own(b2, 0, 128)
    sums2 = jnp.sum(back.astype(F32), axis=0, keepdims=True)
    back = back.T
    for r in range(3):
        total = dotn(back[64:128, :], own(x1, 0, 256, r - 1))
        g_ref[1152:1344, r * 64 : (r + 1) * 64] = total[:, 0:192].T * scale

    back = own(b1, 0, 128)
    sums1 = jnp.sum(back.astype(F32), axis=0, keepdims=True)
    back = back.T
    total = dotn(back[64:128, :], own(x0, 0, 384)).T * scale
    for s in range(3):
        g_ref[1152 + s * 48 : 1152 + (s + 1) * 48, 192:256] = total[s * 128 : s * 128 + 48, :]

    cot = own(c5, 0, 768)
    sums5 = jnp.sum(cot.astype(F32), axis=0, keepdims=True)
    cot = cot.T
    total = None
    for q in range(4):
        field = jnp.concatenate(
            [own(a4, q * 128, q * 128 + 128), own(a4, 512 + q * 128, 640 + q * 128)], axis=1
        )
        term = dotn(cot[q * 128 : q * 128 + 384, :], field)
        total = term if total is None else total + term
    total = total * scale
    for r in range(3):
        for s in range(3):
            sum_p = None
            for p in range(4):
                at = (2 - s) * 128 + (p + 2 - r) * 16
                term = total[at : at + 16, p * 64 : (p + 1) * 64]
                sum_p = term if sum_p is None else sum_p + term
            g_ref[1344 + s * 16 : 1344 + (s + 1) * 16, r * 64 : (r + 1) * 64] = sum_p

    sums5 = sums5[:, 128:256] + sums5[:, 256:384] + sums5[:, 384:512] + sums5[:, 512:640]
    five = sums5
    for t in range(1, 4):
        five = five + lane_roll(sums5, -16 * t)
    biases = [
        split_dot(jnp.broadcast_to(sums4 * scale, (8, 256)), turn4_ref[...])[0:1],
        split_dot(jnp.broadcast_to(sums3 * scale, (8, 256)), turn3_ref[...])[0:1],
        jnp.concatenate([sums2, sums1], axis=1) * scale,
        jnp.concatenate([five, jnp.zeros((1, 128), F32)], axis=1) * scale,
    ]
    for n, value in enumerate(biases):
        high = value.astype(BF).astype(F32)
        g_ref[1392 + 2 * n : 1393 + 2 * n, :] = high
        g_ref[1393 + 2 * n : 1394 + 2 * n, :] = value - high

    half = PACKED // 2
    core = pos_ref[2]
    keep_ref[...] = g_ref[pl.ds(pl.multiple_of(core * half, 16), half), :]
    send_ref[...] = g_ref[pl.ds(pl.multiple_of((1 - core) * half, 16), half), :].astype(BF)


def finish(chans, places, pos_ref, mine_ref, other_ref, g1, g2, g3, g4, g5, c1, c2, c3, c4, c5, full):
    half = PACKED // 2
    size = half // places
    core = pos_ref[2]
    for b in range(places):
        at = pl.multiple_of(lax.bitwise_xor(pos_ref[3], b) * size, 8)
        here = pl.multiple_of(core * half + b * size, 8)
        there = pl.multiple_of((1 - core) * half + b * size, 8)
        full[pl.ds(here, size), :] = mine_ref[pl.ds(at, size), :].astype(F32)
        full[pl.ds(there, size), :] = other_ref[pl.ds(at, size), :].astype(F32)
    g4[...] = full[0:576, :]
    g3[...] = full[576:1152, :]
    for r in range(3):
        g2[r * 192 : (r + 1) * 192, :] = full[1152:1344, r * 64 : (r + 1) * 64]
        for s in range(3):
            at = 1152 + s * 48 + r * 16
            g1[r, s] = full[at : at + chans, 192:256]
            at = 1344 + s * 16
            g5[r, s] = full[at : at + chans, r * 64 : (r + 1) * 64]
    sums = [full[1392 + 2 * n : 1393 + 2 * n, :] + full[1393 + 2 * n : 1394 + 2 * n, :] for n in range(4)]
    c4[...] = sums[0]
    c3[...] = sums[1]
    c2[...] = sums[2][:, 64:128]
    c1[...] = sums[2][:, 192:256]
    c5[...] = sums[3][:, 16 : 16 + chans]


def pairs(count, by):
    return [(i, i + by) for i in range(count) if 0 <= i + by < count]


def coarse_lines(coarse):
    gx, gy = lax.axis_size("gx"), lax.axis_size("gy")
    chans, each = coarse.shape[:2]
    cols = coarse.shape[2] // gy
    wide = cols + 2 * HALO
    tiles = coarse.reshape(chans, each, gy, cols).transpose(2, 1, 0, 3)
    before = jnp.pad(tiles[:-1, :, :, cols - HALO :], ((1, 0), (0, 0), (0, 0), (0, 0)))
    after = jnp.pad(tiles[1:, :, :, :HALO], ((0, 1), (0, 0), (0, 0), (0, 0)))
    pieces = jnp.concatenate([before, tiles, after], axis=3)
    got = lax.all_to_all(pieces, "gy", 0, 0, tiled=True).reshape(gy * each, chans, wide)
    above = lax.ppermute(got[-HALO:], "gx", pairs(gx, 1))
    below = lax.ppermute(got[:HALO], "gx", pairs(gx, -1))
    whole = jnp.concatenate([above, got, below])
    here, before = rows(whole, 1, 3), rows(whole, 2, 2)
    return jnp.concatenate([before[:, :, 36:44], gap(before, 12), here], axis=2)


def cotangent_lines(cotangent):
    gx, gy = lax.axis_size("gx"), lax.axis_size("gy")
    n = FINE_HALO
    left = lax.ppermute(cotangent[:, :, -n:].transpose(2, 0, 1), "gy", pairs(gy, 1))
    right = lax.ppermute(cotangent[:, :, :n].transpose(2, 0, 1), "gy", pairs(gy, -1))
    cot = jnp.concatenate(
        [left.transpose(2, 1, 0), cotangent.transpose(1, 0, 2), right.transpose(2, 1, 0)], axis=2
    )
    above = lax.ppermute(cot[-n:], "gx", pairs(gx, 1))
    below = lax.ppermute(cot[:n], "gx", pairs(gx, -1))
    whole = jnp.concatenate([above, cot, below])
    here, before = rows(whole, 1, 9), rows(whole, 5, 5)
    return jnp.concatenate([before[:, :, 138:152], gap(before, 4), here[:, :, :142]], axis=2)


def rows(value, low, high):
    return jnp.pad(value, ((low, high), (0, 4), (0, 0)))


def gap(value, count):
    return jnp.zeros(value.shape[:2] + (count,), BF)


def total_over_all(keep, send):
    gx, gy = lax.axis_size("gx"), lax.axis_size("gy")
    at_x = lax.axis_index("gx")

    def swap(block, axis, flip):
        count = lax.axis_size(axis)
        return lax.ppermute(block, axis, [(i, i ^ flip) for i in range(count)])

    def tree(terms):
        while len(terms) > 1:
            terms = [terms[n] + terms[n + 1] for n in range(0, len(terms), 2)]
        return terms[0]

    value = keep + swap(send, "gy", 1).astype(F32)
    size = value.shape[0] // gx

    def part(place):
        return lax.dynamic_slice_in_dim(value, place * size, size, 0)

    terms = [part(at_x)]
    for d in range(1, gx):
        terms.append(swap(part(at_x ^ d).astype(BF), "gx", d).astype(F32))
    block = tree(terms).astype(BF)
    terms = [block] + [swap(block, "gy", 2 * d) for d in range(1, gy // 2)]
    block = tree([term.astype(F32) for term in terms]).astype(BF)
    mine = jnp.concatenate([block] + [swap(block, "gx", d) for d in range(1, gx)])
    return mine, swap(mine, "gy", 1)


def local(
    coarse,
    weight_one,
    weight_two,
    weight_three,
    weight_four,
    weight_five,
    bias_one,
    bias_two,
    bias_three,
    bias_four,
    bias_five,
    cotangent,
):
    gx, gy = lax.axis_size("gx"), lax.axis_size("gy")
    chans = coarse.shape[0]
    tile_rows = coarse.shape[1] * gy
    tile_cols = coarse.shape[2] // gy
    assert (tile_rows, tile_cols) == (ROWS, COLS)
    at_x, at_y = lax.axis_index("gx"), lax.axis_index("gy")
    pos = jnp.stack([at_x * ROWS, at_y * COLS, at_y % 2, at_x]).astype(jnp.int32)
    extent = (ROWS * gx, COLS * gy)
    scale = float((16 * extent[0] * extent[1]) ** -0.5)

    smem = pl.BlockSpec(memory_space=pltpu.SMEM)
    vmem = pl.BlockSpec(memory_space=pltpu.VMEM)
    params = pltpu.CompilerParams(vmem_limit_bytes=LIMIT * 1024 * 1024)

    def near(value):
        return pltpu.with_memory_space_constraint(value, pltpu.VMEM)

    def buf(width, kind=BF):
        return pltpu.VMEM((CELLS, width), kind)

    shared = (
        buf(128, F32),
        pltpu.VMEM((6 * PITCH, 160), BF),
        pltpu.VMEM((256, 256), BF),
        pltpu.VMEM((256, 256), BF),
        pltpu.VMEM((256, 384), BF),
        pltpu.VMEM((256, 1536), BF),
        pltpu.VMEM((256, 768), BF),
        pltpu.VMEM((256, 384), BF),
        buf(384),
        buf(256),
        buf(256),
        buf(512),
        buf(256),
        buf(1024),
    )
    hbm = pl.BlockSpec(memory_space=pltpu.HBM)
    weights = (
        weight_one,
        weight_two.reshape(576, 64),
        weight_three.reshape(576, 256),
        weight_four.reshape(576, 256),
        weight_five.transpose(0, 1, 3, 2),
    )
    *fields, fine = pl.pallas_call(
        lambda *refs: forward(extent, *refs),
        out_shape=shared + (jax.ShapeDtypeStruct((4 * ROWS, 16, 4 * COLS), F32),),
        in_specs=[smem, vmem] + [hbm] * 5 + [vmem] * 5,
        out_specs=(vmem,) * 15,
        scratch_shapes=[
            pltpu.VMEM((32, 512), F32),
            pltpu.VMEM((256, 128), F32),
            pltpu.VMEM((3 * PITCH, 64), BF),
            pltpu.VMEM((512, 512), BF),
            pltpu.VMEM((384, 128), BF),
            pltpu.VMEM((768, 128), BF),
            pltpu.VMEM((768, 256), BF),
            pltpu.VMEM((768, 512), BF),
            pltpu.VMEM((256, 2048), BF),
            pltpu.VMEM((1024, 128), BF),
        ]
        + [pltpu.VMEM(w.shape, BF) for w in weights]
        + [pltpu.SemaphoreType.DMA((5,))],
        compiler_params=params,
        name="forward",
    )(
        pos,
        coarse_lines(coarse),
        *[pltpu.with_memory_space_constraint(w, pltpu.HBM) for w in weights],
        bias_one.reshape(1, -1),
        bias_two.reshape(1, -1),
        bias_three.reshape(1, -1),
        bias_four.reshape(1, -1),
        bias_five.reshape(1, -1),
    )
    fields = [near(f) for f in fields]
    half = PACKED // 2
    keep, send = pl.pallas_call(
        lambda *refs: backward(scale, *refs),
        out_shape=(pltpu.VMEM((half, 256), F32), pltpu.VMEM((half, 256), BF)),
        in_specs=[smem] + [vmem] * 15,
        out_specs=(vmem,) * 2,
        scratch_shapes=[
            buf(768),
            buf(1024),
            buf(256),
            buf(128),
            buf(128),
            pltpu.VMEM((PACKED, 256), F32),
        ],
        compiler_params=params,
        name="backward",
    )(pos, cotangent_lines(cotangent), *fields)
    mine, other = total_over_all(keep, send)

    def out(*shape):
        return jax.ShapeDtypeStruct(shape, F32)

    g1, g2, g3, g4, g5, c1, c2, c3, c4, c5 = pl.pallas_call(
        lambda *refs: finish(chans, gx, *refs),
        out_shape=(
            out(3, 3, chans, 64),
            out(576, 64),
            out(576, 256),
            out(576, 256),
            out(3, 3, chans, 64),
            out(1, 64),
            out(1, 64),
            out(1, 256),
            out(1, 256),
            out(1, chans),
        ),
        in_specs=[smem, vmem, vmem],
        out_specs=(vmem,) * 10,
        scratch_shapes=[pltpu.VMEM((PACKED, 256), F32)],
        compiler_params=params,
        name="finish",
    )(pos, mine, other)
    return (
        fine.transpose(1, 0, 2)[:chans],
        g1,
        g2.reshape(3, 3, 64, 64),
        g3.reshape(3, 3, 64, 256),
        g4.reshape(3, 3, 64, 256),
        g5.transpose(0, 1, 3, 2),
        c1.reshape(64),
        c2.reshape(64),
        c3.reshape(256),
        c4.reshape(256),
        c5.reshape(chans),
    )


def solution(mesh):
    in_specs = (
        P(None, ("gx", "gy"), None),
        P(),
        P(),
        P(),
        P(),
        P(),
        P(),
        P(),
        P(),
        P(),
        P(),
        P(None, "gx", "gy"),
    )
    out_specs = (P(None, "gx", "gy"), P(), P(), P(), P(), P(), P(), P(), P(), P(), P())
    return jax.shard_map(local, mesh=mesh, in_specs=in_specs, out_specs=out_specs, check_vma=False)
```

profile of v0, /device:TPU:0, one launch (start us, length us, event | category | flops | bytes accessed | tf_op | source)
XLA Modules:
  0.0 89.1 jit_solution(10065503715289433428)
XLA Ops:
  0.6 0.8 reshape.78
  1.5 0.1 fusion.7
  1.5 0.1 fusion.4
  1.7 0.7 reshape.96
  2.4 6.3 %all-to-all-start = ((bf16[8,2,528]{2,1,0:T(2,128)(2,1)}), bf16[8,2,528]{2,1,0:T(2,128)(2,1)S(1)}, u32[]{:S(2)}, u32[]{:S(2)}) async-start(bf16[8,2,528]{2,1,0:T(2,128)(2,1)} %reshape.96), calls=%async_computation | async-start | bytes 40960 | tf_op jit(solution)/shard_map/all_to_all | solution.py:601
  8.8 1.1 %copy.46 = bf16[12,64,128]{2,0,1:T(8,128)(2,1)S(1)} copy(bf16[12,64,128]{2,1,0:T(8,128)(2,1)} %param.23) | data formatting | bytes 393216 | tf_op args[11]
  9.9 0.1 slice_bitcast_fusion.1
  10.0 2.4 %collective-permute-start.2 = (bf16[12,12,64]{0,1,2:T(8,128)(2,1)S(1)}, bf16[12,12,64]{0,1,2:T(8,128)(2,1)S(1)}, u32[]{:S(2)}, u32[]{:S(2)}) collective-permute-start(bf16[12,12,64]{0,1,2:T(8,128)(2,1)S(1)} %get-tuple-element.103), channel_id=1, source_target_pairs={{0,1},{1,2},{2,3},{3,4},{4,5},{5,6},{6,7},{8,9},{9,10},{10,11},{11... | collective-permute-start | bytes 55304 | tf_op jit(solution)/shard_map/ppermute | solution.py:612
  12.5 1.3 %collective-permute-start.3 = (bf16[12,12,64]{0,1,2:T(8,128)(2,1)S(1)}, bf16[12,12,64]{0,1,2:T(8,128)(2,1)S(1)}, u32[]{:S(2)}, u32[]{:S(2)}) collective-permute-start(bf16[12,12,64]{0,1,2:T(8,128)(2,1)S(1)} %get-tuple-element.104), channel_id=1, source_target_pairs={{1,0},{2,1},{3,2},{4,3},{5,4},{6,5},{7,6},{9,8},{10,9},{11,10},{12... | collective-permute-start | bytes 55304 | tf_op jit(solution)/shard_map/ppermute | solution.py:613
  13.8 0.1 pad_add_fusion.refs_0_
  13.9 0.1 pad.46.clone
  13.9 0.1 pad.35.clone
  14.0 0.4 all-to-all-done
  14.4 0.1 reshape.97
  14.6 1.3 %collective-permute-start.1 = (bf16[6,12,44]{2,1,0:T(8,128)(2,1)S(1)}, bf16[6,12,44]{2,1,0:T(8,128)(2,1)S(1)}, u32[]{:S(2)}, u32[]{:S(2)}) collective-permute-start(bf16[6,12,44]{2,1,0:T(8,128)(2,1)S(1)} %bitcast.64), channel_id=1, source_target_pairs={{8,0},{16,8},{24,16},{9,1},{17,9},{25,17},{10,2},{18,10},{26,18},{... | collective-permute-start | bytes 19016 | tf_op jit(solution)/shard_map/ppermute | solution.py:603
  15.9 4.5 %collective-permute-start = (bf16[6,12,44]{2,1,0:T(8,128)(2,1)S(1)}, bf16[6,12,44]{2,1,0:T(8,128)(2,1)S(1)}, u32[]{:S(2)}, u32[]{:S(2)}) collective-permute-start(bf16[6,12,44]{2,1,0:T(8,128)(2,1)S(1)} %bitcast.63), channel_id=1, source_target_pairs={{0,8},{8,16},{16,24},{1,9},{9,17},{17,25},{2,10},{10,18},{18,26},{... | collective-permute-start | bytes 19016 | tf_op jit(solution)/shard_map/ppermute | solution.py:602
  20.5 0.2 pad_maximum_fusion.6
  20.7 4.3 %collective-permute-start.4 = (bf16[12,12,152]{2,1,0:T(8,128)(2,1)S(1)}, bf16[12,12,152]{2,1,0:T(8,128)(2,1)S(1)}, u32[]{:S(2)}, u32[]{:S(2)}) collective-permute-start(bf16[12,12,152]{2,1,0:T(8,128)(2,1)S(1)} %get-tuple-element.98), channel_id=1, source_target_pairs={{0,8},{8,16},{16,24},{1,9},{9,17},{17,25},{2,10},{10,18},{18,26},{... | collective-permute-start | bytes 131336 | tf_op jit(solution)/shard_map/ppermute | solution.py:617
  25.0 1.3 %collective-permute-start.5 = (bf16[12,12,152]{2,1,0:T(8,128)(2,1)S(1)}, bf16[12,12,152]{2,1,0:T(8,128)(2,1)S(1)}, u32[]{:S(2)}, u32[]{:S(2)}) collective-permute-start(bf16[12,12,152]{2,1,0:T(8,128)(2,1)S(1)} %get-tuple-element.99), channel_id=1, source_target_pairs={{8,0},{16,8},{24,16},{9,1},{17,9},{25,17},{10,2},{18,10},{26,18},{... | collective-permute-start | bytes 131336 | tf_op jit(solution)/shard_map/ppermute | solution.py:618
  26.3 0.1 pad_slice_fusion.2
  26.5 0.1 fusion.1.refs_1_
  26.6 11.5 %forward.1 = (f32[1536,128]{1,0:T(8,128)S(1)}, bf16[288,160]{1,0:T(8,128)(2,1)S(1)}, bf16[256,256]{1,0:T(8,128)(2,1)S(1)}, bf16[256,256]{1,0:T(8,128)(2,1)S(1)},...) custom-call(s32[4]{0:T(128)S(1)} %pad_add_fusion.refs_0_, ...), custom_call_target="tpu_custom_call" | custom-call | tf_op jit(solution)/shard_map/forward/pallas_call | solution.py:719
  38.2 0.4 pad_maximum_fusion.1
  38.5 0.2 pad_slice_fusion.1
  38.7 0.1 pad_slice_fusion
  38.9 0.5 pad_maximum_fusion.refs_1_
  39.4 14.5 %backward.1 = (f32[704,256]{1,0:T(8,128)S(1)}, bf16[704,256]{1,0:T(8,128)(2,1)S(1)}) custom-call(s32[4]{0:T(128)S(1)} %pad_add_fusion.refs_0_, bf16[98,16,160]{2,1,0:T(8,128)(2,1)S(1)} %pad_maximum_fusion.refs_1_, f32[1536,128]{1,0:T(8,128)S(1)} %get-tuple-element.39.refs_2_, bf16[288,160]{1,0:T(8,128)(2,1)S(1)} %get-tuple-element.40.refs_3_, ...), custom_call_target="tpu_custom_call" | custom-call | tf_op jit(solution)/shard_map/backward/pallas_call | solution.py:752
  53.9 1.1 %collective-permute-start.6 = (bf16[704,256]{1,0:T(8,128)(2,1)S(1)}, bf16[704,256]{1,0:T(8,128)(2,1)S(1)}, u32[]{:S(2)}, u32[]{:S(2)}) collective-permute-start(bf16[704,256]{1,0:T(8,128)(2,1)S(1)} %get-tuple-element.54), channel_id=1, source_target_pairs={{0,1},{1,0},{2,3},{3,2},{4,5},{5,4},{6,7},{7,6},{8,9},{9,8},{10,11... | collective-permute-start | bytes 1081352 | tf_op jit(solution)/shard_map/ppermute | solution.py:638
  54.9 1.3 %collective-permute-done.6 = bf16[704,256]{1,0:T(8,128)(2,1)S(1)} collective-permute-done((bf16[704,256]{1,0:T(8,128)(2,1)S(1)}, bf16[704,256]{1,0:T(8,128)(2,1)S(1)}, u32[]{:S(2)}, u32[]{:S(2)}) %collective-permute-start.6) | collective-permute-done | bytes 360480 | tf_op jit(solution)/shard_map/ppermute | solution.py:638
  56.3 0.1 convert_add_fusion
  56.4 2.4 %collective-permute-start.7 = (bf16[176,256]{1,0:T(8,128)(2,1)S(1)}, bf16[176,256]{1,0:T(8,128)(2,1)S(1)}, u32[]{:S(2)}, u32[]{:S(2)}) collective-permute-start(bf16[176,256]{1,0:T(8,128)(2,1)S(1)} %get-tuple-element.100), channel_id=1, source_target_pairs={{0,8},{8,0},{16,24},{24,16},{1,9},{9,1},{17,25},{25,17},{2,10},{10... | collective-permute-start | bytes 270344 | tf_op jit(solution)/shard_map/ppermute | solution.py:638
  58.8 1.5 %collective-permute-start.9 = (bf16[176,256]{1,0:T(8,128)(2,1)S(1)}, bf16[176,256]{1,0:T(8,128)(2,1)S(1)}, u32[]{:S(2)}, u32[]{:S(2)}) collective-permute-start(bf16[176,256]{1,0:T(8,128)(2,1)S(1)} %get-tuple-element.101), channel_id=1, source_target_pairs={{0,24},{8,16},{16,8},{24,0},{1,25},{9,17},{17,9},{25,1},{2,26},{10... | collective-permute-start | bytes 270344 | tf_op jit(solution)/shard_map/ppermute | solution.py:638
  60.4 1.9 %collective-permute-done.7 = bf16[176,256]{1,0:T(8,128)(2,1)S(1)} collective-permute-done((bf16[176,256]{1,0:T(8,128)(2,1)S(1)}, bf16[176,256]{1,0:T(8,128)(2,1)S(1)}, u32[]{:S(2)}, u32[]{:S(2)}) %collective-permute-start.7) | collective-permute-done | bytes 90144 | tf_op jit(solution)/shard_map/ppermute | solution.py:638
  62.3 2.9 %collective-permute-done.9 = bf16[176,256]{1,0:T(8,128)(2,1)S(1)} collective-permute-done((bf16[176,256]{1,0:T(8,128)(2,1)S(1)}, bf16[176,256]{1,0:T(8,128)(2,1)S(1)}, u32[]{:S(2)}, u32[]{:S(2)}) %collective-permute-start.9) | collective-permute-done | bytes 90144 | tf_op jit(solution)/shard_map/ppermute | solution.py:638
  65.2 1.3 %collective-permute-done.8 = bf16[176,256]{1,0:T(8,128)(2,1)S(1)} collective-permute-done((bf16[176,256]{1,0:T(8,128)(2,1)S(1)}, bf16[176,256]{1,0:T(8,128)(2,1)S(1)}, u32[]{:S(2)}, u32[]{:S(2)}) %collective-permute-start.8) | collective-permute-done | bytes 90144 | tf_op jit(solution)/shard_map/ppermute | solution.py:638
  66.6 4.6 %collective-permute-start.12 = (bf16[176,256]{1,0:T(8,128)(2,1)S(1)}, bf16[176,256]{1,0:T(8,128)(2,1)S(1)}, u32[]{:S(2)}, u32[]{:S(2)}) collective-permute-start(bf16[176,256]{1,0:T(8,128)(2,1)S(1)} %add_convert_fusion.1), channel_id=1, source_target_pairs={{0,6},{1,7},{2,4},{3,5},{4,2},{5,3},{6,0},{7,1},{8,14},{9,15},{10,... | collective-permute-start | bytes 270344 | tf_op jit(solution)/shard_map/ppermute | solution.py:638
  71.2 0.6 collective-permute-start.10
  71.8 2.8 %collective-permute-done.12 = bf16[176,256]{1,0:T(8,128)(2,1)S(1)} collective-permute-done((bf16[176,256]{1,0:T(8,128)(2,1)S(1)}, bf16[176,256]{1,0:T(8,128)(2,1)S(1)}, u32[]{:S(2)}, u32[]{:S(2)}) %collective-permute-start.12) | collective-permute-done | bytes 90144 | tf_op jit(solution)/shard_map/ppermute | solution.py:638
  74.6 3.9 %collective-permute-done.11 = bf16[176,256]{1,0:T(8,128)(2,1)S(1)} collective-permute-done((bf16[176,256]{1,0:T(8,128)(2,1)S(1)}, bf16[176,256]{1,0:T(8,128)(2,1)S(1)}, u32[]{:S(2)}, u32[]{:S(2)}) %collective-permute-start.11) | collective-permute-done | bytes 90144 | tf_op jit(solution)/shard_map/ppermute | solution.py:638
  78.6 1.5 %collective-permute-start.15 = (bf16[176,256]{1,0:T(8,128)(2,1)S(1)}, bf16[176,256]{1,0:T(8,128)(2,1)S(1)}, u32[]{:S(2)}, u32[]{:S(2)}) collective-permute-start(bf16[176,256]{1,0:T(8,128)(2,1)S(1)} %add_convert_fusion), channel_id=1, source_target_pairs={{0,24},{8,16},{16,8},{24,0},{1,25},{9,17},{17,9},{25,1},{2,26},{10... | collective-permute-start | bytes 270344 | tf_op jit(solution)/shard_map/ppermute | solution.py:638
  80.1 0.7 collective-permute-start.14
  80.8 1.4 %collective-permute-start.13 = (bf16[176,256]{1,0:T(8,128)(2,1)S(1)}, bf16[176,256]{1,0:T(8,128)(2,1)S(1)}, u32[]{:S(2)}, u32[]{:S(2)}) collective-permute-start(bf16[176,256]{1,0:T(8,128)(2,1)S(1)} %add_convert_fusion), channel_id=1, source_target_pairs={{0,8},{8,0},{16,24},{24,16},{1,9},{9,1},{17,25},{25,17},{2,10},{10... | collective-permute-start | bytes 270344 | tf_op jit(solution)/shard_map/ppermute | solution.py:638
  82.1 2.8 %collective-permute-done.15 = bf16[176,256]{1,0:T(8,128)(2,1)S(1)} collective-permute-done((bf16[176,256]{1,0:T(8,128)(2,1)S(1)}, bf16[176,256]{1,0:T(8,128)(2,1)S(1)}, u32[]{:S(2)}, u32[]{:S(2)}) %collective-permute-start.15) | collective-permute-done | bytes 90144 | tf_op jit(solution)/shard_map/ppermute | solution.py:638
  85.0 0.4 collective-permute-done.14
  85.4 0.1 collective-permute-start.16
  85.4 0.9 copy.42
  86.3 0.8 collective-permute-done.16.refs_2_
  87.1 1.9 %finish.1 = (f32[3,3,12,64]{3,2,1,0:T(8,128)}, f32[576,64]{1,0:T(8,128)}, f32[576,256]{1,0:T(8,128)}, f32[576,256]{1,0:T(8,128)}, f32[3,3,12,64]{3,2,1,0:T(8,128...) custom-call(s32[4]{0:T(128)S(1)} %pad_add_fusion.refs_0_, ...), custom_call_target="tpu_custom_call" | custom-call | tf_op jit(solution)/shard_map/finish/pallas_call | solution.py:773
  (32 shorter events, 0.4 us)
Async XLA Ops:
  2.4 12.0 %all-to-all-start = ((bf16[8,2,528]{2,1,0:T(2,128)(2,1)}), bf16[8,2,528]{2,1,0:T(2,128)(2,1)S(1)}, u32[]{:S(2)}, u32[]{:S(2)}) async-start(bf16[8,2,528]{2,1,0:T(2,128)(2,1)} %reshape.96), calls=%async_computation | async-start | bytes 40960 | tf_op jit(solution)/shard_map/all_to_all | solution.py:601
  9.8 16.7 %copy-start = (f32[256]{0:T(256)S(1)}, f32[256]{0:T(256)}, u32[]{:S(2)}) copy-start(f32[256]{0:T(256)} %param.20) | copy-start | bytes 3076
  9.8 16.7 %copy-start.1 = (f32[256]{0:T(256)S(1)}, f32[256]{0:T(256)}, u32[]{:S(2)}) copy-start(f32[256]{0:T(256)} %param.21) | copy-start | bytes 3076
  9.8 16.7 %copy-start.2 = (f32[64]{0:T(128)S(1)}, f32[64]{0:T(128)}, u32[]{:S(2)}) copy-start(f32[64]{0:T(128)} %param.18) | copy-start | bytes 772
  9.9 16.7 %copy-start.3 = (f32[64]{0:T(128)S(1)}, f32[64]{0:T(128)}, u32[]{:S(2)}) copy-start(f32[64]{0:T(128)} %param.19) | copy-start | bytes 772
  9.9 16.7 %copy-start.4 = (f32[12]{0:T(128)S(1)}, f32[12]{0:T(128)}, u32[]{:S(2)}) copy-start(f32[12]{0:T(128)} %param.22) | copy-start | bytes 148
  10.0 10.4 %collective-permute-start.2 = (bf16[12,12,64]{0,1,2:T(8,128)(2,1)S(1)}, bf16[12,12,64]{0,1,2:T(8,128)(2,1)S(1)}, u32[]{:S(2)}, u32[]{:S(2)}) collective-permute-start(bf16[12,12,64]{0,1,2:T(8,128)(2,1)S(1)} %get-tuple-element.103), channel_id=1, source_target_pairs={{0,1},{1,2},{2,3},{3,4},{4,5},{5,6},{6,7},{8,9},{9,10},{10,11},{11... | collective-permute-start | bytes 55304 | tf_op jit(solution)/shard_map/ppermute | solution.py:612
  12.5 8.0 %collective-permute-start.3 = (bf16[12,12,64]{0,1,2:T(8,128)(2,1)S(1)}, bf16[12,12,64]{0,1,2:T(8,128)(2,1)S(1)}, u32[]{:S(2)}, u32[]{:S(2)}) collective-permute-start(bf16[12,12,64]{0,1,2:T(8,128)(2,1)S(1)} %get-tuple-element.104), channel_id=1, source_target_pairs={{1,0},{2,1},{3,2},{4,3},{5,4},{6,5},{7,6},{9,8},{10,9},{11,10},{12... | collective-permute-start | bytes 55304 | tf_op jit(solution)/shard_map/ppermute | solution.py:613
  14.6 11.7 %collective-permute-start.1 = (bf16[6,12,44]{2,1,0:T(8,128)(2,1)S(1)}, bf16[6,12,44]{2,1,0:T(8,128)(2,1)S(1)}, u32[]{:S(2)}, u32[]{:S(2)}) collective-permute-start(bf16[6,12,44]{2,1,0:T(8,128)(2,1)S(1)} %bitcast.64), channel_id=1, source_target_pairs={{8,0},{16,8},{24,16},{9,1},{17,9},{25,17},{10,2},{18,10},{26,18},{... | collective-permute-start | bytes 19016 | tf_op jit(solution)/shard_map/ppermute | solution.py:603
  15.9 10.4 %collective-permute-start = (bf16[6,12,44]{2,1,0:T(8,128)(2,1)S(1)}, bf16[6,12,44]{2,1,0:T(8,128)(2,1)S(1)}, u32[]{:S(2)}, u32[]{:S(2)}) collective-permute-start(bf16[6,12,44]{2,1,0:T(8,128)(2,1)S(1)} %bitcast.63), channel_id=1, source_target_pairs={{0,8},{8,16},{16,24},{1,9},{9,17},{17,25},{2,10},{10,18},{18,26},{... | collective-permute-start | bytes 19016 | tf_op jit(solution)/shard_map/ppermute | solution.py:602
  20.7 17.5 %collective-permute-start.4 = (bf16[12,12,152]{2,1,0:T(8,128)(2,1)S(1)}, bf16[12,12,152]{2,1,0:T(8,128)(2,1)S(1)}, u32[]{:S(2)}, u32[]{:S(2)}) collective-permute-start(bf16[12,12,152]{2,1,0:T(8,128)(2,1)S(1)} %get-tuple-element.98), channel_id=1, source_target_pairs={{0,8},{8,16},{16,24},{1,9},{9,17},{17,25},{2,10},{10,18},{18,26},{... | collective-permute-start | bytes 131336 | tf_op jit(solution)/shard_map/ppermute | solution.py:617
  25.0 13.2 %collective-permute-start.5 = (bf16[12,12,152]{2,1,0:T(8,128)(2,1)S(1)}, bf16[12,12,152]{2,1,0:T(8,128)(2,1)S(1)}, u32[]{:S(2)}, u32[]{:S(2)}) collective-permute-start(bf16[12,12,152]{2,1,0:T(8,128)(2,1)S(1)} %get-tuple-element.99), channel_id=1, source_target_pairs={{8,0},{16,8},{24,16},{9,1},{17,9},{25,17},{10,2},{18,10},{26,18},{... | collective-permute-start | bytes 131336 | tf_op jit(solution)/shard_map/ppermute | solution.py:618
  53.9 2.4 %collective-permute-start.6 = (bf16[704,256]{1,0:T(8,128)(2,1)S(1)}, bf16[704,256]{1,0:T(8,128)(2,1)S(1)}, u32[]{:S(2)}, u32[]{:S(2)}) collective-permute-start(bf16[704,256]{1,0:T(8,128)(2,1)S(1)} %get-tuple-element.54), channel_id=1, source_target_pairs={{0,1},{1,0},{2,3},{3,2},{4,5},{5,4},{6,7},{7,6},{8,9},{9,8},{10,11... | collective-permute-start | bytes 1081352 | tf_op jit(solution)/shard_map/ppermute | solution.py:638
  56.4 5.9 %collective-permute-start.7 = (bf16[176,256]{1,0:T(8,128)(2,1)S(1)}, bf16[176,256]{1,0:T(8,128)(2,1)S(1)}, u32[]{:S(2)}, u32[]{:S(2)}) collective-permute-start(bf16[176,256]{1,0:T(8,128)(2,1)S(1)} %get-tuple-element.100), channel_id=1, source_target_pairs={{0,8},{8,0},{16,24},{24,16},{1,9},{9,1},{17,25},{25,17},{2,10},{10... | collective-permute-start | bytes 270344 | tf_op jit(solution)/shard_map/ppermute | solution.py:638
  58.8 6.4 %collective-permute-start.9 = (bf16[176,256]{1,0:T(8,128)(2,1)S(1)}, bf16[176,256]{1,0:T(8,128)(2,1)S(1)}, u32[]{:S(2)}, u32[]{:S(2)}) collective-permute-start(bf16[176,256]{1,0:T(8,128)(2,1)S(1)} %get-tuple-element.101), channel_id=1, source_target_pairs={{0,24},{8,16},{16,8},{24,0},{1,25},{9,17},{17,9},{25,1},{2,26},{10... | collective-permute-start | bytes 270344 | tf_op jit(solution)/shard_map/ppermute | solution.py:638
  60.3 6.2 %collective-permute-start.8 = (bf16[176,256]{1,0:T(8,128)(2,1)S(1)}, bf16[176,256]{1,0:T(8,128)(2,1)S(1)}, u32[]{:S(2)}, u32[]{:S(2)}) collective-permute-start(bf16[176,256]{1,0:T(8,128)(2,1)S(1)} %get-tuple-element.102), channel_id=1, source_target_pairs={{0,16},{8,24},{16,0},{24,8},{1,17},{9,25},{17,1},{25,9},{2,18},{10... | collective-permute-start | bytes 270344 | tf_op jit(solution)/shard_map/ppermute | solution.py:638
  66.6 8.0 %collective-permute-start.12 = (bf16[176,256]{1,0:T(8,128)(2,1)S(1)}, bf16[176,256]{1,0:T(8,128)(2,1)S(1)}, u32[]{:S(2)}, u32[]{:S(2)}) collective-permute-start(bf16[176,256]{1,0:T(8,128)(2,1)S(1)} %add_convert_fusion.1), channel_id=1, source_target_pairs={{0,6},{1,7},{2,4},{3,5},{4,2},{5,3},{6,0},{7,1},{8,14},{9,15},{10,... | collective-permute-start | bytes 270344 | tf_op jit(solution)/shard_map/ppermute | solution.py:638
  71.2 7.3 %collective-permute-start.11 = (bf16[176,256]{1,0:T(8,128)(2,1)S(1)}, bf16[176,256]{1,0:T(8,128)(2,1)S(1)}, u32[]{:S(2)}, u32[]{:S(2)}) collective-permute-start(bf16[176,256]{1,0:T(8,128)(2,1)S(1)} %add_convert_fusion.1), channel_id=1, source_target_pairs={{0,4},{1,5},{2,6},{3,7},{4,0},{5,1},{6,2},{7,3},{8,12},{9,13},{10,... | collective-permute-start | bytes 270344 | tf_op jit(solution)/shard_map/ppermute | solution.py:638
  71.2 7.3 %collective-permute-start.10 = (bf16[176,256]{1,0:T(8,128)(2,1)S(1)}, bf16[176,256]{1,0:T(8,128)(2,1)S(1)}, u32[]{:S(2)}, u32[]{:S(2)}) collective-permute-start(bf16[176,256]{1,0:T(8,128)(2,1)S(1)} %add_convert_fusion.1), channel_id=1, source_target_pairs={{0,2},{1,3},{2,0},{3,1},{4,6},{5,7},{6,4},{7,5},{8,10},{9,11},{10,... | collective-permute-start | bytes 270344 | tf_op jit(solution)/shard_map/ppermute | solution.py:638
  78.6 6.4 %collective-permute-start.15 = (bf16[176,256]{1,0:T(8,128)(2,1)S(1)}, bf16[176,256]{1,0:T(8,128)(2,1)S(1)}, u32[]{:S(2)}, u32[]{:S(2)}) collective-permute-start(bf16[176,256]{1,0:T(8,128)(2,1)S(1)} %add_convert_fusion), channel_id=1, source_target_pairs={{0,24},{8,16},{16,8},{24,0},{1,25},{9,17},{17,9},{25,1},{2,26},{10... | collective-permute-start | bytes 270344 | tf_op jit(solution)/shard_map/ppermute | solution.py:638
  80.1 5.2 %collective-permute-start.14 = (bf16[176,256]{1,0:T(8,128)(2,1)S(1)}, bf16[176,256]{1,0:T(8,128)(2,1)S(1)}, u32[]{:S(2)}, u32[]{:S(2)}) collective-permute-start(bf16[176,256]{1,0:T(8,128)(2,1)S(1)} %add_convert_fusion), channel_id=1, source_target_pairs={{0,16},{8,24},{16,0},{24,8},{1,17},{9,25},{17,1},{25,9},{2,18},{10... | collective-permute-start | bytes 270344 | tf_op jit(solution)/shard_map/ppermute | solution.py:638
  80.8 4.6 %collective-permute-start.13 = (bf16[176,256]{1,0:T(8,128)(2,1)S(1)}, bf16[176,256]{1,0:T(8,128)(2,1)S(1)}, u32[]{:S(2)}, u32[]{:S(2)}) collective-permute-start(bf16[176,256]{1,0:T(8,128)(2,1)S(1)} %add_convert_fusion), channel_id=1, source_target_pairs={{0,8},{8,0},{16,24},{24,16},{1,9},{9,1},{17,25},{25,17},{2,10},{10... | collective-permute-start | bytes 270344 | tf_op jit(solution)/shard_map/ppermute | solution.py:638
  85.4 1.7 %collective-permute-start.16 = (bf16[704,256]{1,0:T(8,128)(2,1)S(1)}, bf16[704,256]{1,0:T(8,128)(2,1)S(1)}, u32[]{:S(2)}, u32[]{:S(2)}) collective-permute-start(bf16[704,256]{1,0:T(8,128)(2,1)S(1)} %pad_maximum_fusion.2.refs_1_), channel_id=1, source_target_pairs={{0,1},{1,0},{2,3},{3,2},{4,5},{5,4},{6,7},{7,6},{8,9},{9,8},{10,11... | collective-permute-start | bytes 1081352 | tf_op jit(solution)/shard_map/ppermute | solution.py:638
where the time goes:
time: 89.5 us; the launch traced here: 89.1 us
  starting transfers between devices  35.4 us (40%)
  Pallas kernels  27.9 us (31%)
  waiting for transfers between devices  18.6 us (21%)
  local copies, waits for them, and re-layouts  4.56 us (5%)
  other arithmetic  1.56 us (2%)
  between operations  1.15 us (1%)
    ppermute x11, waiting for transfers between devices, swap(): return lax.ppermute(block, axis, [(i, i ^ flip) for i in range(count)])  18.1 us
    pallas_call x1, Pallas kernels, local(): pl.pallas_call(lambda *refs: backward(scale, *refs), out_shape=(pltpu.VME...  14.5 us
    ppermute x11, starting transfers between devices, swap(): return lax.ppermute(block, axis, [(i, i ^ flip) for i in range(count)])  13.9 us
    pallas_call x1, Pallas kernels, local(): pl.pallas_call(lambda *refs: forward(extent, *refs), out_shape=shared + (...  11.5 us
    all_to_all x1, starting transfers between devices, coarse_lines(): lax.all_to_all(pieces, 'gy', 0, 0, tiled=True)  6.33 us
    ppermute x1, starting transfers between devices, coarse_lines(): above = lax.ppermute(got[-HALO:], 'gx', pairs(gx, 1))  4.55 us
    ppermute x1, starting transfers between devices, cotangent_lines(): above = lax.ppermute(cot[-n:], 'gx', pairs(gx, 1))  4.3 us
    unnamed x14, local copies, waits for them, and re-layouts  2.8 us
  transfers between devices with their start and end apart: 18, of which 10 were waited for; matrix products, arithmetic and copies ran while one was open for 3% of the time, Pallas kernels for 13%

commit v1 on v0

--- a/solution.py
+++ b/solution.py
@@ -13,8 +13,8 @@
 OWN = PITCH * 8
 HALO = 6
 FINE_HALO = 12
-PACKED = 1408
-GROUP0, GROUP5 = 6, 6
+TERMS = 1400
+GROUP0, GROUP5 = 7, 6
 N1, N2, N3, N4 = 3, 5, 3, 4
 M4, M3, M2, M1 = 4, 3, 4, 3
 LIMIT = 12
@@ -114,14 +114,20 @@
     return jnp.where(chosen, 1.0, 0.0).astype(BF)
 
 
-def select(s0_ref, s5_ref, e_ref, turn3_ref, turn4_ref):
-    m, lane = grid(PITCH, 64)
+def select(core, s0_ref, s5_ref, e_ref, turn3_ref, turn4_ref):
+    m, lane = grid(PITCH, 256)
     for s in range(3):
-        s0_ref[s * PITCH : (s + 1) * PITCH, :] = one_hot(lane == m + s + jnp.where(m < 8, 1, 9))
-    m, lane = grid(PITCH, 160)
-    wanted = jnp.where(m < 3, 4 * m + 1, jnp.where(m >= 13, 4 * m - 35, 1000))
+        after = m + 31 + s + HALO + core * COLS
+        here = m - 17 + s + HALO + core * COLS
+        wanted = jnp.where(m < 8, after, jnp.where(here >= 0, here + 128, -1))
+        s0_ref[s * PITCH : (s + 1) * PITCH, :] = one_hot(lane == wanted)
     for u in range(6):
-        s5_ref[u * PITCH : (u + 1) * PITCH, :] = one_hot(lane == wanted + u)
+        col = 4 * jnp.where(m < 8, m + 32, m - 16) + u - 1
+        beyond = jnp.where(col - 128 < FINE_HALO, col + 64, -1)
+        beyond = jnp.where(col == 127, 204, beyond)
+        here = jnp.where(col < 0, col + 140, jnp.where(col < 128, col, col + 12))
+        here = jnp.where(col < -FINE_HALO, -1, here)
+        s5_ref[u * PITCH : (u + 1) * PITCH, :] = one_hot(lane == jnp.where(m < 8, beyond, here))
     cell, lane = grid(512, 512)
     e_ref[...] = one_hot(lane == ((cell >> 5) & 3) * 128 + (cell & 31) * 4 + (cell >> 7))
     new, old = grid(256, 256)
@@ -289,21 +295,26 @@
     for copy in copies:
         copy.start()
     small = (b1_ref, b2_ref, b3_ref, b4_ref, b5_ref)
-    select(s0_ref, s5_ref, e_ref, turn3_ref, turn4_ref)
+    select(pos_ref[2], s0_ref, s5_ref, e_ref, turn3_ref, turn4_ref)
     in_plane(extent, pos_ref, mask)
     low = low_half()
-    clear_margins(((x0, 2, 32), (x1, 3, 30), (x2, 4, 29), (x3, 5, 29), (a4, 5, 29)))
-
-    def coarse_chunk(k):
-        lines = dx_ref[pl.ds(k - 2, 3)].reshape(48, 64)
-        lines = jnp.concatenate([lines, jnp.zeros((80, 64), BF)], axis=0)
-        moved = dott(s0_ref[...], lines).astype(BF)
-        for s in range(3):
-            x0[pl.ds(pl.multiple_of(k * PITCH, 16), PITCH), s * 128 : (s + 1) * 128] = moved[
-                s * PITCH : (s + 1) * PITCH, :
-            ]
-
-    grouped(2, 32, GROUP0, coarse_chunk)
+    clear_margins(((x0, 2, 30), (x1, 3, 30), (x2, 4, 29), (x3, 5, 29), (a4, 5, 29)))
+
+    def coarse_pair(n):
+        lines = []
+        for k in (2 * n, 2 * n + 1):
+            before = dx_ref[pl.ds(k - 2, 3)].reshape(48, 128)
+            here = dx_ref[pl.ds(k - 1, 3)].reshape(48, 128)
+            lines += [jnp.concatenate([before, here], axis=1), jnp.zeros((80, 256), BF)]
+        moved = dott(s0_ref[...], jnp.concatenate(lines, axis=0)).astype(BF)
+        for half in range(2):
+            at = pl.multiple_of((2 * n + half) * PITCH, 16)
+            for s in range(3):
+                x0[pl.ds(at, PITCH), s * 128 : (s + 1) * 128] = moved[
+                    s * PITCH : (s + 1) * PITCH, half * 128 : (half + 1) * 128
+                ]
+
+    grouped(1, 15, GROUP0, coarse_pair)
     for copy in copies:
         copy.wait()
     perms = (turn3_ref[...].T, turn4_ref[...].T)
@@ -385,7 +396,8 @@
     )
     high = z.astype(BF)
     rest = (z - high.astype(F32)).astype(BF)
-    z = dotn(rest, e_ref[...]) + dotn(high, e_ref[...])
+    z = dotn(jnp.concatenate([rest, high], axis=0), e_ref[...])
+    z = z[0:256] + z[256:512]
     for g in range(4):
         for n in range(4):
             for p in range(4):
@@ -397,11 +409,10 @@
 def backward(
     scale,
     pos_ref,
-    dc_ref,
+    center_ref,
+    rim_ref,
     mask,
     s5_ref,
-    turn3_ref,
-    turn4_ref,
     r5,
     r4,
     r3,
@@ -424,16 +435,23 @@
     low = low_half()
     clear_margins(((c5, 5, 29), (b4, 5, 29), (b3, 6, 27), (b2, 7, 27)))
 
-    def cot_chunk(k):
-        lines = dc_ref[pl.ds(4 * (k - 5), 6)].reshape(96, 160)
-        lines = jnp.concatenate([lines, jnp.zeros((32, 160), BF)], axis=0)
-        moved = dott(s5_ref[...], lines).astype(BF)
-        for u in range(6):
-            c5[pl.ds(pl.multiple_of(k * PITCH, 16), PITCH), u * 128 : (u + 1) * 128] = moved[
-                u * PITCH : (u + 1) * PITCH, :
-            ]
-
-    grouped(5, 29, GROUP5, cot_chunk)
+    def cot_pair(n):
+        lines = []
+        for k in (2 * n + 1, 2 * n + 2):
+            at = pl.ds(4 * (k - 5), 6)
+            here = jnp.concatenate(
+                [center_ref[at].reshape(96, 128), rim_ref[at].reshape(96, 128)], axis=1
+            )
+            lines += [here, jnp.zeros((32, 256), BF)]
+        moved = dott(s5_ref[...], jnp.concatenate(lines, axis=0)).astype(BF)
+        for half in range(2):
+            at = pl.multiple_of((2 * n + 1 + half) * PITCH, 16)
+            for u in range(6):
+                c5[pl.ds(at, PITCH), u * 128 : (u + 1) * 128] = moved[
+                    u * PITCH : (u + 1) * PITCH, half * 128 : (half + 1) * 128
+                ]
+
+    grouped(2, 14, GROUP5, cot_pair)
 
     def back_four(start, size):
         ok = take(mask, start, size)
@@ -478,7 +496,7 @@
     blocks(7, 20 // M2, M2, back_narrow(b3, r3, x2, b2))
     blocks(8, 18 // M1, M1, back_narrow(b2, r2, x1, b1))
 
-    g_ref[PACKED - 64 :, :] = jnp.zeros((64, 256), F32)
+    g_ref[1344:, :] = jnp.zeros((g_ref.shape[0] - 1344, 256), F32)
     g_ref[1152:1344, 192:256] = jnp.zeros((192, 64), F32)
 
     back = own(b4, 0, 1024)
@@ -492,7 +510,7 @@
             term = dotn(back[p * 512 : (p + 1) * 512, :], field)
             total = term if total is None else total + term
         total = total[0:256, 0:192] + total[256:512, 64:256]
-        g_ref[r * 192 : (r + 1) * 192, :] = split_dot(total.T * scale, turn4_ref[...])
+        g_ref[r * 192 : (r + 1) * 192, :] = total.T * scale
     sums4 = sums4[:, 0:512] + sums4[:, 512:1024]
     sums4 = sums4[:, 0:256] + sums4[:, 256:512]
 
@@ -501,7 +519,7 @@
     back = back.T
     for r in range(3):
         total = dotn(back, own(x2, 0, 256, r - 1))[:, 0:192]
-        g_ref[576 + r * 192 : 576 + (r + 1) * 192, :] = split_dot(total.T * scale, turn3_ref[...])
+        g_ref[576 + r * 192 : 576 + (r + 1) * 192, :] = total.T * scale
 
     back = own(b2, 0, 128)
     sums2 = jnp.sum(back.astype(F32), axis=0, keepdims=True)
@@ -542,8 +560,8 @@
     for t in range(1, 4):
         five = five + lane_roll(sums5, -16 * t)
     biases = [
-        split_dot(jnp.broadcast_to(sums4 * scale, (8, 256)), turn4_ref[...])[0:1],
-        split_dot(jnp.broadcast_to(sums3 * scale, (8, 256)), turn3_ref[...])[0:1],
+        sums4 * scale,
+        sums3 * scale,
         jnp.concatenate([sums2, sums1], axis=1) * scale,
         jnp.concatenate([five, jnp.zeros((1, 128), F32)], axis=1) * scale,
     ]
@@ -552,90 +570,121 @@
         g_ref[1392 + 2 * n : 1393 + 2 * n, :] = high
         g_ref[1393 + 2 * n : 1394 + 2 * n, :] = value - high
 
-    half = PACKED // 2
+    half = g_ref.shape[0] // 2
     core = pos_ref[2]
     keep_ref[...] = g_ref[pl.ds(pl.multiple_of(core * half, 16), half), :]
     send_ref[...] = g_ref[pl.ds(pl.multiple_of((1 - core) * half, 16), half), :].astype(BF)
 
 
-def finish(chans, places, pos_ref, mine_ref, other_ref, g1, g2, g3, g4, g5, c1, c2, c3, c4, c5, full):
-    half = PACKED // 2
+def finish(chans, places, pos_ref, mine_ref, other_ref, turn3_ref, turn4_ref, g1, g2, g3, g4, g5, c1, c2, c3, c4, c5, full):
+    half = full.shape[0] // 2
     size = half // places
     core = pos_ref[2]
     for b in range(places):
-        at = pl.multiple_of(lax.bitwise_xor(pos_ref[3], b) * size, 8)
-        here = pl.multiple_of(core * half + b * size, 8)
-        there = pl.multiple_of((1 - core) * half + b * size, 8)
-        full[pl.ds(here, size), :] = mine_ref[pl.ds(at, size), :].astype(F32)
-        full[pl.ds(there, size), :] = other_ref[pl.ds(at, size), :].astype(F32)
-    g4[...] = full[0:576, :]
-    g3[...] = full[576:1152, :]
+        at = pl.multiple_of(lax.bitwise_xor(pos_ref[3], b) * size, 16)
+        here = pl.multiple_of(core * half + b * size, 16)
+        there = pl.multiple_of((1 - core) * half + b * size, 16)
+        full[pl.ds(here, size), :] = mine_ref[pl.ds(at, size), :]
+        full[pl.ds(there, size), :] = other_ref[pl.ds(at, size), :]
+    g4[...] = dotn(full[0:576, :], turn4_ref[...])
+    g3[...] = dotn(full[576:1152, :], turn3_ref[...])
     for r in range(3):
-        g2[r * 192 : (r + 1) * 192, :] = full[1152:1344, r * 64 : (r + 1) * 64]
+        g2[r * 192 : (r + 1) * 192, :] = full[1152:1344, r * 64 : (r + 1) * 64].astype(F32)
         for s in range(3):
             at = 1152 + s * 48 + r * 16
-            g1[r, s] = full[at : at + chans, 192:256]
+            g1[r, s] = full[at : at + 16, 192:256].astype(F32)[:chans]
             at = 1344 + s * 16
-            g5[r, s] = full[at : at + chans, r * 64 : (r + 1) * 64]
-    sums = [full[1392 + 2 * n : 1393 + 2 * n, :] + full[1393 + 2 * n : 1394 + 2 * n, :] for n in range(4)]
-    c4[...] = sums[0]
-    c3[...] = sums[1]
+            g5[r, s] = full[at : at + 16, r * 64 : (r + 1) * 64].astype(F32)[:chans]
+    terms = full[1392:1408, :]
+    turned4 = dotn(terms, turn4_ref[...])
+    turned3 = dotn(terms, turn3_ref[...])
+    terms = terms.astype(F32)
+    c4[...] = turned4[0:1] + turned4[1:2]
+    c3[...] = turned3[2:3] + turned3[3:4]
+    sums = [None, None, terms[4:5] + terms[5:6], terms[6:7] + terms[7:8]]
     c2[...] = sums[2][:, 64:128]
     c1[...] = sums[2][:, 192:256]
     c5[...] = sums[3][:, 16 : 16 + chans]
 
 
-def pairs(count, by):
-    return [(i, i + by) for i in range(count) if 0 <= i + by < count]
-
-
-def coarse_lines(coarse):
-    gx, gy = lax.axis_size("gx"), lax.axis_size("gy")
-    chans, each = coarse.shape[:2]
-    cols = coarse.shape[2] // gy
-    wide = cols + 2 * HALO
-    tiles = coarse.reshape(chans, each, gy, cols).transpose(2, 1, 0, 3)
-    before = jnp.pad(tiles[:-1, :, :, cols - HALO :], ((1, 0), (0, 0), (0, 0), (0, 0)))
-    after = jnp.pad(tiles[1:, :, :, :HALO], ((0, 1), (0, 0), (0, 0), (0, 0)))
-    pieces = jnp.concatenate([before, tiles, after], axis=3)
-    got = lax.all_to_all(pieces, "gy", 0, 0, tiled=True).reshape(gy * each, chans, wide)
-    above = lax.ppermute(got[-HALO:], "gx", pairs(gx, 1))
-    below = lax.ppermute(got[:HALO], "gx", pairs(gx, -1))
-    whole = jnp.concatenate([above, got, below])
-    here, before = rows(whole, 1, 3), rows(whole, 2, 2)
-    return jnp.concatenate([before[:, :, 36:44], gap(before, 12), here], axis=2)
-
-
-def cotangent_lines(cotangent):
-    gx, gy = lax.axis_size("gx"), lax.axis_size("gy")
+def exchange(axis, first, last):
+    count = lax.axis_size(axis)
+    odd = lax.axis_index(axis) % 2 == 1
+    even_swap = [(i, i ^ 1) for i in range(count)]
+    odd_swap = [(i, ((i + 1) ^ 1) - 1) for i in range(1, count - 1)]
+    one = lax.ppermute(jnp.where(odd, first, last), axis, even_swap)
+    two = lax.ppermute(jnp.where(odd, last, first), axis, odd_swap)
+    return jnp.where(odd, one, two), jnp.where(odd, two, one)
+
+
+def swap(block, axis, flip):
+    return lax.ppermute(block, axis, [(i, i ^ flip) for i in range(lax.axis_size(axis))])
+
+
+def chip_window(coarse):
+    gy, at = lax.axis_size("gy"), lax.axis_index("gy")
+    chans, each, ny = coarse.shape
+    cols = 2 * ny // gy
+    block = jnp.pad(coarse.transpose(1, 0, 2), ((0, 0), (0, 16 - chans), (HALO, HALO)))
+    other = swap(block, "gy", 1)
+    block = jnp.where(
+        at % 2 == 0, jnp.concatenate([block, other]), jnp.concatenate([other, block])
+    )
+    held = jnp.stack(
+        [block[:, :, cols * c : cols * (c + 1) + 2 * HALO] for c in range(gy // 2)]
+    )
+    flip, bits = gy // 2, 0
+    while flip > 1:
+        half = held.shape[0] // 2
+        high = (at & flip) != 0
+        mine = jnp.where(high, held[half:], held[:half])
+        other = swap(jnp.where(high, held[:half], held[half:]), "gy", flip)
+        held = jnp.where(
+            high,
+            jnp.concatenate([other, mine], axis=1),
+            jnp.concatenate([mine, other], axis=1),
+        )
+        flip, bits = flip // 2, bits + 1
+    tail = (2 * each,) + held.shape[2:]
+    held = held.reshape((2,) * bits + tail)
+    held = held.transpose(tuple(reversed(range(bits))) + (bits, bits + 1, bits + 2))
+    return held.reshape((gy * each,) + tail[1:])
+
+
+def halo_lines(coarse, cotangent):
     n = FINE_HALO
-    left = lax.ppermute(cotangent[:, :, -n:].transpose(2, 0, 1), "gy", pairs(gy, 1))
-    right = lax.ppermute(cotangent[:, :, :n].transpose(2, 0, 1), "gy", pairs(gy, -1))
-    cot = jnp.concatenate(
-        [left.transpose(2, 1, 0), cotangent.transpose(1, 0, 2), right.transpose(2, 1, 0)], axis=2
-    )
-    above = lax.ppermute(cot[-n:], "gx", pairs(gx, 1))
-    below = lax.ppermute(cot[:n], "gx", pairs(gx, -1))
-    whole = jnp.concatenate([above, cot, below])
-    here, before = rows(whole, 1, 9), rows(whole, 5, 5)
-    return jnp.concatenate([before[:, :, 138:152], gap(before, 4), here[:, :, :142]], axis=2)
-
-
-def rows(value, low, high):
-    return jnp.pad(value, ((low, high), (0, 4), (0, 0)))
-
-
-def gap(value, count):
-    return jnp.zeros(value.shape[:2] + (count,), BF)
+    chans = coarse.shape[0]
+    left, right = exchange(
+        "gy", cotangent[:, :, :n].transpose(2, 0, 1), cotangent[:, :, -n:].transpose(2, 0, 1)
+    )
+    got = chip_window(coarse)
+    wide = got.shape[2]
+    cot = jnp.pad(cotangent.transpose(1, 0, 2), ((0, 0), (0, 16 - chans), (0, 0)))
+    rim = jnp.concatenate([left.transpose(2, 1, 0), right.transpose(2, 1, 0)], axis=2)
+    rim = jnp.pad(rim, ((0, 0), (0, 16 - chans), (0, 0)))
+
+    def edge(cot_rows, coarse_rows):
+        side = jnp.pad(got[coarse_rows], ((0, n - HALO), (0, 0), (0, 128 - 2 * n - wide)))
+        side = jnp.concatenate([rim[cot_rows], side], axis=2)
+        return jnp.concatenate([cot[cot_rows], side])
+
+    first = edge(slice(0, n), slice(0, HALO))
+    last = edge(slice(-n, None), slice(-HALO, None))
+    above, below = exchange("gx", first, last)
+    lanes = slice(2 * n, 2 * n + wide)
+    whole = jnp.concatenate([above[n : n + HALO, :, lanes], got, below[n : n + HALO, :, lanes]])
+    lines0 = jnp.pad(whole, ((2, 2), (0, 0), (0, 128 - wide)))
+    rim = jnp.concatenate([above[n:, :, : 2 * n], rim, below[n:, :, : 2 * n]])
+    center = jnp.concatenate([above[:n], cot, below[:n]])
+    before = jnp.concatenate([rim[:, :, n:], center[:, :, 127:]], axis=2)
+    rim = jnp.pad(rim, ((1, 9), (0, 0), (0, 64 - 2 * n)))
+    before = jnp.pad(before, ((5, 5), (0, 0), (0, 63 - n)))
+    return lines0, jnp.pad(center, ((1, 9), (0, 0), (0, 0))), jnp.concatenate([rim, before], axis=2)
 
 
 def total_over_all(keep, send):
     gx, gy = lax.axis_size("gx"), lax.axis_size("gy")
     at_x = lax.axis_index("gx")
-
-    def swap(block, axis, flip):
-        count = lax.axis_size(axis)
-        return lax.ppermute(block, axis, [(i, i ^ flip) for i in range(count)])
 
     def tree(terms):
         while len(terms) > 1:
@@ -651,9 +700,13 @@
     terms = [part(at_x)]
     for d in range(1, gx):
         terms.append(swap(part(at_x ^ d).astype(BF), "gx", d).astype(F32))
-    block = tree(terms).astype(BF)
-    terms = [block] + [swap(block, "gy", 2 * d) for d in range(1, gy // 2)]
-    block = tree([term.astype(F32) for term in terms]).astype(BF)
+    block = tree(terms)
+    flip = 2
+    while flip < gy:
+        block = block.astype(BF)
+        block = block.astype(F32) + swap(block, "gy", flip).astype(F32)
+        flip *= 2
+    block = block.astype(BF)
     mine = jnp.concatenate([block] + [swap(block, "gx", d) for d in range(1, gx)])
     return mine, swap(mine, "gy", 1)
 
@@ -692,9 +745,10 @@
     def buf(width, kind=BF):
         return pltpu.VMEM((CELLS, width), kind)
 
+    lines0, center, rim = halo_lines(coarse, cotangent)
     shared = (
         buf(128, F32),
-        pltpu.VMEM((6 * PITCH, 160), BF),
+        pltpu.VMEM((6 * PITCH, 256), BF),
         pltpu.VMEM((256, 256), BF),
         pltpu.VMEM((256, 256), BF),
         pltpu.VMEM((256, 384), BF),
@@ -724,7 +778,7 @@
         scratch_shapes=[
             pltpu.VMEM((32, 512), F32),
             pltpu.VMEM((256, 128), F32),
-            pltpu.VMEM((3 * PITCH, 64), BF),
+            pltpu.VMEM((3 * PITCH, 256), BF),
             pltpu.VMEM((512, 512), BF),
             pltpu.VMEM((384, 128), BF),
             pltpu.VMEM((768, 128), BF),
@@ -739,7 +793,7 @@
         name="forward",
     )(
         pos,
-        coarse_lines(coarse),
+        lines0,
         *[pltpu.with_memory_space_constraint(w, pltpu.HBM) for w in weights],
         bias_one.reshape(1, -1),
         bias_two.reshape(1, -1),
@@ -748,11 +802,11 @@
         bias_five.reshape(1, -1),
     )
     fields = [near(f) for f in fields]
-    half = PACKED // 2
+    half = -(-TERMS // (32 * gx)) * 16 * gx
     keep, send = pl.pallas_call(
         lambda *refs: backward(scale, *refs),
         out_shape=(pltpu.VMEM((half, 256), F32), pltpu.VMEM((half, 256), BF)),
-        in_specs=[smem] + [vmem] * 15,
+        in_specs=[smem] + [vmem] * 14,
         out_specs=(vmem,) * 2,
         scratch_shapes=[
             buf(768),
@@ -760,11 +814,11 @@
             buf(256),
             buf(128),
             buf(128),
-            pltpu.VMEM((PACKED, 256), F32),
+            pltpu.VMEM((2 * half, 256), F32),
         ],
         compiler_params=params,
         name="backward",
-    )(pos, cotangent_lines(cotangent), *fields)
+    )(pos, center, rim, *fields[:2], *fields[4:])
     mine, other = total_over_all(keep, send)
 
     def out(*shape):
@@ -784,12 +838,12 @@
             out(1, 256),
             out(1, chans),
         ),
-        in_specs=[smem, vmem, vmem],
+        in_specs=[smem] + [vmem] * 4,
         out_specs=(vmem,) * 10,
-        scratch_shapes=[pltpu.VMEM((PACKED, 256), F32)],
+        scratch_shapes=[pltpu.VMEM((2 * half, 256), BF)],
         compiler_params=params,
         name="finish",
-    )(pos, mine, other)
+    )(pos, mine, other, fields[2], fields[3])
     return (
         fine.transpose(1, 0, 2)[:chans],
         g1,

time: 89.5 us -> 79.6 us (0.89)
  starting transfers between devices: 35.4 us -> 26.6 us
  Pallas kernels: 27.9 us -> 24.1 us
  waiting for transfers between devices: 18.6 us -> 21.6 us
    all_to_all x1 -> x0, starting transfers between devices: 6.33 us -> none  [coarse_lines(): lax.all_to_all(pieces, 'gy', 0, 0, tiled=True)]
    ppermute x17, waiting for transfers between devices: 18.1 us -> 21.6 us  [the longest x13 19.2 us: swap(): lax.ppermute(block, axis, [(i, i ^ flip) for i in range(lax.axis_size(axi...]
    pallas_call x1, Pallas kernels: 14.5 us -> 11.3 us  [local(): pl.pallas_call(lambda *refs: backward(scale, *refs), out_shape=(pltpu.VME...]
    ppermute x17, starting transfers between devices: 29.1 us -> 26.6 us  [the longest x13 23.7 us: swap(): lax.ppermute(block, axis, [(i, i ^ flip) for i in range(lax.axis_size(axi...]
    unnamed x14 -> x16, local copies, waits for them, and re-layouts: 2.8 us -> 1.37 us
    slice x7 -> x12, local copies, waits for them, and re-layouts: 0.56 us -> 1.69 us  [the longest x1 1.14 us: halo_lines(): cotangent[:, :, :n].transpose(2, 0, 1)]
    pad x0 -> x4, local copies, waits for them, and re-layouts: none -> 0.99 us  [the longest x1 0.84 us: chip_window(): jnp.pad(coarse.transpose(1, 0, 2), ((0, 0), (0, 16 - chans), (HALO, HALO)))]
  transfers between devices with their start and end apart: 18 -> 17, of which waited for: 10 -> 12; matrix products, arithmetic and copies ran while one was open for 3% -> 4% of each run, Pallas kernels for 13% -> 0%
where the time goes in v1:
time: 79.6 us; the launch traced here: 79.3 us
  starting transfers between devices  26.6 us (33%)
  Pallas kernels  24.1 us (30%)
  waiting for transfers between devices  21.6 us (27%)
  local copies, waits for them, and re-layouts  4.45 us (6%)
  other arithmetic  1.43 us (2%)
  between operations  1.1 us (1%)
    ppermute x13, starting transfers between devices, swap(): lax.ppermute(block, axis, [(i, i ^ flip) for i in range(lax.axis_size(axi...  23.7 us
    ppermute x13, waiting for transfers between devices, swap(): lax.ppermute(block, axis, [(i, i ^ flip) for i in range(lax.axis_size(axi...  19.2 us
    pallas_call x1, Pallas kernels, local(): pl.pallas_call(lambda *refs: backward(scale, *refs), out_shape=(pltpu.VME...  11.3 us
    pallas_call x1, Pallas kernels, local(): pl.pallas_call(lambda *refs: forward(extent, *refs), out_shape=shared + (...  10.8 us
    ppermute x2, waiting for transfers between devices, exchange(): one = lax.ppermute(jnp.where(odd, first, last), axis, even_swap)  2.35 us
    pallas_call x1, Pallas kernels, local(): pl.pallas_call(lambda *refs: finish(chans, gx, *refs), out_shape=(out(3,...  1.99 us
    ppermute x2, starting transfers between devices, exchange(): one = lax.ppermute(jnp.where(odd, first, last), axis, even_swap)  1.67 us
  transfers between devices with their start and end apart: 17, of which 12 were waited for; matrix products, arithmetic and copies ran while one was open for 4% of the time, Pallas kernels for 0%

profile of v1, /device:TPU:0, one launch (start us, length us, event | category | flops | bytes accessed | tf_op | source)
XLA Modules:
  0.0 79.3 jit_solution(16349541681784062484)
XLA Ops:
  0.7 0.8 %pad.37 = bf16[2,16,268]{2,0,1:T(2,128)(2,1)S(1)} pad(bf16[2,12,256]{2,0,1:T(2,128)(2,1)} %bitcast.63, bf16[]{:T(256)} %constant.40.clone.1), padding=0_0x0_4x6_6 | pad | bytes 29442 | tf_op jit(solution)/shard_map/jit(_pad)/pad | solution.py:628
  1.5 0.5 collective-permute-start.2
  2.0 1.1 %fusion.23 = (bf16[12,64,12]{2,1,0:T(8,128)(2,1)S(1)}, bf16[12,64,12]{2,1,0:T(8,128)(2,1)S(1)}) fusion(bf16[12,64,128]{2,1,0:T(8,128)(2,1)} %param.23), kind=kLoop, calls=%fused_computation.72 | loop fusion | bytes 73728 | tf_op jit(solution)/shard_map/slice | solution.py:658
  3.2 0.2 copy.47
  3.3 0.2 copy.48
  3.5 0.1 collective-permute-start
  3.6 0.7 collective-permute-start.1
  4.3 0.1 copy.50
  4.6 0.1 maximum_select_fusion.2
  4.7 0.1 slice_bitcast_fusion.3
  4.9 5.4 %collective-permute-start.3 = (bf16[2,4,16,76]{3,1,2,0:T(4,128)(2,1)S(1)}, bf16[2,4,16,76]{3,1,2,0:T(4,128)(2,1)S(1)}, u32[]{:S(2)}, u32[]{:S(2)}) collective-permute-start(bf16[2,4,16,76]{3,1,2,0:T(4,128)(2,1)S(1)} %get-tuple-element.119), channel_id=1, source_target_pairs={{0,4},{1,5},{2,6},{3,7},{4,0},{5,1},{6,2},{7,3},{8,12},{9,13},{10,... | collective-permute-start | bytes 58376 | tf_op jit(solution)/shard_map/ppermute | solution.py:621
  10.4 0.3 copy.44
  10.6 1.6 %collective-permute-done.3 = bf16[2,4,16,76]{3,1,2,0:T(4,128)(2,1)S(1)} collective-permute-done((bf16[2,4,16,76]{3,1,2,0:T(4,128)(2,1)S(1)}, bf16[2,4,16,76]{3,1,2,0:T(4,128)(2,1)S(1)}, u32[]{:S(2)}, u32[]{:S(2)}) %collective-permute-start.3) | collective-permute-done | bytes 19488 | tf_op jit(solution)/shard_map/ppermute | solution.py:621
  12.2 0.1 maximum_select_fusion
  12.3 2.0 %collective-permute-start.4 = (bf16[1,8,16,76]{3,1,2,0:T(8,128)(2,1)S(1)}, bf16[1,8,16,76]{3,1,2,0:T(8,128)(2,1)S(1)}, u32[]{:S(2)}, u32[]{:S(2)}) collective-permute-start(bf16[1,8,16,76]{3,1,2,0:T(8,128)(2,1)S(1)} %get-tuple-element.117), channel_id=1, source_target_pairs={{0,2},{1,3},{2,0},{3,1},{4,6},{5,7},{6,4},{7,5},{8,10},{9,11},{10,... | collective-permute-start | bytes 58376 | tf_op jit(solution)/shard_map/ppermute | solution.py:621
  14.3 2.2 %collective-permute-done.4 = bf16[1,8,16,76]{3,1,2,0:T(8,128)(2,1)S(1)} collective-permute-done((bf16[1,8,16,76]{3,1,2,0:T(8,128)(2,1)S(1)}, bf16[1,8,16,76]{3,1,2,0:T(8,128)(2,1)S(1)}, u32[]{:S(2)}, u32[]{:S(2)}) %collective-permute-start.4) | collective-permute-done | bytes 19488 | tf_op jit(solution)/shard_map/ppermute | solution.py:621
  16.5 0.1 broadcast_select_fusion.3
  16.6 1.5 %collective-permute-start.5 = (bf16[24,16,128]{2,1,0:T(8,128)(2,1)S(1)}, bf16[24,16,128]{2,1,0:T(8,128)(2,1)S(1)}, u32[]{:S(2)}, u32[]{:S(2)}) collective-permute-start(bf16[24,16,128]{2,1,0:T(8,128)(2,1)S(1)} %get-tuple-element.105), channel_id=1, source_target_pairs={{0,8},{8,0},{16,24},{24,16},{1,9},{9,1},{17,25},{25,17},{2,10},{10... | collective-permute-start | bytes 294920 | tf_op jit(solution)/shard_map/ppermute | solution.py:615
  18.2 0.7 collective-permute-start.6
  18.8 0.1 pad_add_fusion.refs_0_
  19.0 2.4 %collective-permute-done.5 = bf16[24,16,128]{2,1,0:T(8,128)(2,1)S(1)} collective-permute-done((bf16[24,16,128]{2,1,0:T(8,128)(2,1)S(1)}, bf16[24,16,128]{2,1,0:T(8,128)(2,1)S(1)}, u32[]{:S(2)}, u32[]{:S(2)}) %collective-permute-start.5) | collective-permute-done | bytes 98336 | tf_op jit(solution)/shard_map/ppermute | solution.py:615
  21.6 0.2 slice.116
  21.8 0.1 pad_maximum_fusion.1
  22.0 0.2 slice.115
  22.1 0.3 fusion.6
  22.4 0.2 fusion.8.refs_2_
  22.8 10.8 %forward.1 = (f32[1536,128]{1,0:T(8,128)S(1)}, bf16[288,256]{1,0:T(8,128)(2,1)S(1)}, bf16[256,256]{1,0:T(8,128)(2,1)S(1)}, bf16[256,256]{1,0:T(8,128)(2,1)S(1)},...) custom-call(s32[4]{0:T(128)S(1)} %pad_add_fusion.refs_0_, ...), custom_call_target="tpu_custom_call" | custom-call | tf_op jit(solution)/shard_map/forward/pallas_call | solution.py:773
  33.6 11.3 %backward.1 = (f32[704,256]{1,0:T(8,128)S(1)}, bf16[704,256]{1,0:T(8,128)(2,1)S(1)}) custom-call(s32[4]{0:T(128)S(1)} %pad_add_fusion.refs_0_, bf16[98,16,128]{2,1,0:T(8,128)(2,1)S(1)} %pad.41.refs_1_, bf16[98,16,128]{2,1,0:T(8,128)(2,1)S(1)} %fusion.8.refs_2_, f32[1536,128]{1,0:T(8,128)S(1)} %get-tuple-element.39.refs_3_, ...), custom_call_target="tpu_custom_call" | custom-call | tf_op jit(solution)/shard_map/backward/pallas_call | solution.py:806
  45.0 1.6 %collective-permute-done.7 = bf16[704,256]{1,0:T(8,128)(2,1)S(1)} collective-permute-done((bf16[704,256]{1,0:T(8,128)(2,1)S(1)}, bf16[704,256]{1,0:T(8,128)(2,1)S(1)}, u32[]{:S(2)}, u32[]{:S(2)}) %collective-permute-start.7) | collective-permute-done | bytes 360480 | tf_op jit(solution)/shard_map/ppermute | solution.py:621
  46.6 0.1 convert_add_fusion
  46.8 2.5 %collective-permute-start.10 = (bf16[176,256]{1,0:T(8,128)(2,1)S(1)}, bf16[176,256]{1,0:T(8,128)(2,1)S(1)}, u32[]{:S(2)}, u32[]{:S(2)}) collective-permute-start(bf16[176,256]{1,0:T(8,128)(2,1)S(1)} %get-tuple-element.99), channel_id=1, source_target_pairs={{0,24},{8,16},{16,8},{24,0},{1,25},{9,17},{17,9},{25,1},{2,26},{10... | collective-permute-start | bytes 270344 | tf_op jit(solution)/shard_map/ppermute | solution.py:621
  49.3 3.8 %collective-permute-start.9 = (bf16[176,256]{1,0:T(8,128)(2,1)S(1)}, bf16[176,256]{1,0:T(8,128)(2,1)S(1)}, u32[]{:S(2)}, u32[]{:S(2)}) collective-permute-start(bf16[176,256]{1,0:T(8,128)(2,1)S(1)} %get-tuple-element.100), channel_id=1, source_target_pairs={{0,16},{8,24},{16,0},{24,8},{1,17},{9,25},{17,1},{25,9},{2,18},{10... | collective-permute-start | bytes 270344 | tf_op jit(solution)/shard_map/ppermute | solution.py:621
  53.1 1.0 %collective-permute-start.8 = (bf16[176,256]{1,0:T(8,128)(2,1)S(1)}, bf16[176,256]{1,0:T(8,128)(2,1)S(1)}, u32[]{:S(2)}, u32[]{:S(2)}) collective-permute-start(bf16[176,256]{1,0:T(8,128)(2,1)S(1)} %get-tuple-element.98), channel_id=1, source_target_pairs={{0,8},{8,0},{16,24},{24,16},{1,9},{9,1},{17,25},{25,17},{2,10},{10... | collective-permute-start | bytes 270344 | tf_op jit(solution)/shard_map/ppermute | solution.py:621
  54.1 2.9 %collective-permute-done.9 = bf16[176,256]{1,0:T(8,128)(2,1)S(1)} collective-permute-done((bf16[176,256]{1,0:T(8,128)(2,1)S(1)}, bf16[176,256]{1,0:T(8,128)(2,1)S(1)}, u32[]{:S(2)}, u32[]{:S(2)}) %collective-permute-start.9) | collective-permute-done | bytes 90144 | tf_op jit(solution)/shard_map/ppermute | solution.py:621
  56.9 1.7 %collective-permute-done.8 = bf16[176,256]{1,0:T(8,128)(2,1)S(1)} collective-permute-done((bf16[176,256]{1,0:T(8,128)(2,1)S(1)}, bf16[176,256]{1,0:T(8,128)(2,1)S(1)}, u32[]{:S(2)}, u32[]{:S(2)}) %collective-permute-start.8) | collective-permute-done | bytes 90144 | tf_op jit(solution)/shard_map/ppermute | solution.py:621
  58.7 1.8 %collective-permute-start.11 = (bf16[176,256]{1,0:T(8,128)(2,1)S(1)}, bf16[176,256]{1,0:T(8,128)(2,1)S(1)}, u32[]{:S(2)}, u32[]{:S(2)}) collective-permute-start(bf16[176,256]{1,0:T(8,128)(2,1)S(1)} %add_convert_fusion.2), channel_id=1, source_target_pairs={{0,2},{1,3},{2,0},{3,1},{4,6},{5,7},{6,4},{7,5},{8,10},{9,11},{10,... | collective-permute-start | bytes 270344 | tf_op jit(solution)/shard_map/ppermute | solution.py:621
  60.5 2.8 %collective-permute-done.11 = bf16[176,256]{1,0:T(8,128)(2,1)S(1)} collective-permute-done((bf16[176,256]{1,0:T(8,128)(2,1)S(1)}, bf16[176,256]{1,0:T(8,128)(2,1)S(1)}, u32[]{:S(2)}, u32[]{:S(2)}) %collective-permute-start.11) | collective-permute-done | bytes 90144 | tf_op jit(solution)/shard_map/ppermute | solution.py:621
  63.3 3.0 %collective-permute-start.12 = (bf16[176,256]{1,0:T(8,128)(2,1)S(1)}, bf16[176,256]{1,0:T(8,128)(2,1)S(1)}, u32[]{:S(2)}, u32[]{:S(2)}) collective-permute-start(bf16[176,256]{1,0:T(8,128)(2,1)S(1)} %add_convert_fusion.1), channel_id=1, source_target_pairs={{0,4},{1,5},{2,6},{3,7},{4,0},{5,1},{6,2},{7,3},{8,12},{9,13},{10,... | collective-permute-start | bytes 270344 | tf_op jit(solution)/shard_map/ppermute | solution.py:621
  66.3 2.5 %collective-permute-done.12 = bf16[176,256]{1,0:T(8,128)(2,1)S(1)} collective-permute-done((bf16[176,256]{1,0:T(8,128)(2,1)S(1)}, bf16[176,256]{1,0:T(8,128)(2,1)S(1)}, u32[]{:S(2)}, u32[]{:S(2)}) %collective-permute-start.12) | collective-permute-done | bytes 90144 | tf_op jit(solution)/shard_map/ppermute | solution.py:621
  68.9 1.4 %collective-permute-start.15 = (bf16[176,256]{1,0:T(8,128)(2,1)S(1)}, bf16[176,256]{1,0:T(8,128)(2,1)S(1)}, u32[]{:S(2)}, u32[]{:S(2)}) collective-permute-start(bf16[176,256]{1,0:T(8,128)(2,1)S(1)} %add_convert_fusion), channel_id=1, source_target_pairs={{0,24},{8,16},{16,8},{24,0},{1,25},{9,17},{17,9},{25,1},{2,26},{10... | collective-permute-start | bytes 270344 | tf_op jit(solution)/shard_map/ppermute | solution.py:621
  70.3 0.7 collective-permute-start.14
  71.0 1.4 %collective-permute-start.13 = (bf16[176,256]{1,0:T(8,128)(2,1)S(1)}, bf16[176,256]{1,0:T(8,128)(2,1)S(1)}, u32[]{:S(2)}, u32[]{:S(2)}) collective-permute-start(bf16[176,256]{1,0:T(8,128)(2,1)S(1)} %add_convert_fusion), channel_id=1, source_target_pairs={{0,8},{8,0},{16,24},{24,16},{1,9},{9,1},{17,25},{25,17},{2,10},{10... | collective-permute-start | bytes 270344 | tf_op jit(solution)/shard_map/ppermute | solution.py:621
  72.4 2.0 %collective-permute-done.15 = bf16[176,256]{1,0:T(8,128)(2,1)S(1)} collective-permute-done((bf16[176,256]{1,0:T(8,128)(2,1)S(1)}, bf16[176,256]{1,0:T(8,128)(2,1)S(1)}, u32[]{:S(2)}, u32[]{:S(2)}) %collective-permute-start.15) | collective-permute-done | bytes 90144 | tf_op jit(solution)/shard_map/ppermute | solution.py:621
  74.4 0.9 %collective-permute-done.14 = bf16[176,256]{1,0:T(8,128)(2,1)S(1)} collective-permute-done((bf16[176,256]{1,0:T(8,128)(2,1)S(1)}, bf16[176,256]{1,0:T(8,128)(2,1)S(1)}, u32[]{:S(2)}, u32[]{:S(2)}) %collective-permute-start.14) | collective-permute-done | bytes 90144 | tf_op jit(solution)/shard_map/ppermute | solution.py:621
  75.3 0.2 collective-permute-done.13
  75.7 0.9 %copy.46 = f32[12,64,128]{2,1,0:T(8,128)} copy(f32[12,64,128]{2,0,1:T(8,128)S(1)} %bitcast.48) | data formatting | bytes 786432
  76.5 0.8 %collective-permute-done.16.refs_2_ = bf16[704,256]{1,0:T(8,128)(2,1)S(1)} collective-permute-done((bf16[704,256]{1,0:T(8,128)(2,1)S(1)}, bf16[704,256]{1,0:T(8,128)(2,1)S(1)}, u32[]{:S(2)}, u32[]{:S(2)}) %collective-permute-start.16) | collective-permute-done | bytes 360480 | tf_op jit(solution)/shard_map/ppermute | solution.py:621
  77.3 2.0 %finish.1 = (f32[3,3,12,64]{3,2,1,0:T(8,128)}, f32[576,64]{1,0:T(8,128)}, f32[576,256]{1,0:T(8,128)}, f32[576,256]{1,0:T(8,128)}, f32[3,3,12,64]{3,2,1,0:T(8,128...) custom-call(s32[4]{0:T(128)S(1)} %pad_add_fusion.refs_0_, ...), custom_call_target="tpu_custom_call" | custom-call | tf_op jit(solution)/shard_map/finish/pallas_call | solution.py:827
  (46 shorter events, 1.0 us)
Async XLA Ops:
  0.6 3.7 %copy-start.5 = (bf16[12,64,128]{2,1,0:T(8,128)(2,1)S(1)}, bf16[12,64,128]{2,1,0:T(8,128)(2,1)}, u32[]{:S(2)}) copy-start(bf16[12,64,128]{2,1,0:T(8,128)(2,1)} %param.23) | copy-start | bytes 589828
  1.5 3.1 %collective-permute-start.2 = (bf16[2,16,268]{2,0,1:T(2,128)(2,1)S(1)}, bf16[2,16,268]{2,0,1:T(2,128)(2,1)S(1)}, u32[]{:S(2)}, u32[]{:S(2)}) collective-permute-start(bf16[2,16,268]{2,0,1:T(2,128)(2,1)S(1)} %pad.37), channel_id=1, source_target_pairs={{0,1},{1,0},{2,3},{3,2},{4,5},{5,4},{6,7},{7,6},{8,9},{9,8},{10,11... | collective-permute-start | bytes 51464 | tf_op jit(solution)/shard_map/ppermute | solution.py:621
  3.5 6.8 %collective-permute-start = (bf16[12,12,64]{2,0,1:T(8,128)(2,1)S(1)}, bf16[12,12,64]{2,0,1:T(8,128)(2,1)S(1)}, u32[]{:S(2)}, u32[]{:S(2)}) collective-permute-start(bf16[12,12,64]{2,0,1:T(8,128)(2,1)S(1)} %get-tuple-element.113), channel_id=1, source_target_pairs={{0,1},{1,0},{2,3},{3,2},{4,5},{5,4},{6,7},{7,6},{8,9},{9,8},{10,11... | collective-permute-start | bytes 55304 | tf_op jit(solution)/shard_map/ppermute | solution.py:615
  3.6 6.7 %collective-permute-start.1 = (bf16[12,12,64]{2,0,1:T(8,128)(2,1)S(1)}, bf16[12,12,64]{2,0,1:T(8,128)(2,1)S(1)}, u32[]{:S(2)}, u32[]{:S(2)}) collective-permute-start(bf16[12,12,64]{2,0,1:T(8,128)(2,1)S(1)} %get-tuple-element.114), channel_id=1, source_target_pairs={{1,2},{2,1},{3,4},{4,3},{5,6},{6,5},{9,10},{10,9},{11,12},{12,11},... | collective-permute-start | bytes 55304 | tf_op jit(solution)/shard_map/ppermute | solution.py:616
  4.9 7.3 %collective-permute-start.3 = (bf16[2,4,16,76]{3,1,2,0:T(4,128)(2,1)S(1)}, bf16[2,4,16,76]{3,1,2,0:T(4,128)(2,1)S(1)}, u32[]{:S(2)}, u32[]{:S(2)}) collective-permute-start(bf16[2,4,16,76]{3,1,2,0:T(4,128)(2,1)S(1)} %get-tuple-element.119), channel_id=1, source_target_pairs={{0,4},{1,5},{2,6},{3,7},{4,0},{5,1},{6,2},{7,3},{8,12},{9,13},{10,... | collective-permute-start | bytes 58376 | tf_op jit(solution)/shard_map/ppermute | solution.py:621
  12.3 4.2 %collective-permute-start.4 = (bf16[1,8,16,76]{3,1,2,0:T(8,128)(2,1)S(1)}, bf16[1,8,16,76]{3,1,2,0:T(8,128)(2,1)S(1)}, u32[]{:S(2)}, u32[]{:S(2)}) collective-permute-start(bf16[1,8,16,76]{3,1,2,0:T(8,128)(2,1)S(1)} %get-tuple-element.117), channel_id=1, source_target_pairs={{0,2},{1,3},{2,0},{3,1},{4,6},{5,7},{6,4},{7,5},{8,10},{9,11},{10,... | collective-permute-start | bytes 58376 | tf_op jit(solution)/shard_map/ppermute | solution.py:621
  16.6 4.7 %collective-permute-start.5 = (bf16[24,16,128]{2,1,0:T(8,128)(2,1)S(1)}, bf16[24,16,128]{2,1,0:T(8,128)(2,1)S(1)}, u32[]{:S(2)}, u32[]{:S(2)}) collective-permute-start(bf16[24,16,128]{2,1,0:T(8,128)(2,1)S(1)} %get-tuple-element.105), channel_id=1, source_target_pairs={{0,8},{8,0},{16,24},{24,16},{1,9},{9,1},{17,25},{25,17},{2,10},{10... | collective-permute-start | bytes 294920 | tf_op jit(solution)/shard_map/ppermute | solution.py:615
  18.2 3.2 %collective-permute-start.6 = (bf16[24,16,128]{2,1,0:T(8,128)(2,1)S(1)}, bf16[24,16,128]{2,1,0:T(8,128)(2,1)S(1)}, u32[]{:S(2)}, u32[]{:S(2)}) collective-permute-start(bf16[24,16,128]{2,1,0:T(8,128)(2,1)S(1)} %get-tuple-element.106), channel_id=1, source_target_pairs={{8,16},{16,8},{9,17},{17,9},{10,18},{18,10},{11,19},{19,11},{12,20... | collective-permute-start | bytes 294920 | tf_op jit(solution)/shard_map/ppermute | solution.py:616
  21.9 0.8 %copy-start = (f32[256]{0:T(256)S(1)}, f32[256]{0:T(256)}, u32[]{:S(2)}) copy-start(f32[256]{0:T(256)} %param.20) | copy-start | bytes 3076
  21.9 0.8 %copy-start.1 = (f32[256]{0:T(256)S(1)}, f32[256]{0:T(256)}, u32[]{:S(2)}) copy-start(f32[256]{0:T(256)} %param.21) | copy-start | bytes 3076
  21.9 0.8 copy-start.2
  21.9 0.8 copy-start.3
  22.0 0.8 copy-start.4
  44.9 1.7 %collective-permute-start.7 = (bf16[704,256]{1,0:T(8,128)(2,1)S(1)}, bf16[704,256]{1,0:T(8,128)(2,1)S(1)}, u32[]{:S(2)}, u32[]{:S(2)}) collective-permute-start(bf16[704,256]{1,0:T(8,128)(2,1)S(1)} %get-tuple-element.52), channel_id=1, source_target_pairs={{0,1},{1,0},{2,3},{3,2},{4,5},{5,4},{6,7},{7,6},{8,9},{9,8},{10,11... | collective-permute-start | bytes 1081352 | tf_op jit(solution)/shard_map/ppermute | solution.py:621
  46.8 7.3 %collective-permute-start.10 = (bf16[176,256]{1,0:T(8,128)(2,1)S(1)}, bf16[176,256]{1,0:T(8,128)(2,1)S(1)}, u32[]{:S(2)}, u32[]{:S(2)}) collective-permute-start(bf16[176,256]{1,0:T(8,128)(2,1)S(1)} %get-tuple-element.99), channel_id=1, source_target_pairs={{0,24},{8,16},{16,8},{24,0},{1,25},{9,17},{17,9},{25,1},{2,26},{10... | collective-permute-start | bytes 270344 | tf_op jit(solution)/shard_map/ppermute | solution.py:621
  49.3 7.7 %collective-permute-start.9 = (bf16[176,256]{1,0:T(8,128)(2,1)S(1)}, bf16[176,256]{1,0:T(8,128)(2,1)S(1)}, u32[]{:S(2)}, u32[]{:S(2)}) collective-permute-start(bf16[176,256]{1,0:T(8,128)(2,1)S(1)} %get-tuple-element.100), channel_id=1, source_target_pairs={{0,16},{8,24},{16,0},{24,8},{1,17},{9,25},{17,1},{25,9},{2,18},{10... | collective-permute-start | bytes 270344 | tf_op jit(solution)/shard_map/ppermute | solution.py:621
  53.1 5.6 %collective-permute-start.8 = (bf16[176,256]{1,0:T(8,128)(2,1)S(1)}, bf16[176,256]{1,0:T(8,128)(2,1)S(1)}, u32[]{:S(2)}, u32[]{:S(2)}) collective-permute-start(bf16[176,256]{1,0:T(8,128)(2,1)S(1)} %get-tuple-element.98), channel_id=1, source_target_pairs={{0,8},{8,0},{16,24},{24,16},{1,9},{9,1},{17,25},{25,17},{2,10},{10... | collective-permute-start | bytes 270344 | tf_op jit(solution)/shard_map/ppermute | solution.py:621
  58.7 4.6 %collective-permute-start.11 = (bf16[176,256]{1,0:T(8,128)(2,1)S(1)}, bf16[176,256]{1,0:T(8,128)(2,1)S(1)}, u32[]{:S(2)}, u32[]{:S(2)}) collective-permute-start(bf16[176,256]{1,0:T(8,128)(2,1)S(1)} %add_convert_fusion.2), channel_id=1, source_target_pairs={{0,2},{1,3},{2,0},{3,1},{4,6},{5,7},{6,4},{7,5},{8,10},{9,11},{10,... | collective-permute-start | bytes 270344 | tf_op jit(solution)/shard_map/ppermute | solution.py:621
  63.3 5.5 %collective-permute-start.12 = (bf16[176,256]{1,0:T(8,128)(2,1)S(1)}, bf16[176,256]{1,0:T(8,128)(2,1)S(1)}, u32[]{:S(2)}, u32[]{:S(2)}) collective-permute-start(bf16[176,256]{1,0:T(8,128)(2,1)S(1)} %add_convert_fusion.1), channel_id=1, source_target_pairs={{0,4},{1,5},{2,6},{3,7},{4,0},{5,1},{6,2},{7,3},{8,12},{9,13},{10,... | collective-permute-start | bytes 270344 | tf_op jit(solution)/shard_map/ppermute | solution.py:621
  68.9 5.5 %collective-permute-start.15 = (bf16[176,256]{1,0:T(8,128)(2,1)S(1)}, bf16[176,256]{1,0:T(8,128)(2,1)S(1)}, u32[]{:S(2)}, u32[]{:S(2)}) collective-permute-start(bf16[176,256]{1,0:T(8,128)(2,1)S(1)} %add_convert_fusion), channel_id=1, source_target_pairs={{0,24},{8,16},{16,8},{24,0},{1,25},{9,17},{17,9},{25,1},{2,26},{10... | collective-permute-start | bytes 270344 | tf_op jit(solution)/shard_map/ppermute | solution.py:621
  70.3 5.0 %collective-permute-start.14 = (bf16[176,256]{1,0:T(8,128)(2,1)S(1)}, bf16[176,256]{1,0:T(8,128)(2,1)S(1)}, u32[]{:S(2)}, u32[]{:S(2)}) collective-permute-start(bf16[176,256]{1,0:T(8,128)(2,1)S(1)} %add_convert_fusion), channel_id=1, source_target_pairs={{0,16},{8,24},{16,0},{24,8},{1,17},{9,25},{17,1},{25,9},{2,18},{10... | collective-permute-start | bytes 270344 | tf_op jit(solution)/shard_map/ppermute | solution.py:621
  71.0 4.5 %collective-permute-start.13 = (bf16[176,256]{1,0:T(8,128)(2,1)S(1)}, bf16[176,256]{1,0:T(8,128)(2,1)S(1)}, u32[]{:S(2)}, u32[]{:S(2)}) collective-permute-start(bf16[176,256]{1,0:T(8,128)(2,1)S(1)} %add_convert_fusion), channel_id=1, source_target_pairs={{0,8},{8,0},{16,24},{24,16},{1,9},{9,1},{17,25},{25,17},{2,10},{10... | collective-permute-start | bytes 270344 | tf_op jit(solution)/shard_map/ppermute | solution.py:621
  75.6 1.7 %collective-permute-start.16 = (bf16[704,256]{1,0:T(8,128)(2,1)S(1)}, bf16[704,256]{1,0:T(8,128)(2,1)S(1)}, u32[]{:S(2)}, u32[]{:S(2)}) collective-permute-start(bf16[704,256]{1,0:T(8,128)(2,1)S(1)} %pad_maximum_fusion.2.refs_1_), channel_id=1, source_target_pairs={{0,1},{1,0},{2,3},{3,2},{4,5},{5,4},{6,7},{7,6},{8,9},{9,8},{10,11... | collective-permute-start | bytes 1081352 | tf_op jit(solution)/shard_map/ppermute | solution.py:621

commit v2 on v1

--- a/solution.py
+++ b/solution.py
@@ -114,7 +114,7 @@
     return jnp.where(chosen, 1.0, 0.0).astype(BF)
 
 
-def select(core, s0_ref, s5_ref, e_ref, turn3_ref, turn4_ref):
+def select(core, s0_ref, s5_ref, turn3_ref, turn4_ref):
     m, lane = grid(PITCH, 256)
     for s in range(3):
         after = m + 31 + s + HALO + core * COLS
@@ -128,15 +128,13 @@
         here = jnp.where(col < 0, col + 140, jnp.where(col < 128, col, col + 12))
         here = jnp.where(col < -FINE_HALO, -1, here)
         s5_ref[u * PITCH : (u + 1) * PITCH, :] = one_hot(lane == jnp.where(m < 8, beyond, here))
-    cell, lane = grid(512, 512)
-    e_ref[...] = one_hot(lane == ((cell >> 5) & 3) * 128 + (cell & 31) * 4 + (cell >> 7))
     new, old = grid(256, 256)
     turn3_ref[...] = one_hot(old == 4 * (new & 63) + 2 * (new >> 7) + 1 - ((new >> 6) & 1))
     turn4_ref[...] = one_hot(old == 4 * (new & 63) + 2 * ((new >> 6) & 1) + (new >> 7))
 
 
-def small_terms(perms, small, bias_ref, bias5_ref):
-    b1_ref, b2_ref, b3_ref, b4_ref, b5_ref = small
+def small_terms(perms, small, bias_ref):
+    b1_ref, b2_ref, b3_ref, b4_ref = small
     perm3, perm4 = perms
 
     def wide(value):
@@ -147,21 +145,17 @@
     bias_ref[16:24, 0:256] = split_dot(wide(b3_ref[...]), perm3)
     four = split_dot(wide(b4_ref[...]), perm4)
     bias_ref[24:32, :] = jnp.concatenate([four, four], axis=1)
-    chans = b5_ref.shape[1]
-    five = jnp.concatenate([b5_ref[...], jnp.zeros((1, 128 - chans), F32)], axis=1)
-    five = sum(lane_roll(five, 16 * n) for n in range(8))
-    bias5_ref[...] = jnp.concatenate([jnp.broadcast_to(five, (128, 128)).T] * 2, axis=0)
 
 
 def arrange(perms, weights, there, back):
     w1_ref, w2_ref, w3_ref, w4_ref, w5_ref = weights
-    k1, k2, k3, k4, k5, k5s = there
+    k1, k2, k3, k4 = there
     r5, r4, r3, r2 = back
     perm3, perm4 = perms
     chans = w1_ref.shape[2]
     w3p = dotn(w3_ref[...], perm3).astype(BF)
     w4p = dotn(w4_ref[...], perm4).astype(BF)
-    for ref in (k1, k2, k3, k4, k5, k5s, r4, r3, r2):
+    for ref in (k1, k2, k3, k4, r4, r3, r2):
         ref[...] = jnp.zeros(ref.shape, BF)
     for r in range(3):
         for s in range(3):
@@ -192,15 +186,36 @@
                         r4[(1 - q) * 64 : (2 - q) * 64, at : at + 256] = block
                     if q_src == 1 - q and s == 2 - 2 * q:
                         r4[128 + (1 - q) * 64 : 128 + (2 - q) * 64, at : at + 256] = block
-    gap_rows = jnp.zeros((16 - chans, 64), F32)
-    turned = []
+    columns = output_columns(w5_ref)
+    for p in range(4):
+        for v in range(3):
+            r5[p * 64 : (p + 1) * 64, v * 128 : (v + 1) * 128] = lane_roll(
+                columns[2 - v].T, 16 * p
+            ).astype(BF)
+
+
+def output_columns(w5_ref):
+    gap_rows = jnp.zeros((16 - w5_ref.shape[2], 64), F32)
+    columns = []
     for s in range(3):
         column = []
         for r in (2, 1, 0):
             column += [w5_ref[r, s].astype(F32), gap_rows]
-        turned.append(jnp.concatenate(column + [jnp.zeros((80, 64), F32)], axis=0))
-    w5 = [value.T for value in turned]
-    turned = [value.astype(BF) for value in turned]
+        columns.append(jnp.concatenate(column + [jnp.zeros((80, 64), F32)], axis=0))
+    return columns
+
+
+def fine_field(kept_hbm, w5_ref, b5_ref, fine_ref, e_ref, k5, k5s, a4, sem):
+    copy = pltpu.make_async_copy(kept_hbm, a4, sem)
+    copy.start()
+    low = low_half()
+    cell, lane = grid(512, 512)
+    e_ref[...] = one_hot(lane == ((cell >> 5) & 3) * 128 + (cell & 31) * 4 + (cell >> 7))
+    k5[...] = jnp.zeros(k5.shape, BF)
+    k5s[...] = jnp.zeros(k5s.shape, BF)
+    columns = output_columns(w5_ref)
+    w5 = [value.T for value in columns]
+    columns = [value.astype(BF) for value in columns]
     empty = jnp.zeros((64, 64), BF)
     for t in range(6):
         at = 64 if t == 0 else (1536 if t == 5 else 512 + ((t - 1) // 2) * 512 + ((t - 1) % 2) * 64)
@@ -212,14 +227,47 @@
             for src in range(4):
                 for q in range(max(src - 1, 0), min(src + 1, 3) + 1):
                     k5[q * 64 + p * 16 : q * 64 + p * 16 + 16, at + src * 128 : at + src * 128 + 64] = (
-                        turned[src - q + 1][b * 16 : b * 16 + 16, :]
+                        columns[src - q + 1][b * 16 : b * 16 + 16, :]
                     )
         rows = [lane_roll(w5[s], 16 * (t - 2)).astype(BF)[:, :64] for s in (0, 2)]
         k5s[side : side + 64, :] = jnp.concatenate([rows[0], empty], axis=1)
         k5s[512 + side : 512 + side + 64, :] = jnp.concatenate([empty, rows[1]], axis=1)
-    for p in range(4):
-        for v in range(3):
-            r5[p * 64 : (p + 1) * 64, v * 128 : (v + 1) * 128] = lane_roll(w5[2 - v], 16 * p).astype(BF)
+    chans = b5_ref.shape[1]
+    five = jnp.concatenate([b5_ref[...], jnp.zeros((1, 128 - chans), F32)], axis=1)
+    five = sum(lane_roll(five, 16 * n) for n in range(8))
+    five = jnp.concatenate([jnp.broadcast_to(five, (128, 128)).T] * 2, axis=0)
+    copy.wait()
+    size = ROWS * PITCH
+    wide = size + 32
+    at = OWN - 16
+    side = []
+    for low_lane in (384, 0):
+        side.append(take(a4, at - PITCH, wide, 512 + low_lane, 640 + low_lane))
+        side.append(take(a4, at, wide, low_lane, low_lane + 128))
+        side.append(take(a4, at, wide, 512 + low_lane, 640 + low_lane))
+        side.append(take(a4, at + PITCH, wide, low_lane, low_lane + 128))
+    side = dotn(jnp.concatenate(side, axis=1), k5s[...])
+    side = jnp.where(low, roll(side, 1), roll(side, -1))[16 : 16 + size]
+    side = side.reshape(ROWS, PITCH, 128)[:, 16:48, :].reshape(ROWS * COLS, 128).T
+    field = jnp.concatenate(
+        [own(a4, 512, 1024, -1), own(a4, 0, 1024), own(a4, 0, 512, 1)], axis=1
+    )
+    z = dott(k5[...], field) + five[:, 0:1]
+    z = [z[0:64] + side[0:64], z[64:128], z[128:192], z[192:256] + side[64:128]]
+    z = jnp.concatenate(
+        [jnp.concatenate([z[q][:, g * 128 : (g + 1) * 128] for q in range(4)], axis=1) for g in range(4)],
+        axis=0,
+    )
+    high = z.astype(BF)
+    rest = (z - high.astype(F32)).astype(BF)
+    z = dotn(jnp.concatenate([rest, high], axis=0), e_ref[...])
+    z = z[0:256] + z[256:512]
+    for g in range(4):
+        for n in range(4):
+            for p in range(4):
+                fine_ref[16 * g + 4 * n + p] = z[
+                    g * 64 + p * 16 : g * 64 + p * 16 + 16, n * 128 : (n + 1) * 128
+                ]
 
 
 def in_plane(extent, pos_ref, mask):
@@ -237,7 +285,9 @@
 def forward(
     extent,
     pos_ref,
-    dx_ref,
+    window_ref,
+    above_ref,
+    below_ref,
     w1_hbm,
     w2_hbm,
     w3_hbm,
@@ -247,7 +297,6 @@
     b2_ref,
     b3_ref,
     b4_ref,
-    b5_ref,
     mask,
     s5_ref,
     turn3_ref,
@@ -262,22 +311,18 @@
     x3,
     a3,
     a4,
-    fine_ref,
     bias_ref,
-    bias5_ref,
     s0_ref,
-    e_ref,
     k1,
     k2,
     k3,
     k4,
-    k5,
-    k5s,
     w1_ref,
     w2_ref,
     w3_ref,
     w4_ref,
     w5_ref,
+    dx_ref,
     sems,
 ):
     copies = [
@@ -294,11 +339,20 @@
     ]
     for copy in copies:
         copy.start()
-    small = (b1_ref, b2_ref, b3_ref, b4_ref, b5_ref)
-    select(pos_ref[2], s0_ref, s5_ref, e_ref, turn3_ref, turn4_ref)
+    small = (b1_ref, b2_ref, b3_ref, b4_ref)
+    select(pos_ref[2], s0_ref, s5_ref, turn3_ref, turn4_ref)
     in_plane(extent, pos_ref, mask)
     low = low_half()
     clear_margins(((x0, 2, 30), (x1, 3, 30), (x2, 4, 29), (x3, 5, 29), (a4, 5, 29)))
+
+    lane = lax.broadcasted_iota(jnp.int32, (1, 128), 1)
+    dx_ref[0:2] = jnp.zeros((2, 16, 128), BF)
+    dx_ref[8:24] = window_ref[...]
+    dx_ref[30:32] = jnp.zeros((2, 16, 128), BF)
+    for ref, at in ((above_ref, 2), (below_ref, 24)):
+        sent = ref[FINE_HALO : FINE_HALO + HALO].reshape(HALO * 16, 128).astype(F32)
+        sent = jnp.where(lane < 2 * COLS + 2 * HALO, lane_roll(sent, -2 * FINE_HALO), 0.0)
+        dx_ref[at : at + HALO] = sent.astype(BF).reshape(HALO, 16, 128)
 
     def coarse_pair(n):
         lines = []
@@ -318,11 +372,11 @@
     for copy in copies:
         copy.wait()
     perms = (turn3_ref[...].T, turn4_ref[...].T)
-    small_terms(perms, small, bias_ref, bias5_ref)
+    small_terms(perms, small, bias_ref)
     arrange(
         perms,
         (w1_ref, w2_ref, w3_ref, w4_ref, w5_ref),
-        (k1, k2, k3, k4, k5, k5s),
+        (k1, k2, k3, k4),
         (r5, r4, r3, r2),
     )
 
@@ -373,44 +427,14 @@
 
     blocks(5, 24 // N4, N4, conv_four)
 
-    size = ROWS * PITCH
-    wide = size + 32
-    at = OWN - 16
-    side = []
-    for low_lane in (384, 0):
-        side.append(take(a4, at - PITCH, wide, 512 + low_lane, 640 + low_lane))
-        side.append(take(a4, at, wide, low_lane, low_lane + 128))
-        side.append(take(a4, at, wide, 512 + low_lane, 640 + low_lane))
-        side.append(take(a4, at + PITCH, wide, low_lane, low_lane + 128))
-    side = dotn(jnp.concatenate(side, axis=1), k5s[...])
-    side = jnp.where(low, roll(side, 1), roll(side, -1))[16 : 16 + size]
-    side = side.reshape(ROWS, PITCH, 128)[:, 16:48, :].reshape(ROWS * COLS, 128).T
-    field = jnp.concatenate(
-        [own(a4, 512, 1024, -1), own(a4, 0, 1024), own(a4, 0, 512, 1)], axis=1
-    )
-    z = dott(k5[...], field) + bias5_ref[:, 0:1]
-    z = [z[0:64] + side[0:64], z[64:128], z[128:192], z[192:256] + side[64:128]]
-    z = jnp.concatenate(
-        [jnp.concatenate([z[q][:, g * 128 : (g + 1) * 128] for q in range(4)], axis=1) for g in range(4)],
-        axis=0,
-    )
-    high = z.astype(BF)
-    rest = (z - high.astype(F32)).astype(BF)
-    z = dotn(jnp.concatenate([rest, high], axis=0), e_ref[...])
-    z = z[0:256] + z[256:512]
-    for g in range(4):
-        for n in range(4):
-            for p in range(4):
-                fine_ref[16 * g + 4 * n + p] = z[
-                    g * 64 + p * 16 : g * 64 + p * 16 + 16, n * 128 : (n + 1) * 128
-                ]
-
 
 def backward(
     scale,
     pos_ref,
-    center_ref,
-    rim_ref,
+    above_ref,
+    below_ref,
+    cot_ref,
+    sides_ref,
     mask,
     s5_ref,
     r5,
@@ -425,15 +449,43 @@
     a4,
     keep_ref,
     send_ref,
+    kept_hbm,
     c5,
     b4,
     b3,
     b2,
     b1,
     g_ref,
+    center_ref,
+    rim_ref,
+    sem,
 ):
+    kept = pltpu.make_async_copy(a4, kept_hbm, sem)
+    kept.start()
     low = low_half()
     clear_margins(((c5, 5, 29), (b4, 5, 29), (b3, 6, 27), (b2, 7, 27)))
+
+    n = FINE_HALO
+    rows = 4 * ROWS
+    lane = lax.broadcasted_iota(jnp.int32, (1, 128), 1)
+    for ref, inside, parts in (
+        (center_ref, cot_ref, slice(0, n)),
+        (rim_ref, sides_ref, slice(n, 2 * n)),
+    ):
+        ref[0] = jnp.zeros((16, 128), BF)
+        ref[1 : n + 1] = above_ref[parts]
+        ref[n + 1 : n + 1 + rows] = inside[...]
+        ref[n + 1 + rows : 2 * n + 1 + rows] = below_ref[parts]
+        ref[2 * n + 1 + rows :] = jnp.zeros((9, 16, 128), BF)
+    count = (2 * n + 10 + rows) * 16
+    sides = rim_ref[...].reshape(count, 128).astype(F32)
+    before = lane_roll(sides[: count - 64], 64 - n)
+    corner = lane_roll(center_ref[...].reshape(count, 128).astype(F32)[: count - 64], 77)
+    before = jnp.where(lane < 64 + n, before, corner)
+    before = jnp.concatenate([jnp.zeros((64, 128), F32), before], axis=0)
+    sides = jnp.where(lane < 2 * n, sides, jnp.where(lane < 64, 0.0, before))
+    sides = jnp.where(lane < 65 + n, sides, 0.0)
+    rim_ref[...] = sides.astype(BF).reshape(count // 16, 16, 128)
 
     def cot_pair(n):
         lines = []
@@ -574,6 +626,7 @@
     core = pos_ref[2]
     keep_ref[...] = g_ref[pl.ds(pl.multiple_of(core * half, 16), half), :]
     send_ref[...] = g_ref[pl.ds(pl.multiple_of((1 - core) * half, 16), half), :].astype(BF)
+    kept.wait()
 
 
 def finish(chans, places, pos_ref, mine_ref, other_ref, turn3_ref, turn4_ref, g1, g2, g3, g4, g5, c1, c2, c3, c4, c5, full):
@@ -621,7 +674,7 @@
     return lax.ppermute(block, axis, [(i, i ^ flip) for i in range(lax.axis_size(axis))])
 
 
-def chip_window(coarse):
+def chip_window(coarse, beside):
     gy, at = lax.axis_size("gy"), lax.axis_index("gy")
     chans, each, ny = coarse.shape
     cols = 2 * ny // gy
@@ -645,23 +698,24 @@
             jnp.concatenate([mine, other], axis=1),
         )
         flip, bits = flip // 2, bits + 1
+        if bits == 1:
+            held, beside = lax.optimization_barrier((held, beside))
     tail = (2 * each,) + held.shape[2:]
     held = held.reshape((2,) * bits + tail)
     held = held.transpose(tuple(reversed(range(bits))) + (bits, bits + 1, bits + 2))
-    return held.reshape((gy * each,) + tail[1:])
-
-
-def halo_lines(coarse, cotangent):
+    return held.reshape((gy * each,) + tail[1:]), beside
+
+
+def halo_pieces(coarse, cotangent):
     n = FINE_HALO
-    chans = coarse.shape[0]
-    left, right = exchange(
-        "gy", cotangent[:, :, :n].transpose(2, 0, 1), cotangent[:, :, -n:].transpose(2, 0, 1)
-    )
-    got = chip_window(coarse)
+    spare = 16 - coarse.shape[0]
+    edges = (cotangent[:, :, :n].transpose(2, 0, 1), cotangent[:, :, -n:].transpose(2, 0, 1))
+    got, edges = chip_window(coarse, edges)
+    left, right = exchange("gy", *edges)
     wide = got.shape[2]
-    cot = jnp.pad(cotangent.transpose(1, 0, 2), ((0, 0), (0, 16 - chans), (0, 0)))
+    cot = jnp.pad(cotangent.transpose(1, 0, 2), ((0, 0), (0, spare), (0, 0)))
     rim = jnp.concatenate([left.transpose(2, 1, 0), right.transpose(2, 1, 0)], axis=2)
-    rim = jnp.pad(rim, ((0, 0), (0, 16 - chans), (0, 0)))
+    rim = jnp.pad(rim, ((0, 0), (0, spare), (0, 0)))
 
     def edge(cot_rows, coarse_rows):
         side = jnp.pad(got[coarse_rows], ((0, n - HALO), (0, 0), (0, 128 - 2 * n - wide)))
@@ -671,18 +725,11 @@
     first = edge(slice(0, n), slice(0, HALO))
     last = edge(slice(-n, None), slice(-HALO, None))
     above, below = exchange("gx", first, last)
-    lanes = slice(2 * n, 2 * n + wide)
-    whole = jnp.concatenate([above[n : n + HALO, :, lanes], got, below[n : n + HALO, :, lanes]])
-    lines0 = jnp.pad(whole, ((2, 2), (0, 0), (0, 128 - wide)))
-    rim = jnp.concatenate([above[n:, :, : 2 * n], rim, below[n:, :, : 2 * n]])
-    center = jnp.concatenate([above[:n], cot, below[:n]])
-    before = jnp.concatenate([rim[:, :, n:], center[:, :, 127:]], axis=2)
-    rim = jnp.pad(rim, ((1, 9), (0, 0), (0, 64 - 2 * n)))
-    before = jnp.pad(before, ((5, 5), (0, 0), (0, 63 - n)))
-    return lines0, jnp.pad(center, ((1, 9), (0, 0), (0, 0))), jnp.concatenate([rim, before], axis=2)
-
-
-def total_over_all(keep, send):
+    got = jnp.pad(got, ((0, 0), (0, 0), (0, 128 - wide)))
+    return got, above, below, cot, jnp.pad(rim, ((0, 0), (0, 0), (0, 128 - 2 * n)))
+
+
+def total_over_all(keep, send, beside):
     gx, gy = lax.axis_size("gx"), lax.axis_size("gy")
     at_x = lax.axis_index("gx")
 
@@ -697,10 +744,9 @@
     def part(place):
         return lax.dynamic_slice_in_dim(value, place * size, size, 0)
 
-    terms = [part(at_x)]
-    for d in range(1, gx):
-        terms.append(swap(part(at_x ^ d).astype(BF), "gx", d).astype(F32))
-    block = tree(terms)
+    terms = [swap(part(at_x ^ d).astype(BF), "gx", d) for d in range(1, gx)]
+    terms, beside = lax.optimization_barrier((terms, beside))
+    block = tree([part(at_x)] + [term.astype(F32) for term in terms])
     flip = 2
     while flip < gy:
         block = block.astype(BF)
@@ -708,7 +754,7 @@
         flip *= 2
     block = block.astype(BF)
     mine = jnp.concatenate([block] + [swap(block, "gx", d) for d in range(1, gx)])
-    return mine, swap(mine, "gy", 1)
+    return mine, swap(mine, "gy", 1), beside
 
 
 def local(
@@ -745,7 +791,7 @@
     def buf(width, kind=BF):
         return pltpu.VMEM((CELLS, width), kind)
 
-    lines0, center, rim = halo_lines(coarse, cotangent)
+    window, above, below, cot, rim = halo_pieces(coarse, cotangent)
     shared = (
         buf(128, F32),
         pltpu.VMEM((6 * PITCH, 256), BF),
@@ -770,44 +816,46 @@
         weight_four.reshape(576, 256),
         weight_five.transpose(0, 1, 3, 2),
     )
-    *fields, fine = pl.pallas_call(
+    fields = pl.pallas_call(
         lambda *refs: forward(extent, *refs),
-        out_shape=shared + (jax.ShapeDtypeStruct((4 * ROWS, 16, 4 * COLS), F32),),
-        in_specs=[smem, vmem] + [hbm] * 5 + [vmem] * 5,
-        out_specs=(vmem,) * 15,
+        out_shape=shared,
+        in_specs=[smem] + [vmem] * 3 + [hbm] * 5 + [vmem] * 4,
+        out_specs=(vmem,) * 14,
         scratch_shapes=[
             pltpu.VMEM((32, 512), F32),
-            pltpu.VMEM((256, 128), F32),
             pltpu.VMEM((3 * PITCH, 256), BF),
-            pltpu.VMEM((512, 512), BF),
             pltpu.VMEM((384, 128), BF),
             pltpu.VMEM((768, 128), BF),
             pltpu.VMEM((768, 256), BF),
             pltpu.VMEM((768, 512), BF),
-            pltpu.VMEM((256, 2048), BF),
-            pltpu.VMEM((1024, 128), BF),
         ]
         + [pltpu.VMEM(w.shape, BF) for w in weights]
+        + [pltpu.VMEM((32, 16, 128), BF)]
         + [pltpu.SemaphoreType.DMA((5,))],
         compiler_params=params,
         name="forward",
     )(
         pos,
-        lines0,
+        window,
+        above,
+        below,
         *[pltpu.with_memory_space_constraint(w, pltpu.HBM) for w in weights],
         bias_one.reshape(1, -1),
         bias_two.reshape(1, -1),
         bias_three.reshape(1, -1),
         bias_four.reshape(1, -1),
-        bias_five.reshape(1, -1),
     )
     fields = [near(f) for f in fields]
     half = -(-TERMS // (32 * gx)) * 16 * gx
-    keep, send = pl.pallas_call(
+    keep, send, kept = pl.pallas_call(
         lambda *refs: backward(scale, *refs),
-        out_shape=(pltpu.VMEM((half, 256), F32), pltpu.VMEM((half, 256), BF)),
-        in_specs=[smem] + [vmem] * 14,
-        out_specs=(vmem,) * 2,
+        out_shape=(
+            pltpu.VMEM((half, 256), F32),
+            pltpu.VMEM((half, 256), BF),
+            pltpu.HBM((CELLS, 1024), BF),
+        ),
+        in_specs=[smem] + [vmem] * 16,
+        out_specs=(vmem, vmem, hbm),
         scratch_shapes=[
             buf(768),
             buf(1024),
@@ -815,11 +863,29 @@
             buf(128),
             buf(128),
             pltpu.VMEM((2 * half, 256), F32),
+            pltpu.VMEM((98, 16, 128), BF),
+            pltpu.VMEM((98, 16, 128), BF),
+            pltpu.SemaphoreType.DMA,
         ],
         compiler_params=params,
         name="backward",
-    )(pos, center, rim, *fields[:2], *fields[4:])
-    mine, other = total_over_all(keep, send)
+    )(pos, above, below, cot, rim, *fields[:2], *fields[4:])
+    fine = pl.pallas_call(
+        fine_field,
+        out_shape=jax.ShapeDtypeStruct((4 * ROWS, 16, 4 * COLS), F32),
+        in_specs=[hbm, vmem, vmem],
+        out_specs=vmem,
+        scratch_shapes=[
+            pltpu.VMEM((512, 512), BF),
+            pltpu.VMEM((256, 2048), BF),
+            pltpu.VMEM((1024, 128), BF),
+            buf(1024),
+            pltpu.SemaphoreType.DMA,
+        ],
+        compiler_params=params,
+        name="fine",
+    )(pltpu.with_memory_space_constraint(kept, pltpu.HBM), weights[4], bias_five.reshape(1, -1))
+    mine, other, fine = total_over_all(keep, send, fine)
 
     def out(*shape):
         return jax.ShapeDtypeStruct(shape, F32)

time: 79.6 us -> 78 us (0.980)
  waiting for transfers between devices: 21.6 us -> 17.9 us
  Pallas kernels: 24.1 us -> 26.5 us
    ppermute x13, waiting for transfers between devices: 19.2 us -> 15.7 us  [swap(): lax.ppermute(block, axis, [(i, i ^ flip) for i in range(lax.axis_size(axi...]
    pallas_call x1 -> x2, Pallas kernels: 10.8 us -> 12.7 us  [the longest x1 8.53 us: local(): pl.pallas_call(lambda *refs: forward(extent, *refs), out_shape=shared, in...]
    unnamed x16, local copies, waits for them, and re-layouts: 1.37 us -> 2.3 us
    slice x9 -> x1, local copies, waits for them, and re-layouts: 1.64 us -> 1.14 us  [halo_pieces(): cotangent[:, :, -n:].transpose(2, 0, 1)]
  transfers between devices with their start and end apart: 17 -> 17, of which waited for: 12 -> 11; matrix products, arithmetic and copies ran while one was open for 4% -> 5% of each run, Pallas kernels for 0% -> 5%
where the time goes in v2:
time: 78 us; the launch traced here: 77.5 us
  Pallas kernels  26.5 us (34%)
  starting transfers between devices  26.4 us (34%)
  waiting for transfers between devices  17.9 us (23%)
  local copies, waits for them, and re-layouts  4.88 us (6%)
  between operations  1.06 us (1%)
    ppermute x13, starting transfers between devices, swap(): lax.ppermute(block, axis, [(i, i ^ flip) for i in range(lax.axis_size(axi...  23.1 us
    ppermute x13, waiting for transfers between devices, swap(): lax.ppermute(block, axis, [(i, i ^ flip) for i in range(lax.axis_size(axi...  15.7 us
    pallas_call x1, Pallas kernels, local(): pl.pallas_call(lambda *refs: backward(scale, *refs), out_shape=(pltpu.VME...  11.8 us
    pallas_call x1, Pallas kernels, local(): pl.pallas_call(lambda *refs: forward(extent, *refs), out_shape=shared, in...  8.53 us
    pallas_call x1, Pallas kernels, local(): pl.pallas_call(fine_field, out_shape=jax.ShapeDtypeStruct((4 * ROWS, 16,...  4.2 us
    unnamed x16, local copies, waits for them, and re-layouts  2.3 us
    ppermute x2, waiting for transfers between devices, exchange(): one = lax.ppermute(jnp.where(odd, first, last), axis, even_swap)  2.18 us
    pallas_call x1, Pallas kernels, local(): pl.pallas_call(lambda *refs: finish(chans, gx, *refs), out_shape=(out(3,...  2 us
  transfers between devices with their start and end apart: 17, of which 11 were waited for; matrix products, arithmetic and copies ran while one was open for 5% of the time, Pallas kernels for 5%

profile of v2, /device:TPU:0, one launch (start us, length us, event | category | flops | bytes accessed | tf_op | source)
XLA Modules:
  0.0 77.5 jit_solution(11409836798234376861)
XLA Ops:
  0.6 0.8 %pad.28 = bf16[2,16,268]{2,0,1:T(2,128)(2,1)S(1)} pad(bf16[2,12,256]{2,0,1:T(2,128)(2,1)} %bitcast.64, bf16[]{:T(256)} %constant.40.clone.1), padding=0_0x0_4x6_6 | pad | bytes 29442 | tf_op jit(solution)/shard_map/jit(_pad)/pad | solution.py:681
  1.4 0.5 collective-permute-start
  2.0 1.1 %fusion.9 = (bf16[12,64,12]{2,1,0:T(8,128)(2,1)S(1)}, bf16[12,64,12]{2,1,0:T(8,128)(2,1)S(1)}) fusion(bf16[12,64,128]{2,1,0:T(8,128)(2,1)} %param.23), kind=kLoop, calls=%fused_computation.47 | loop fusion | bytes 73728 | tf_op jit(solution)/shard_map/slice | solution.py:712
  3.2 1.1 %copy.37 = bf16[12,64,128]{2,0,1:T(8,128)(2,1)S(1)} copy(bf16[12,64,128]{2,1,0:T(8,128)(2,1)} %param.23) | data formatting | bytes 393216 | tf_op args[11]
  4.3 0.1 maximum_select_fusion.2
  4.4 0.1 slice_bitcast_fusion.3
  4.5 0.1 broadcast_select_fusion.9
  4.6 3.7 %collective-permute-start.1 = (bf16[2,4,16,76]{3,1,2,0:T(4,128)(2,1)S(1)}, bf16[2,4,16,76]{3,1,2,0:T(4,128)(2,1)S(1)}, u32[]{:S(2)}, u32[]{:S(2)}) collective-permute-start(bf16[2,4,16,76]{3,1,2,0:T(4,128)(2,1)S(1)} %get-tuple-element.122), channel_id=1, source_target_pairs={{0,4},{1,5},{2,6},{3,7},{4,0},{5,1},{6,2},{7,3},{8,12},{9,13},{10,... | collective-permute-start | bytes 58376 | tf_op jit(solution)/shard_map/ppermute | solution.py:674
  8.3 0.1 pad.27.refs_3_
  8.3 0.2 copy.34
  8.5 0.2 copy.35
  8.7 1.6 %collective-permute-done.1 = bf16[2,4,16,76]{3,1,2,0:T(4,128)(2,1)S(1)} collective-permute-done((bf16[2,4,16,76]{3,1,2,0:T(4,128)(2,1)S(1)}, bf16[2,4,16,76]{3,1,2,0:T(4,128)(2,1)S(1)}, u32[]{:S(2)}, u32[]{:S(2)}) %collective-permute-start.1) | collective-permute-done | bytes 19488 | tf_op jit(solution)/shard_map/ppermute | solution.py:674
  10.3 0.1 maximum_select_fusion
  10.4 0.1 collective-permute-start.2
  10.5 0.7 collective-permute-start.3
  11.1 3.4 %collective-permute-start.4 = (bf16[1,8,16,76]{3,1,2,0:T(8,128)(2,1)S(1)}, bf16[1,8,16,76]{3,1,2,0:T(8,128)(2,1)S(1)}, u32[]{:S(2)}, u32[]{:S(2)}) collective-permute-start(bf16[1,8,16,76]{3,1,2,0:T(8,128)(2,1)S(1)} %get-tuple-element.120), channel_id=1, source_target_pairs={{0,2},{1,3},{2,0},{3,1},{4,6},{5,7},{6,4},{7,5},{8,10},{9,11},{10,... | collective-permute-start | bytes 58376 | tf_op jit(solution)/shard_map/ppermute | solution.py:674
  14.6 0.3 copy.31
  14.9 1.9 %collective-permute-done.4 = bf16[1,8,16,76]{3,1,2,0:T(8,128)(2,1)S(1)} collective-permute-done((bf16[1,8,16,76]{3,1,2,0:T(8,128)(2,1)S(1)}, bf16[1,8,16,76]{3,1,2,0:T(8,128)(2,1)S(1)}, u32[]{:S(2)}, u32[]{:S(2)}) %collective-permute-start.4) | collective-permute-done | bytes 19488 | tf_op jit(solution)/shard_map/ppermute | solution.py:674
  16.9 0.1 broadcast_select_fusion.2
  17.0 1.9 %collective-permute-start.5 = (bf16[24,16,128]{2,1,0:T(8,128)(2,1)S(1)}, bf16[24,16,128]{2,1,0:T(8,128)(2,1)S(1)}, u32[]{:S(2)}, u32[]{:S(2)}) collective-permute-start(bf16[24,16,128]{2,1,0:T(8,128)(2,1)S(1)} %get-tuple-element.109), channel_id=1, source_target_pairs={{0,8},{8,0},{16,24},{24,16},{1,9},{9,1},{17,25},{25,17},{2,10},{10... | collective-permute-start | bytes 294920 | tf_op jit(solution)/shard_map/ppermute | solution.py:668
  18.9 0.7 collective-permute-start.6
  19.6 0.1 pad_add_fusion.refs_0_
  19.7 0.1 pad.29
  19.8 0.1 pad.32.refs_4_
  19.8 2.2 %collective-permute-done.5 = bf16[24,16,128]{2,1,0:T(8,128)(2,1)S(1)} collective-permute-done((bf16[24,16,128]{2,1,0:T(8,128)(2,1)S(1)}, bf16[24,16,128]{2,1,0:T(8,128)(2,1)S(1)}, u32[]{:S(2)}, u32[]{:S(2)}) %collective-permute-start.5) | collective-permute-done | bytes 98336 | tf_op jit(solution)/shard_map/ppermute | solution.py:668
  22.1 8.5 %forward.1 = (f32[1536,128]{1,0:T(8,128)S(1)}, bf16[288,256]{1,0:T(8,128)(2,1)S(1)}, bf16[256,256]{1,0:T(8,128)(2,1)S(1)}, bf16[256,256]{1,0:T(8,128)(2,1)S(1)},...) custom-call(s32[4]{0:T(128)S(1)} %pad_add_fusion.refs_0_, ...), custom_call_target="tpu_custom_call" | custom-call | tf_op jit(solution)/shard_map/forward/pallas_call | solution.py:819
  30.6 11.8 %backward.1 = (f32[704,256]{1,0:T(8,128)S(1)}, bf16[704,256]{1,0:T(8,128)(2,1)S(1)}, bf16[1536,1024]{1,0:T(8,128)(2,1)}) custom-call(s32[4]{0:T(128)S(1)} %pad_add_fusion.refs_0_, bf16[24,16,128]{2,1,0:T(8,128)(2,1)S(1)} %get-tuple-element.111.refs_2_.refs_1_, bf16[24,16,128]{2,1,0:T(8,128)(2,1)S(1)} %get-tuple-element.110.refs_3_.refs_2_, ...), custom_call_target="tpu_custom_call" | custom-call | tf_op jit(solution)/shard_map/backward/pallas_call | solution.py:850
  42.4 0.1 collective-permute-start.7
  42.5 1.6 %collective-permute-done.7 = bf16[704,256]{1,0:T(8,128)(2,1)S(1)} collective-permute-done((bf16[704,256]{1,0:T(8,128)(2,1)S(1)}, bf16[704,256]{1,0:T(8,128)(2,1)S(1)}, u32[]{:S(2)}, u32[]{:S(2)}) %collective-permute-start.7) | collective-permute-done | bytes 360480 | tf_op jit(solution)/shard_map/ppermute | solution.py:674
  44.2 0.1 convert_add_fusion
  44.3 3.0 %collective-permute-start.10 = (bf16[176,256]{1,0:T(8,128)(2,1)S(1)}, bf16[176,256]{1,0:T(8,128)(2,1)S(1)}, u32[]{:S(2)}, u32[]{:S(2)}) collective-permute-start(bf16[176,256]{1,0:T(8,128)(2,1)S(1)} %get-tuple-element.101), channel_id=1, source_target_pairs={{0,24},{8,16},{16,8},{24,0},{1,25},{9,17},{17,9},{25,1},{2,26},{10... | collective-permute-start | bytes 270344 | tf_op jit(solution)/shard_map/ppermute | solution.py:674
  47.3 4.4 %collective-permute-start.8 = (bf16[176,256]{1,0:T(8,128)(2,1)S(1)}, bf16[176,256]{1,0:T(8,128)(2,1)S(1)}, u32[]{:S(2)}, u32[]{:S(2)}) collective-permute-start(bf16[176,256]{1,0:T(8,128)(2,1)S(1)} %get-tuple-element.103), channel_id=1, source_target_pairs={{0,8},{8,0},{16,24},{24,16},{1,9},{9,1},{17,25},{25,17},{2,10},{10... | collective-permute-start | bytes 270344 | tf_op jit(solution)/shard_map/ppermute | solution.py:674
  51.7 4.2 %fine.1 = f32[64,16,128]{2,1,0:T(8,128)S(1)} custom-call(bf16[1536,1024]{1,0:T(8,128)(2,1)} %get-tuple-element.62.kept_hbm, bf16[3,3,12,64]{3,2,1,0:T(8,128)(2,1)S(1)} %bitcast.48, f32[1,12]{1,0:T(1,128)S(1)} %bitcast.53), custom_call_target="tpu_custom_call" | custom-call | tf_op jit(solution)/shard_map/fine/pallas_call | solution.py:873
  55.9 0.3 collective-permute-done.8
  56.3 1.7 %collective-permute-start.11 = (bf16[176,256]{1,0:T(8,128)(2,1)S(1)}, bf16[176,256]{1,0:T(8,128)(2,1)S(1)}, u32[]{:S(2)}, u32[]{:S(2)}) collective-permute-start(bf16[176,256]{1,0:T(8,128)(2,1)S(1)} %add_convert_fusion.2), channel_id=1, source_target_pairs={{0,2},{1,3},{2,0},{3,1},{4,6},{5,7},{6,4},{7,5},{8,10},{9,11},{10,... | collective-permute-start | bytes 270344 | tf_op jit(solution)/shard_map/ppermute | solution.py:674
  58.0 2.9 %collective-permute-done.11 = bf16[176,256]{1,0:T(8,128)(2,1)S(1)} collective-permute-done((bf16[176,256]{1,0:T(8,128)(2,1)S(1)}, bf16[176,256]{1,0:T(8,128)(2,1)S(1)}, u32[]{:S(2)}, u32[]{:S(2)}) %collective-permute-start.11) | collective-permute-done | bytes 90144 | tf_op jit(solution)/shard_map/ppermute | solution.py:674
  60.9 2.8 %collective-permute-start.12 = (bf16[176,256]{1,0:T(8,128)(2,1)S(1)}, bf16[176,256]{1,0:T(8,128)(2,1)S(1)}, u32[]{:S(2)}, u32[]{:S(2)}) collective-permute-start(bf16[176,256]{1,0:T(8,128)(2,1)S(1)} %add_convert_fusion.1), channel_id=1, source_target_pairs={{0,4},{1,5},{2,6},{3,7},{4,0},{5,1},{6,2},{7,3},{8,12},{9,13},{10,... | collective-permute-start | bytes 270344 | tf_op jit(solution)/shard_map/ppermute | solution.py:674
  63.7 2.7 %collective-permute-done.12 = bf16[176,256]{1,0:T(8,128)(2,1)S(1)} collective-permute-done((bf16[176,256]{1,0:T(8,128)(2,1)S(1)}, bf16[176,256]{1,0:T(8,128)(2,1)S(1)}, u32[]{:S(2)}, u32[]{:S(2)}) %collective-permute-start.12) | collective-permute-done | bytes 90144 | tf_op jit(solution)/shard_map/ppermute | solution.py:674
  66.4 0.7 collective-permute-start.13
  67.2 1.1 %collective-permute-start.14 = (bf16[176,256]{1,0:T(8,128)(2,1)S(1)}, bf16[176,256]{1,0:T(8,128)(2,1)S(1)}, u32[]{:S(2)}, u32[]{:S(2)}) collective-permute-start(bf16[176,256]{1,0:T(8,128)(2,1)S(1)} %add_convert_fusion), channel_id=1, source_target_pairs={{0,16},{8,24},{16,0},{24,8},{1,17},{9,25},{17,1},{25,9},{2,18},{10... | collective-permute-start | bytes 270344 | tf_op jit(solution)/shard_map/ppermute | solution.py:674
  68.3 1.7 %collective-permute-start.15 = (bf16[176,256]{1,0:T(8,128)(2,1)S(1)}, bf16[176,256]{1,0:T(8,128)(2,1)S(1)}, u32[]{:S(2)}, u32[]{:S(2)}) collective-permute-start(bf16[176,256]{1,0:T(8,128)(2,1)S(1)} %add_convert_fusion), channel_id=1, source_target_pairs={{0,24},{8,16},{16,8},{24,0},{1,25},{9,17},{17,9},{25,1},{2,26},{10... | collective-permute-start | bytes 270344 | tf_op jit(solution)/shard_map/ppermute | solution.py:674
  70.0 1.0 %collective-permute-done.13 = bf16[176,256]{1,0:T(8,128)(2,1)S(1)} collective-permute-done((bf16[176,256]{1,0:T(8,128)(2,1)S(1)}, bf16[176,256]{1,0:T(8,128)(2,1)S(1)}, u32[]{:S(2)}, u32[]{:S(2)}) %collective-permute-start.13) | collective-permute-done | bytes 90144 | tf_op jit(solution)/shard_map/ppermute | solution.py:674
  71.0 0.7 collective-permute-done.14
  71.7 2.0 %collective-permute-done.15 = bf16[176,256]{1,0:T(8,128)(2,1)S(1)} collective-permute-done((bf16[176,256]{1,0:T(8,128)(2,1)S(1)}, bf16[176,256]{1,0:T(8,128)(2,1)S(1)}, u32[]{:S(2)}, u32[]{:S(2)}) %collective-permute-start.15) | collective-permute-done | bytes 90144 | tf_op jit(solution)/shard_map/ppermute | solution.py:674
  73.8 0.1 collective-permute-start.16
  73.8 0.9 %copy.33 = f32[12,64,128]{2,1,0:T(8,128)} copy(f32[12,64,128]{2,0,1:T(8,128)S(1)} %bitcast.46) | data formatting | bytes 786432
  74.7 0.8 %collective-permute-done.16.refs_2_ = bf16[704,256]{1,0:T(8,128)(2,1)S(1)} collective-permute-done((bf16[704,256]{1,0:T(8,128)(2,1)S(1)}, bf16[704,256]{1,0:T(8,128)(2,1)S(1)}, u32[]{:S(2)}, u32[]{:S(2)}) %collective-permute-start.16) | collective-permute-done | bytes 360480 | tf_op jit(solution)/shard_map/ppermute | solution.py:674
  75.5 2.0 %finish.1 = (f32[3,3,12,64]{3,2,1,0:T(8,128)}, f32[576,64]{1,0:T(8,128)}, f32[576,256]{1,0:T(8,128)}, f32[576,256]{1,0:T(8,128)}, f32[3,3,12,64]{3,2,1,0:T(8,128...) custom-call(s32[4]{0:T(128)S(1)} %pad_add_fusion.refs_0_, ...), custom_call_target="tpu_custom_call" | custom-call | tf_op jit(solution)/shard_map/finish/pallas_call | solution.py:893
  (35 shorter events, 0.4 us)
Async XLA Ops:
  1.4 2.8 %collective-permute-start = (bf16[2,16,268]{2,0,1:T(2,128)(2,1)S(1)}, bf16[2,16,268]{2,0,1:T(2,128)(2,1)S(1)}, u32[]{:S(2)}, u32[]{:S(2)}) collective-permute-start(bf16[2,16,268]{2,0,1:T(2,128)(2,1)S(1)} %pad.28), channel_id=1, source_target_pairs={{0,1},{1,0},{2,3},{3,2},{4,5},{5,4},{6,7},{7,6},{8,9},{9,8},{10,11... | collective-permute-start | bytes 51464 | tf_op jit(solution)/shard_map/ppermute | solution.py:674
  3.1 18.9 %copy-start.1 = (f32[256]{0:T(256)S(1)}, f32[256]{0:T(256)}, u32[]{:S(2)}) copy-start(f32[256]{0:T(256)} %param.20) | copy-start | bytes 3076
  3.1 18.9 %copy-start.2 = (f32[256]{0:T(256)S(1)}, f32[256]{0:T(256)}, u32[]{:S(2)}) copy-start(f32[256]{0:T(256)} %param.21) | copy-start | bytes 3076
  3.1 18.9 %copy-start.3 = (f32[64]{0:T(128)S(1)}, f32[64]{0:T(128)}, u32[]{:S(2)}) copy-start(f32[64]{0:T(128)} %param.18) | copy-start | bytes 772
  3.1 18.9 %copy-start.4 = (f32[64]{0:T(128)S(1)}, f32[64]{0:T(128)}, u32[]{:S(2)}) copy-start(f32[64]{0:T(128)} %param.19) | copy-start | bytes 772
  4.6 5.7 %collective-permute-start.1 = (bf16[2,4,16,76]{3,1,2,0:T(4,128)(2,1)S(1)}, bf16[2,4,16,76]{3,1,2,0:T(4,128)(2,1)S(1)}, u32[]{:S(2)}, u32[]{:S(2)}) collective-permute-start(bf16[2,4,16,76]{3,1,2,0:T(4,128)(2,1)S(1)} %get-tuple-element.122), channel_id=1, source_target_pairs={{0,4},{1,5},{2,6},{3,7},{4,0},{5,1},{6,2},{7,3},{8,12},{9,13},{10,... | collective-permute-start | bytes 58376 | tf_op jit(solution)/shard_map/ppermute | solution.py:674
  10.4 4.2 %collective-permute-start.2 = (bf16[12,12,64]{2,0,1:T(8,128)(2,1)S(1)}, bf16[12,12,64]{2,0,1:T(8,128)(2,1)S(1)}, u32[]{:S(2)}, u32[]{:S(2)}) collective-permute-start(bf16[12,12,64]{2,0,1:T(8,128)(2,1)S(1)} %get-tuple-element.116), channel_id=1, source_target_pairs={{0,1},{1,0},{2,3},{3,2},{4,5},{5,4},{6,7},{7,6},{8,9},{9,8},{10,11... | collective-permute-start | bytes 55304 | tf_op jit(solution)/shard_map/ppermute | solution.py:668
  10.5 4.1 %collective-permute-start.3 = (bf16[12,12,64]{2,0,1:T(8,128)(2,1)S(1)}, bf16[12,12,64]{2,0,1:T(8,128)(2,1)S(1)}, u32[]{:S(2)}, u32[]{:S(2)}) collective-permute-start(bf16[12,12,64]{2,0,1:T(8,128)(2,1)S(1)} %get-tuple-element.117), channel_id=1, source_target_pairs={{1,2},{2,1},{3,4},{4,3},{5,6},{6,5},{9,10},{10,9},{11,12},{12,11},... | collective-permute-start | bytes 55304 | tf_op jit(solution)/shard_map/ppermute | solution.py:669
  11.1 5.7 %collective-permute-start.4 = (bf16[1,8,16,76]{3,1,2,0:T(8,128)(2,1)S(1)}, bf16[1,8,16,76]{3,1,2,0:T(8,128)(2,1)S(1)}, u32[]{:S(2)}, u32[]{:S(2)}) collective-permute-start(bf16[1,8,16,76]{3,1,2,0:T(8,128)(2,1)S(1)} %get-tuple-element.120), channel_id=1, source_target_pairs={{0,2},{1,3},{2,0},{3,1},{4,6},{5,7},{6,4},{7,5},{8,10},{9,11},{10,... | collective-permute-start | bytes 58376 | tf_op jit(solution)/shard_map/ppermute | solution.py:674
  17.0 5.0 %collective-permute-start.5 = (bf16[24,16,128]{2,1,0:T(8,128)(2,1)S(1)}, bf16[24,16,128]{2,1,0:T(8,128)(2,1)S(1)}, u32[]{:S(2)}, u32[]{:S(2)}) collective-permute-start(bf16[24,16,128]{2,1,0:T(8,128)(2,1)S(1)} %get-tuple-element.109), channel_id=1, source_target_pairs={{0,8},{8,0},{16,24},{24,16},{1,9},{9,1},{17,25},{25,17},{2,10},{10... | collective-permute-start | bytes 294920 | tf_op jit(solution)/shard_map/ppermute | solution.py:668
  18.9 3.1 %collective-permute-start.6 = (bf16[24,16,128]{2,1,0:T(8,128)(2,1)S(1)}, bf16[24,16,128]{2,1,0:T(8,128)(2,1)S(1)}, u32[]{:S(2)}, u32[]{:S(2)}) collective-permute-start(bf16[24,16,128]{2,1,0:T(8,128)(2,1)S(1)} %get-tuple-element.108), channel_id=1, source_target_pairs={{8,16},{16,8},{9,17},{17,9},{10,18},{18,10},{11,19},{19,11},{12,20... | collective-permute-start | bytes 294920 | tf_op jit(solution)/shard_map/ppermute | solution.py:669
  30.6 21.1 %copy-start = (bf16[3,3,64,12]{2,3,1,0:T(8,128)(2,1)S(1)}, bf16[3,3,64,12]{2,3,1,0:T(8,128)(2,1)}, u32[]{:S(2)}) copy-start(bf16[3,3,64,12]{2,3,1,0:T(8,128)(2,1)} %param.17) | copy-start | bytes 41476
  30.6 21.1 %copy-start.5 = (f32[12]{0:T(128)S(1)}, f32[12]{0:T(128)}, u32[]{:S(2)}) copy-start(f32[12]{0:T(128)} %param.22) | copy-start | bytes 148
  42.4 1.7 %collective-permute-start.7 = (bf16[704,256]{1,0:T(8,128)(2,1)S(1)}, bf16[704,256]{1,0:T(8,128)(2,1)S(1)}, u32[]{:S(2)}, u32[]{:S(2)}) collective-permute-start(bf16[704,256]{1,0:T(8,128)(2,1)S(1)} %get-tuple-element.61), channel_id=1, source_target_pairs={{0,1},{1,0},{2,3},{3,2},{4,5},{5,4},{6,7},{7,6},{8,9},{9,8},{10,11... | collective-permute-start | bytes 1081352 | tf_op jit(solution)/shard_map/ppermute | solution.py:674
  44.3 11.6 %collective-permute-start.10 = (bf16[176,256]{1,0:T(8,128)(2,1)S(1)}, bf16[176,256]{1,0:T(8,128)(2,1)S(1)}, u32[]{:S(2)}, u32[]{:S(2)}) collective-permute-start(bf16[176,256]{1,0:T(8,128)(2,1)S(1)} %get-tuple-element.101), channel_id=1, source_target_pairs={{0,24},{8,16},{16,8},{24,0},{1,25},{9,17},{17,9},{25,1},{2,26},{10... | collective-permute-start | bytes 270344 | tf_op jit(solution)/shard_map/ppermute | solution.py:674
  47.3 9.0 %collective-permute-start.8 = (bf16[176,256]{1,0:T(8,128)(2,1)S(1)}, bf16[176,256]{1,0:T(8,128)(2,1)S(1)}, u32[]{:S(2)}, u32[]{:S(2)}) collective-permute-start(bf16[176,256]{1,0:T(8,128)(2,1)S(1)} %get-tuple-element.103), channel_id=1, source_target_pairs={{0,8},{8,0},{16,24},{24,16},{1,9},{9,1},{17,25},{25,17},{2,10},{10... | collective-permute-start | bytes 270344 | tf_op jit(solution)/shard_map/ppermute | solution.py:674
  51.7 4.6 %collective-permute-start.9 = (bf16[176,256]{1,0:T(8,128)(2,1)S(1)}, bf16[176,256]{1,0:T(8,128)(2,1)S(1)}, u32[]{:S(2)}, u32[]{:S(2)}) collective-permute-start(bf16[176,256]{1,0:T(8,128)(2,1)S(1)} %get-tuple-element.102), channel_id=1, source_target_pairs={{0,16},{8,24},{16,0},{24,8},{1,17},{9,25},{17,1},{25,9},{2,18},{10... | collective-permute-start | bytes 270344 | tf_op jit(solution)/shard_map/ppermute | solution.py:674
  56.3 4.6 %collective-permute-start.11 = (bf16[176,256]{1,0:T(8,128)(2,1)S(1)}, bf16[176,256]{1,0:T(8,128)(2,1)S(1)}, u32[]{:S(2)}, u32[]{:S(2)}) collective-permute-start(bf16[176,256]{1,0:T(8,128)(2,1)S(1)} %add_convert_fusion.2), channel_id=1, source_target_pairs={{0,2},{1,3},{2,0},{3,1},{4,6},{5,7},{6,4},{7,5},{8,10},{9,11},{10,... | collective-permute-start | bytes 270344 | tf_op jit(solution)/shard_map/ppermute | solution.py:674
  60.9 5.5 %collective-permute-start.12 = (bf16[176,256]{1,0:T(8,128)(2,1)S(1)}, bf16[176,256]{1,0:T(8,128)(2,1)S(1)}, u32[]{:S(2)}, u32[]{:S(2)}) collective-permute-start(bf16[176,256]{1,0:T(8,128)(2,1)S(1)} %add_convert_fusion.1), channel_id=1, source_target_pairs={{0,4},{1,5},{2,6},{3,7},{4,0},{5,1},{6,2},{7,3},{8,12},{9,13},{10,... | collective-permute-start | bytes 270344 | tf_op jit(solution)/shard_map/ppermute | solution.py:674
  66.4 4.6 %collective-permute-start.13 = (bf16[176,256]{1,0:T(8,128)(2,1)S(1)}, bf16[176,256]{1,0:T(8,128)(2,1)S(1)}, u32[]{:S(2)}, u32[]{:S(2)}) collective-permute-start(bf16[176,256]{1,0:T(8,128)(2,1)S(1)} %add_convert_fusion), channel_id=1, source_target_pairs={{0,8},{8,0},{16,24},{24,16},{1,9},{9,1},{17,25},{25,17},{2,10},{10... | collective-permute-start | bytes 270344 | tf_op jit(solution)/shard_map/ppermute | solution.py:674
  67.2 4.5 %collective-permute-start.14 = (bf16[176,256]{1,0:T(8,128)(2,1)S(1)}, bf16[176,256]{1,0:T(8,128)(2,1)S(1)}, u32[]{:S(2)}, u32[]{:S(2)}) collective-permute-start(bf16[176,256]{1,0:T(8,128)(2,1)S(1)} %add_convert_fusion), channel_id=1, source_target_pairs={{0,16},{8,24},{16,0},{24,8},{1,17},{9,25},{17,1},{25,9},{2,18},{10... | collective-permute-start | bytes 270344 | tf_op jit(solution)/shard_map/ppermute | solution.py:674
  68.3 5.4 %collective-permute-start.15 = (bf16[176,256]{1,0:T(8,128)(2,1)S(1)}, bf16[176,256]{1,0:T(8,128)(2,1)S(1)}, u32[]{:S(2)}, u32[]{:S(2)}) collective-permute-start(bf16[176,256]{1,0:T(8,128)(2,1)S(1)} %add_convert_fusion), channel_id=1, source_target_pairs={{0,24},{8,16},{16,8},{24,0},{1,25},{9,17},{17,9},{25,1},{2,26},{10... | collective-permute-start | bytes 270344 | tf_op jit(solution)/shard_map/ppermute | solution.py:674
  73.8 1.7 %collective-permute-start.16 = (bf16[704,256]{1,0:T(8,128)(2,1)S(1)}, bf16[704,256]{1,0:T(8,128)(2,1)S(1)}, u32[]{:S(2)}, u32[]{:S(2)}) collective-permute-start(bf16[704,256]{1,0:T(8,128)(2,1)S(1)} %pad_maximum_fusion.refs_1_), channel_id=1, source_target_pairs={{0,1},{1,0},{2,3},{3,2},{4,5},{5,4},{6,7},{7,6},{8,9},{9,8},{10,11... | collective-permute-start | bytes 1081352 | tf_op jit(solution)/shard_map/ppermute | solution.py:674

commit v3 on v2

--- a/solution.py
+++ b/solution.py
@@ -11,13 +11,15 @@
 ROWS, COLS, PITCH, CHUNKS = 16, 32, 48, 32
 CELLS = PITCH * CHUNKS
 OWN = PITCH * 8
+NEAR = OWN - PITCH - 16
+NEAR_CELLS = PITCH * (ROWS + 2) + 32
 HALO = 6
 FINE_HALO = 12
 TERMS = 1400
-GROUP0, GROUP5 = 7, 6
-N1, N2, N3, N4 = 3, 5, 3, 4
-M4, M3, M2, M1 = 4, 3, 4, 3
-LIMIT = 12
+GROUP0, GROUP5 = 7, 12
+N1, N2, N3, N4 = 1, 1, 1, 1
+M4, M3, M2, M1 = 1, 1, 1, 1
+LIMIT = 16
 
 
 def dotn(left, right):
@@ -206,7 +208,7 @@
 
 
 def fine_field(kept_hbm, w5_ref, b5_ref, fine_ref, e_ref, k5, k5s, a4, sem):
-    copy = pltpu.make_async_copy(kept_hbm, a4, sem)
+    copy = pltpu.make_async_copy(kept_hbm, a4.at[pl.ds(NEAR, NEAR_CELLS)], sem)
     copy.start()
     low = low_half()
     cell, lane = grid(512, 512)
@@ -460,7 +462,7 @@
     rim_ref,
     sem,
 ):
-    kept = pltpu.make_async_copy(a4, kept_hbm, sem)
+    kept = pltpu.make_async_copy(a4.at[pl.ds(NEAR, NEAR_CELLS)], kept_hbm, sem)
     kept.start()
     low = low_half()
     clear_margins(((c5, 5, 29), (b4, 5, 29), (b3, 6, 27), (b2, 7, 27)))
@@ -729,7 +731,7 @@
     return got, above, below, cot, jnp.pad(rim, ((0, 0), (0, 0), (0, 128 - 2 * n)))
 
 
-def total_over_all(keep, send, beside):
+def total_over_all(keep, send, beside, chans):
     gx, gy = lax.axis_size("gx"), lax.axis_size("gy")
     at_x = lax.axis_index("gx")
 
@@ -746,12 +748,16 @@
 
     terms = [swap(part(at_x ^ d).astype(BF), "gx", d) for d in range(1, gx)]
     terms, beside = lax.optimization_barrier((terms, beside))
+    beside = beside.transpose(1, 0, 2)[:chans]
     block = tree([part(at_x)] + [term.astype(F32) for term in terms])
     flip = 2
     while flip < gy:
         block = block.astype(BF)
-        block = block.astype(F32) + swap(block, "gy", flip).astype(F32)
+        other = swap(block, "gy", flip)
         flip *= 2
+        if flip == gy:
+            other, beside = lax.optimization_barrier((other, beside))
+        block = block.astype(F32) + other.astype(F32)
     block = block.astype(BF)
     mine = jnp.concatenate([block] + [swap(block, "gx", d) for d in range(1, gx)])
     return mine, swap(mine, "gy", 1), beside
@@ -852,7 +858,7 @@
         out_shape=(
             pltpu.VMEM((half, 256), F32),
             pltpu.VMEM((half, 256), BF),
-            pltpu.HBM((CELLS, 1024), BF),
+            pltpu.HBM((NEAR_CELLS, 1024), BF),
         ),
         in_specs=[smem] + [vmem] * 16,
         out_specs=(vmem, vmem, hbm),
@@ -885,7 +891,7 @@
         compiler_params=params,
         name="fine",
     )(pltpu.with_memory_space_constraint(kept, pltpu.HBM), weights[4], bias_five.reshape(1, -1))
-    mine, other, fine = total_over_all(keep, send, fine)
+    mine, other, fine = total_over_all(keep, send, fine, chans)
 
     def out(*shape):
         return jax.ShapeDtypeStruct(shape, F32)
@@ -911,7 +917,7 @@
         name="finish",
     )(pos, mine, other, fields[2], fields[3])
     return (
-        fine.transpose(1, 0, 2)[:chans],
+        fine,
         g1,
         g2.reshape(3, 3, 64, 64),
         g3.reshape(3, 3, 64, 256),

time: 78 us -> 73.1 us (0.937)
  Pallas kernels: 26.5 us -> 21.4 us
    pallas_call x1, Pallas kernels: 11.8 us -> 8.73 us  [local(): pl.pallas_call(lambda *refs: backward(scale, *refs), out_shape=(pltpu.VME...]
    pallas_call x1, Pallas kernels: 8.53 us -> 6.89 us  [local(): pl.pallas_call(lambda *refs: forward(extent, *refs), out_shape=shared, in...]
  transfers between devices with their start and end apart: 17 -> 17, of which waited for: 11 -> 11; matrix products, arithmetic and copies ran while one was open for 5% -> 6% of each run, Pallas kernels for 5% -> 5%
where the time goes in v3:
time: 73.1 us; the launch traced here: 72.6 us
  starting transfers between devices  26.4 us (36%)
  Pallas kernels  21.4 us (29%)
  waiting for transfers between devices  18 us (25%)
  local copies, waits for them, and re-layouts  4.88 us (7%)
  between operations  1.07 us (1%)
  other arithmetic  0.75 us (1%)
    ppermute x13, starting transfers between devices, swap(): lax.ppermute(block, axis, [(i, i ^ flip) for i in range(lax.axis_size(axi...  23.1 us
    ppermute x13, waiting for transfers between devices, swap(): lax.ppermute(block, axis, [(i, i ^ flip) for i in range(lax.axis_size(axi...  15.8 us
    pallas_call x1, Pallas kernels, local(): pl.pallas_call(lambda *refs: backward(scale, *refs), out_shape=(pltpu.VME...  8.73 us
    pallas_call x1, Pallas kernels, local(): pl.pallas_call(lambda *refs: forward(extent, *refs), out_shape=shared, in...  6.89 us
    pallas_call x1, Pallas kernels, local(): pl.pallas_call(fine_field, out_shape=jax.ShapeDtypeStruct((4 * ROWS, 16,...  3.8 us
    unnamed x16, local copies, waits for them, and re-layouts  2.29 us
    ppermute x2, waiting for transfers between devices, exchange(): one = lax.ppermute(jnp.where(odd, first, last), axis, even_swap)  2.18 us
    pallas_call x1, Pallas kernels, local(): pl.pallas_call(lambda *refs: finish(chans, gx, *refs), out_shape=(out(3,...  1.99 us
  transfers between devices with their start and end apart: 17, of which 11 were waited for; matrix products, arithmetic and copies ran while one was open for 6% of the time, Pallas kernels for 5%

profile of v3, /device:TPU:0, one launch (start us, length us, event | category | flops | bytes accessed | tf_op | source)
XLA Modules:
  0.0 72.6 jit_solution(15412798058678129004)
XLA Ops:
  0.6 0.8 %pad.28 = bf16[2,16,268]{2,0,1:T(2,128)(2,1)S(1)} pad(bf16[2,12,256]{2,0,1:T(2,128)(2,1)} %bitcast.64, bf16[]{:T(256)} %constant.40.clone.1), padding=0_0x0_4x6_6 | pad | bytes 29442 | tf_op jit(solution)/shard_map/jit(_pad)/pad | solution.py:683
  1.4 0.5 collective-permute-start
  2.0 1.1 %fusion.9 = (bf16[12,64,12]{2,1,0:T(8,128)(2,1)S(1)}, bf16[12,64,12]{2,1,0:T(8,128)(2,1)S(1)}) fusion(bf16[12,64,128]{2,1,0:T(8,128)(2,1)} %param.23), kind=kLoop, calls=%fused_computation.47 | loop fusion | bytes 73728 | tf_op jit(solution)/shard_map/slice | solution.py:714
  3.1 1.1 %copy.37 = bf16[12,64,128]{2,0,1:T(8,128)(2,1)S(1)} copy(bf16[12,64,128]{2,1,0:T(8,128)(2,1)} %param.23) | data formatting | bytes 393216 | tf_op args[11]
  4.2 0.1 maximum_select_fusion.2
  4.3 0.1 slice_bitcast_fusion.3
  4.4 0.1 broadcast_select_fusion.9
  4.5 3.7 %collective-permute-start.1 = (bf16[2,4,16,76]{3,1,2,0:T(4,128)(2,1)S(1)}, bf16[2,4,16,76]{3,1,2,0:T(4,128)(2,1)S(1)}, u32[]{:S(2)}, u32[]{:S(2)}) collective-permute-start(bf16[2,4,16,76]{3,1,2,0:T(4,128)(2,1)S(1)} %get-tuple-element.126), channel_id=1, source_target_pairs={{0,4},{1,5},{2,6},{3,7},{4,0},{5,1},{6,2},{7,3},{8,12},{9,13},{10,... | collective-permute-start | bytes 58376 | tf_op jit(solution)/shard_map/ppermute | solution.py:676
  8.2 0.1 pad.27.refs_3_
  8.3 0.2 copy.34
  8.4 0.2 copy.35
  8.6 1.6 %collective-permute-done.1 = bf16[2,4,16,76]{3,1,2,0:T(4,128)(2,1)S(1)} collective-permute-done((bf16[2,4,16,76]{3,1,2,0:T(4,128)(2,1)S(1)}, bf16[2,4,16,76]{3,1,2,0:T(4,128)(2,1)S(1)}, u32[]{:S(2)}, u32[]{:S(2)}) %collective-permute-start.1) | collective-permute-done | bytes 19488 | tf_op jit(solution)/shard_map/ppermute | solution.py:676
  10.2 0.1 maximum_select_fusion
  10.4 0.1 collective-permute-start.2
  10.4 0.7 collective-permute-start.3
  11.1 3.4 %collective-permute-start.4 = (bf16[1,8,16,76]{3,1,2,0:T(8,128)(2,1)S(1)}, bf16[1,8,16,76]{3,1,2,0:T(8,128)(2,1)S(1)}, u32[]{:S(2)}, u32[]{:S(2)}) collective-permute-start(bf16[1,8,16,76]{3,1,2,0:T(8,128)(2,1)S(1)} %get-tuple-element.124), channel_id=1, source_target_pairs={{0,2},{1,3},{2,0},{3,1},{4,6},{5,7},{6,4},{7,5},{8,10},{9,11},{10,... | collective-permute-start | bytes 58376 | tf_op jit(solution)/shard_map/ppermute | solution.py:676
  14.6 0.3 copy.31
  14.9 1.9 %collective-permute-done.4 = bf16[1,8,16,76]{3,1,2,0:T(8,128)(2,1)S(1)} collective-permute-done((bf16[1,8,16,76]{3,1,2,0:T(8,128)(2,1)S(1)}, bf16[1,8,16,76]{3,1,2,0:T(8,128)(2,1)S(1)}, u32[]{:S(2)}, u32[]{:S(2)}) %collective-permute-start.4) | collective-permute-done | bytes 19488 | tf_op jit(solution)/shard_map/ppermute | solution.py:676
  16.9 0.1 broadcast_select_fusion.2
  17.0 1.9 %collective-permute-start.5 = (bf16[24,16,128]{2,1,0:T(8,128)(2,1)S(1)}, bf16[24,16,128]{2,1,0:T(8,128)(2,1)S(1)}, u32[]{:S(2)}, u32[]{:S(2)}) collective-permute-start(bf16[24,16,128]{2,1,0:T(8,128)(2,1)S(1)} %get-tuple-element.113), channel_id=1, source_target_pairs={{0,8},{8,0},{16,24},{24,16},{1,9},{9,1},{17,25},{25,17},{2,10},{10... | collective-permute-start | bytes 294920 | tf_op jit(solution)/shard_map/ppermute | solution.py:670
  18.9 0.7 collective-permute-start.6
  19.6 0.1 pad_add_fusion.refs_0_
  19.7 0.1 pad.29
  19.8 0.1 pad.32.refs_4_
  19.8 2.2 %collective-permute-done.5 = bf16[24,16,128]{2,1,0:T(8,128)(2,1)S(1)} collective-permute-done((bf16[24,16,128]{2,1,0:T(8,128)(2,1)S(1)}, bf16[24,16,128]{2,1,0:T(8,128)(2,1)S(1)}, u32[]{:S(2)}, u32[]{:S(2)}) %collective-permute-start.5) | collective-permute-done | bytes 98336 | tf_op jit(solution)/shard_map/ppermute | solution.py:670
  22.1 6.9 %forward.1 = (f32[1536,128]{1,0:T(8,128)S(1)}, bf16[288,256]{1,0:T(8,128)(2,1)S(1)}, bf16[256,256]{1,0:T(8,128)(2,1)S(1)}, bf16[256,256]{1,0:T(8,128)(2,1)S(1)},...) custom-call(s32[4]{0:T(128)S(1)} %pad_add_fusion.refs_0_, ...), custom_call_target="tpu_custom_call" | custom-call | tf_op jit(solution)/shard_map/forward/pallas_call | solution.py:825
  29.0 8.7 %backward.1 = (f32[704,256]{1,0:T(8,128)S(1)}, bf16[704,256]{1,0:T(8,128)(2,1)S(1)}, bf16[896,1024]{1,0:T(8,128)(2,1)}) custom-call(s32[4]{0:T(128)S(1)} %pad_add_fusion.refs_0_, bf16[24,16,128]{2,1,0:T(8,128)(2,1)S(1)} %get-tuple-element.115.refs_2_.refs_1_, bf16[24,16,128]{2,1,0:T(8,128)(2,1)S(1)} %get-tuple-element.114.refs_3_.refs_2_, ...), custom_call_target="tpu_custom_call" | custom-call | tf_op jit(solution)/shard_map/backward/pallas_call | solution.py:856
  37.7 0.1 collective-permute-start.7
  37.8 1.6 %collective-permute-done.7 = bf16[704,256]{1,0:T(8,128)(2,1)S(1)} collective-permute-done((bf16[704,256]{1,0:T(8,128)(2,1)S(1)}, bf16[704,256]{1,0:T(8,128)(2,1)S(1)}, u32[]{:S(2)}, u32[]{:S(2)}) %collective-permute-start.7) | collective-permute-done | bytes 360480 | tf_op jit(solution)/shard_map/ppermute | solution.py:676
  39.5 0.1 convert_add_fusion
  39.6 3.0 %collective-permute-start.10 = (bf16[176,256]{1,0:T(8,128)(2,1)S(1)}, bf16[176,256]{1,0:T(8,128)(2,1)S(1)}, u32[]{:S(2)}, u32[]{:S(2)}) collective-permute-start(bf16[176,256]{1,0:T(8,128)(2,1)S(1)} %get-tuple-element.105), channel_id=1, source_target_pairs={{0,24},{8,16},{16,8},{24,0},{1,25},{9,17},{17,9},{25,1},{2,26},{10... | collective-permute-start | bytes 270344 | tf_op jit(solution)/shard_map/ppermute | solution.py:676
  42.6 4.4 %collective-permute-start.8 = (bf16[176,256]{1,0:T(8,128)(2,1)S(1)}, bf16[176,256]{1,0:T(8,128)(2,1)S(1)}, u32[]{:S(2)}, u32[]{:S(2)}) collective-permute-start(bf16[176,256]{1,0:T(8,128)(2,1)S(1)} %get-tuple-element.107), channel_id=1, source_target_pairs={{0,8},{8,0},{16,24},{24,16},{1,9},{9,1},{17,25},{25,17},{2,10},{10... | collective-permute-start | bytes 270344 | tf_op jit(solution)/shard_map/ppermute | solution.py:676
  47.0 3.8 %fine.1 = f32[64,16,128]{2,1,0:T(8,128)S(1)} custom-call(bf16[896,1024]{1,0:T(8,128)(2,1)} %get-tuple-element.64.kept_hbm, bf16[3,3,12,64]{3,2,1,0:T(8,128)(2,1)S(1)} %bitcast.48, f32[1,12]{1,0:T(1,128)S(1)} %bitcast.53), custom_call_target="tpu_custom_call" | custom-call | tf_op jit(solution)/shard_map/fine/pallas_call | solution.py:879
  50.8 0.7 %collective-permute-done.8 = bf16[176,256]{1,0:T(8,128)(2,1)S(1)} collective-permute-done((bf16[176,256]{1,0:T(8,128)(2,1)S(1)}, bf16[176,256]{1,0:T(8,128)(2,1)S(1)}, u32[]{:S(2)}, u32[]{:S(2)}) %collective-permute-start.8) | collective-permute-done | bytes 90144 | tf_op jit(solution)/shard_map/ppermute | solution.py:676
  51.6 1.7 %collective-permute-start.11 = (bf16[176,256]{1,0:T(8,128)(2,1)S(1)}, bf16[176,256]{1,0:T(8,128)(2,1)S(1)}, u32[]{:S(2)}, u32[]{:S(2)}) collective-permute-start(bf16[176,256]{1,0:T(8,128)(2,1)S(1)} %add_convert_fusion.2), channel_id=1, source_target_pairs={{0,2},{1,3},{2,0},{3,1},{4,6},{5,7},{6,4},{7,5},{8,10},{9,11},{10,... | collective-permute-start | bytes 270344 | tf_op jit(solution)/shard_map/ppermute | solution.py:676
  53.3 2.9 %collective-permute-done.11 = bf16[176,256]{1,0:T(8,128)(2,1)S(1)} collective-permute-done((bf16[176,256]{1,0:T(8,128)(2,1)S(1)}, bf16[176,256]{1,0:T(8,128)(2,1)S(1)}, u32[]{:S(2)}, u32[]{:S(2)}) %collective-permute-start.11) | collective-permute-done | bytes 90144 | tf_op jit(solution)/shard_map/ppermute | solution.py:676
  56.3 2.8 %collective-permute-start.12 = (bf16[176,256]{1,0:T(8,128)(2,1)S(1)}, bf16[176,256]{1,0:T(8,128)(2,1)S(1)}, u32[]{:S(2)}, u32[]{:S(2)}) collective-permute-start(bf16[176,256]{1,0:T(8,128)(2,1)S(1)} %add_convert_fusion.1), channel_id=1, source_target_pairs={{0,4},{1,5},{2,6},{3,7},{4,0},{5,1},{6,2},{7,3},{8,12},{9,13},{10,... | collective-permute-start | bytes 270344 | tf_op jit(solution)/shard_map/ppermute | solution.py:676
  59.0 2.7 %collective-permute-done.12 = bf16[176,256]{1,0:T(8,128)(2,1)S(1)} collective-permute-done((bf16[176,256]{1,0:T(8,128)(2,1)S(1)}, bf16[176,256]{1,0:T(8,128)(2,1)S(1)}, u32[]{:S(2)}, u32[]{:S(2)}) %collective-permute-start.12) | collective-permute-done | bytes 90144 | tf_op jit(solution)/shard_map/ppermute | solution.py:676
  61.8 0.6 collective-permute-start.13
  62.4 1.0 %collective-permute-start.14 = (bf16[176,256]{1,0:T(8,128)(2,1)S(1)}, bf16[176,256]{1,0:T(8,128)(2,1)S(1)}, u32[]{:S(2)}, u32[]{:S(2)}) collective-permute-start(bf16[176,256]{1,0:T(8,128)(2,1)S(1)} %add_convert_fusion), channel_id=1, source_target_pairs={{0,16},{8,24},{16,0},{24,8},{1,17},{9,25},{17,1},{25,9},{2,18},{10... | collective-permute-start | bytes 270344 | tf_op jit(solution)/shard_map/ppermute | solution.py:676
  63.4 2.0 %collective-permute-start.15 = (bf16[176,256]{1,0:T(8,128)(2,1)S(1)}, bf16[176,256]{1,0:T(8,128)(2,1)S(1)}, u32[]{:S(2)}, u32[]{:S(2)}) collective-permute-start(bf16[176,256]{1,0:T(8,128)(2,1)S(1)} %add_convert_fusion), channel_id=1, source_target_pairs={{0,24},{8,16},{16,8},{24,0},{1,25},{9,17},{17,9},{25,1},{2,26},{10... | collective-permute-start | bytes 270344 | tf_op jit(solution)/shard_map/ppermute | solution.py:676
  65.3 1.0 %collective-permute-done.13 = bf16[176,256]{1,0:T(8,128)(2,1)S(1)} collective-permute-done((bf16[176,256]{1,0:T(8,128)(2,1)S(1)}, bf16[176,256]{1,0:T(8,128)(2,1)S(1)}, u32[]{:S(2)}, u32[]{:S(2)}) %collective-permute-start.13) | collective-permute-done | bytes 90144 | tf_op jit(solution)/shard_map/ppermute | solution.py:676
  66.4 0.5 collective-permute-done.14
  66.9 1.9 %collective-permute-done.15 = bf16[176,256]{1,0:T(8,128)(2,1)S(1)} collective-permute-done((bf16[176,256]{1,0:T(8,128)(2,1)S(1)}, bf16[176,256]{1,0:T(8,128)(2,1)S(1)}, u32[]{:S(2)}, u32[]{:S(2)}) %collective-permute-start.15) | collective-permute-done | bytes 90144 | tf_op jit(solution)/shard_map/ppermute | solution.py:676
  68.8 0.1 collective-permute-start.16
  68.9 0.9 %copy.33 = f32[12,64,128]{2,1,0:T(8,128)} copy(f32[12,64,128]{2,0,1:T(8,128)S(1)} %bitcast.46) | data formatting | bytes 786432
  69.8 0.8 %collective-permute-done.16.refs_2_ = bf16[704,256]{1,0:T(8,128)(2,1)S(1)} collective-permute-done((bf16[704,256]{1,0:T(8,128)(2,1)S(1)}, bf16[704,256]{1,0:T(8,128)(2,1)S(1)}, u32[]{:S(2)}, u32[]{:S(2)}) %collective-permute-start.16) | collective-permute-done | bytes 360480 | tf_op jit(solution)/shard_map/ppermute | solution.py:676
  70.6 2.0 %finish.1 = (f32[3,3,12,64]{3,2,1,0:T(8,128)}, f32[576,64]{1,0:T(8,128)}, f32[576,256]{1,0:T(8,128)}, f32[576,256]{1,0:T(8,128)}, f32[3,3,12,64]{3,2,1,0:T(8,128...) custom-call(s32[4]{0:T(128)S(1)} %pad_add_fusion.refs_0_, ...), custom_call_target="tpu_custom_call" | custom-call | tf_op jit(solution)/shard_map/finish/pallas_call | solution.py:899
  (35 shorter events, 0.4 us)
Async XLA Ops:
  1.4 2.8 %collective-permute-start = (bf16[2,16,268]{2,0,1:T(2,128)(2,1)S(1)}, bf16[2,16,268]{2,0,1:T(2,128)(2,1)S(1)}, u32[]{:S(2)}, u32[]{:S(2)}) collective-permute-start(bf16[2,16,268]{2,0,1:T(2,128)(2,1)S(1)} %pad.28), channel_id=1, source_target_pairs={{0,1},{1,0},{2,3},{3,2},{4,5},{5,4},{6,7},{7,6},{8,9},{9,8},{10,11... | collective-permute-start | bytes 51464 | tf_op jit(solution)/shard_map/ppermute | solution.py:676
  4.5 5.7 %collective-permute-start.1 = (bf16[2,4,16,76]{3,1,2,0:T(4,128)(2,1)S(1)}, bf16[2,4,16,76]{3,1,2,0:T(4,128)(2,1)S(1)}, u32[]{:S(2)}, u32[]{:S(2)}) collective-permute-start(bf16[2,4,16,76]{3,1,2,0:T(4,128)(2,1)S(1)} %get-tuple-element.126), channel_id=1, source_target_pairs={{0,4},{1,5},{2,6},{3,7},{4,0},{5,1},{6,2},{7,3},{8,12},{9,13},{10,... | collective-permute-start | bytes 58376 | tf_op jit(solution)/shard_map/ppermute | solution.py:676
  10.3 11.7 %copy-start.1 = (f32[256]{0:T(256)S(1)}, f32[256]{0:T(256)}, u32[]{:S(2)}) copy-start(f32[256]{0:T(256)} %param.20) | copy-start | bytes 3076
  10.3 11.7 %copy-start.2 = (f32[256]{0:T(256)S(1)}, f32[256]{0:T(256)}, u32[]{:S(2)}) copy-start(f32[256]{0:T(256)} %param.21) | copy-start | bytes 3076
  10.3 11.7 %copy-start.3 = (f32[64]{0:T(128)S(1)}, f32[64]{0:T(128)}, u32[]{:S(2)}) copy-start(f32[64]{0:T(128)} %param.18) | copy-start | bytes 772
  10.4 11.7 %copy-start.4 = (f32[64]{0:T(128)S(1)}, f32[64]{0:T(128)}, u32[]{:S(2)}) copy-start(f32[64]{0:T(128)} %param.19) | copy-start | bytes 772
  10.4 4.2 %collective-permute-start.2 = (bf16[12,12,64]{2,0,1:T(8,128)(2,1)S(1)}, bf16[12,12,64]{2,0,1:T(8,128)(2,1)S(1)}, u32[]{:S(2)}, u32[]{:S(2)}) collective-permute-start(bf16[12,12,64]{2,0,1:T(8,128)(2,1)S(1)} %get-tuple-element.120), channel_id=1, source_target_pairs={{0,1},{1,0},{2,3},{3,2},{4,5},{5,4},{6,7},{7,6},{8,9},{9,8},{10,11... | collective-permute-start | bytes 55304 | tf_op jit(solution)/shard_map/ppermute | solution.py:670
  10.4 4.1 %collective-permute-start.3 = (bf16[12,12,64]{2,0,1:T(8,128)(2,1)S(1)}, bf16[12,12,64]{2,0,1:T(8,128)(2,1)S(1)}, u32[]{:S(2)}, u32[]{:S(2)}) collective-permute-start(bf16[12,12,64]{2,0,1:T(8,128)(2,1)S(1)} %get-tuple-element.121), channel_id=1, source_target_pairs={{1,2},{2,1},{3,4},{4,3},{5,6},{6,5},{9,10},{10,9},{11,12},{12,11},... | collective-permute-start | bytes 55304 | tf_op jit(solution)/shard_map/ppermute | solution.py:671
  11.1 5.7 %collective-permute-start.4 = (bf16[1,8,16,76]{3,1,2,0:T(8,128)(2,1)S(1)}, bf16[1,8,16,76]{3,1,2,0:T(8,128)(2,1)S(1)}, u32[]{:S(2)}, u32[]{:S(2)}) collective-permute-start(bf16[1,8,16,76]{3,1,2,0:T(8,128)(2,1)S(1)} %get-tuple-element.124), channel_id=1, source_target_pairs={{0,2},{1,3},{2,0},{3,1},{4,6},{5,7},{6,4},{7,5},{8,10},{9,11},{10,... | collective-permute-start | bytes 58376 | tf_op jit(solution)/shard_map/ppermute | solution.py:676
  17.0 5.0 %collective-permute-start.5 = (bf16[24,16,128]{2,1,0:T(8,128)(2,1)S(1)}, bf16[24,16,128]{2,1,0:T(8,128)(2,1)S(1)}, u32[]{:S(2)}, u32[]{:S(2)}) collective-permute-start(bf16[24,16,128]{2,1,0:T(8,128)(2,1)S(1)} %get-tuple-element.113), channel_id=1, source_target_pairs={{0,8},{8,0},{16,24},{24,16},{1,9},{9,1},{17,25},{25,17},{2,10},{10... | collective-permute-start | bytes 294920 | tf_op jit(solution)/shard_map/ppermute | solution.py:670
  18.9 3.1 %collective-permute-start.6 = (bf16[24,16,128]{2,1,0:T(8,128)(2,1)S(1)}, bf16[24,16,128]{2,1,0:T(8,128)(2,1)S(1)}, u32[]{:S(2)}, u32[]{:S(2)}) collective-permute-start(bf16[24,16,128]{2,1,0:T(8,128)(2,1)S(1)} %get-tuple-element.112), channel_id=1, source_target_pairs={{8,16},{16,8},{9,17},{17,9},{10,18},{18,10},{11,19},{19,11},{12,20... | collective-permute-start | bytes 294920 | tf_op jit(solution)/shard_map/ppermute | solution.py:671
  37.7 9.3 %copy-start = (bf16[3,3,64,12]{2,3,1,0:T(8,128)(2,1)S(1)}, bf16[3,3,64,12]{2,3,1,0:T(8,128)(2,1)}, u32[]{:S(2)}) copy-start(bf16[3,3,64,12]{2,3,1,0:T(8,128)(2,1)} %param.17) | copy-start | bytes 41476
  37.7 9.3 %copy-start.5 = (f32[12]{0:T(128)S(1)}, f32[12]{0:T(128)}, u32[]{:S(2)}) copy-start(f32[12]{0:T(128)} %param.22) | copy-start | bytes 148
  37.7 1.7 %collective-permute-start.7 = (bf16[704,256]{1,0:T(8,128)(2,1)S(1)}, bf16[704,256]{1,0:T(8,128)(2,1)S(1)}, u32[]{:S(2)}, u32[]{:S(2)}) collective-permute-start(bf16[704,256]{1,0:T(8,128)(2,1)S(1)} %get-tuple-element.63), channel_id=1, source_target_pairs={{0,1},{1,0},{2,3},{3,2},{4,5},{5,4},{6,7},{7,6},{8,9},{9,8},{10,11... | collective-permute-start | bytes 1081352 | tf_op jit(solution)/shard_map/ppermute | solution.py:676
  39.6 11.2 %collective-permute-start.10 = (bf16[176,256]{1,0:T(8,128)(2,1)S(1)}, bf16[176,256]{1,0:T(8,128)(2,1)S(1)}, u32[]{:S(2)}, u32[]{:S(2)}) collective-permute-start(bf16[176,256]{1,0:T(8,128)(2,1)S(1)} %get-tuple-element.105), channel_id=1, source_target_pairs={{0,24},{8,16},{16,8},{24,0},{1,25},{9,17},{17,9},{25,1},{2,26},{10... | collective-permute-start | bytes 270344 | tf_op jit(solution)/shard_map/ppermute | solution.py:676
  42.6 9.0 %collective-permute-start.8 = (bf16[176,256]{1,0:T(8,128)(2,1)S(1)}, bf16[176,256]{1,0:T(8,128)(2,1)S(1)}, u32[]{:S(2)}, u32[]{:S(2)}) collective-permute-start(bf16[176,256]{1,0:T(8,128)(2,1)S(1)} %get-tuple-element.107), channel_id=1, source_target_pairs={{0,8},{8,0},{16,24},{24,16},{1,9},{9,1},{17,25},{25,17},{2,10},{10... | collective-permute-start | bytes 270344 | tf_op jit(solution)/shard_map/ppermute | solution.py:676
  47.0 4.6 %collective-permute-start.9 = (bf16[176,256]{1,0:T(8,128)(2,1)S(1)}, bf16[176,256]{1,0:T(8,128)(2,1)S(1)}, u32[]{:S(2)}, u32[]{:S(2)}) collective-permute-start(bf16[176,256]{1,0:T(8,128)(2,1)S(1)} %get-tuple-element.106), channel_id=1, source_target_pairs={{0,16},{8,24},{16,0},{24,8},{1,17},{9,25},{17,1},{25,9},{2,18},{10... | collective-permute-start | bytes 270344 | tf_op jit(solution)/shard_map/ppermute | solution.py:676
  51.6 4.6 %collective-permute-start.11 = (bf16[176,256]{1,0:T(8,128)(2,1)S(1)}, bf16[176,256]{1,0:T(8,128)(2,1)S(1)}, u32[]{:S(2)}, u32[]{:S(2)}) collective-permute-start(bf16[176,256]{1,0:T(8,128)(2,1)S(1)} %add_convert_fusion.2), channel_id=1, source_target_pairs={{0,2},{1,3},{2,0},{3,1},{4,6},{5,7},{6,4},{7,5},{8,10},{9,11},{10,... | collective-permute-start | bytes 270344 | tf_op jit(solution)/shard_map/ppermute | solution.py:676
  56.3 5.5 %collective-permute-start.12 = (bf16[176,256]{1,0:T(8,128)(2,1)S(1)}, bf16[176,256]{1,0:T(8,128)(2,1)S(1)}, u32[]{:S(2)}, u32[]{:S(2)}) collective-permute-start(bf16[176,256]{1,0:T(8,128)(2,1)S(1)} %add_convert_fusion.1), channel_id=1, source_target_pairs={{0,4},{1,5},{2,6},{3,7},{4,0},{5,1},{6,2},{7,3},{8,12},{9,13},{10,... | collective-permute-start | bytes 270344 | tf_op jit(solution)/shard_map/ppermute | solution.py:676
  61.8 4.6 %collective-permute-start.13 = (bf16[176,256]{1,0:T(8,128)(2,1)S(1)}, bf16[176,256]{1,0:T(8,128)(2,1)S(1)}, u32[]{:S(2)}, u32[]{:S(2)}) collective-permute-start(bf16[176,256]{1,0:T(8,128)(2,1)S(1)} %add_convert_fusion), channel_id=1, source_target_pairs={{0,8},{8,0},{16,24},{24,16},{1,9},{9,1},{17,25},{25,17},{2,10},{10... | collective-permute-start | bytes 270344 | tf_op jit(solution)/shard_map/ppermute | solution.py:676
  62.4 4.5 %collective-permute-start.14 = (bf16[176,256]{1,0:T(8,128)(2,1)S(1)}, bf16[176,256]{1,0:T(8,128)(2,1)S(1)}, u32[]{:S(2)}, u32[]{:S(2)}) collective-permute-start(bf16[176,256]{1,0:T(8,128)(2,1)S(1)} %add_convert_fusion), channel_id=1, source_target_pairs={{0,16},{8,24},{16,0},{24,8},{1,17},{9,25},{17,1},{25,9},{2,18},{10... | collective-permute-start | bytes 270344 | tf_op jit(solution)/shard_map/ppermute | solution.py:676
  63.4 5.4 %collective-permute-start.15 = (bf16[176,256]{1,0:T(8,128)(2,1)S(1)}, bf16[176,256]{1,0:T(8,128)(2,1)S(1)}, u32[]{:S(2)}, u32[]{:S(2)}) collective-permute-start(bf16[176,256]{1,0:T(8,128)(2,1)S(1)} %add_convert_fusion), channel_id=1, source_target_pairs={{0,24},{8,16},{16,8},{24,0},{1,25},{9,17},{17,9},{25,1},{2,26},{10... | collective-permute-start | bytes 270344 | tf_op jit(solution)/shard_map/ppermute | solution.py:676
  68.8 1.7 %collective-permute-start.16 = (bf16[704,256]{1,0:T(8,128)(2,1)S(1)}, bf16[704,256]{1,0:T(8,128)(2,1)S(1)}, u32[]{:S(2)}, u32[]{:S(2)}) collective-permute-start(bf16[704,256]{1,0:T(8,128)(2,1)S(1)} %pad_maximum_fusion.refs_1_), channel_id=1, source_target_pairs={{0,1},{1,0},{2,3},{3,2},{4,5},{5,4},{6,7},{7,6},{8,9},{9,8},{10,11... | collective-permute-start | bytes 1081352 | tf_op jit(solution)/shard_map/ppermute | solution.py:676

commit v4 on v3

--- a/solution.py
+++ b/solution.py
@@ -19,7 +19,8 @@
 GROUP0, GROUP5 = 7, 12
 N1, N2, N3, N4 = 1, 1, 1, 1
 M4, M3, M2, M1 = 1, 1, 1, 1
-LIMIT = 16
+LIMIT = 12
+BIG = 34
 
 
 def dotn(left, right):
@@ -822,12 +823,9 @@
         weight_four.reshape(576, 256),
         weight_five.transpose(0, 1, 3, 2),
     )
-    fields = pl.pallas_call(
-        lambda *refs: forward(extent, *refs),
-        out_shape=shared,
-        in_specs=[smem] + [vmem] * 3 + [hbm] * 5 + [vmem] * 4,
-        out_specs=(vmem,) * 14,
-        scratch_shapes=[
+    half = -(-TERMS // (32 * gx)) * 16 * gx
+    first_scratch = (
+        [
             pltpu.VMEM((32, 512), F32),
             pltpu.VMEM((3 * PITCH, 256), BF),
             pltpu.VMEM((384, 128), BF),
@@ -837,9 +835,44 @@
         ]
         + [pltpu.VMEM(w.shape, BF) for w in weights]
         + [pltpu.VMEM((32, 16, 128), BF)]
-        + [pltpu.SemaphoreType.DMA((5,))],
-        compiler_params=params,
-        name="forward",
+        + [pltpu.SemaphoreType.DMA((5,))]
+    )
+    second_scratch = [
+            buf(768),
+            buf(1024),
+            buf(256),
+            buf(128),
+            buf(128),
+            pltpu.VMEM((2 * half, 256), F32),
+            pltpu.VMEM((98, 16, 128), BF),
+            pltpu.VMEM((98, 16, 128), BF),
+            pltpu.SemaphoreType.DMA,
+        ]
+
+    def gradients(*refs):
+        place, sent, weight_refs, tile = refs[:1], refs[1:4], refs[4:13], refs[13:15]
+        results, turns = refs[15:18], refs[18:20]
+        rest = refs[20:]
+        fields = rest[:2] + turns + rest[2:12]
+        first = rest[12 : 12 + len(first_scratch)]
+        second = rest[12 + len(first_scratch) :]
+        forward(extent, *place, *sent, *weight_refs, *fields, *first)
+        backward(scale, *place, *sent[1:], *tile, *fields[:2], *fields[4:], *results, *second)
+
+    keep, send, kept, turn3, turn4 = pl.pallas_call(
+        gradients,
+        out_shape=(
+            pltpu.VMEM((half, 256), F32),
+            pltpu.VMEM((half, 256), BF),
+            pltpu.HBM((NEAR_CELLS, 1024), BF),
+            shared[2],
+            shared[3],
+        ),
+        in_specs=[smem] + [vmem] * 3 + [hbm] * 5 + [vmem] * 6,
+        out_specs=(vmem, vmem, hbm, vmem, vmem),
+        scratch_shapes=list(shared[:2] + shared[4:]) + first_scratch + second_scratch,
+        compiler_params=pltpu.CompilerParams(vmem_limit_bytes=BIG * 1024 * 1024),
+        name="gradients",
     )(
         pos,
         window,
@@ -850,32 +883,9 @@
         bias_two.reshape(1, -1),
         bias_three.reshape(1, -1),
         bias_four.reshape(1, -1),
-    )
-    fields = [near(f) for f in fields]
-    half = -(-TERMS // (32 * gx)) * 16 * gx
-    keep, send, kept = pl.pallas_call(
-        lambda *refs: backward(scale, *refs),
-        out_shape=(
-            pltpu.VMEM((half, 256), F32),
-            pltpu.VMEM((half, 256), BF),
-            pltpu.HBM((NEAR_CELLS, 1024), BF),
-        ),
-        in_specs=[smem] + [vmem] * 16,
-        out_specs=(vmem, vmem, hbm),
-        scratch_shapes=[
-            buf(768),
-            buf(1024),
-            buf(256),
-            buf(128),
-            buf(128),
-            pltpu.VMEM((2 * half, 256), F32),
-            pltpu.VMEM((98, 16, 128), BF),
-            pltpu.VMEM((98, 16, 128), BF),
-            pltpu.SemaphoreType.DMA,
-        ],
-        compiler_params=params,
-        name="backward",
-    )(pos, above, below, cot, rim, *fields[:2], *fields[4:])
+        cot,
+        rim,
+    )
     fine = pl.pallas_call(
         fine_field,
         out_shape=jax.ShapeDtypeStruct((4 * ROWS, 16, 4 * COLS), F32),
@@ -915,7 +925,7 @@
         scratch_shapes=[pltpu.VMEM((2 * half, 256), BF)],
         compiler_params=params,
         name="finish",
-    )(pos, mine, other, fields[2], fields[3])
+    )(pos, mine, other, near(turn3), near(turn4))
     return (
         fine,
         g1,

time: 73.1 us -> 71.2 us (0.974)
  Pallas kernels: 21.4 us -> 19.6 us
    pallas_call x2 -> x1, Pallas kernels: 15.6 us -> 13.8 us  [local(): pl.pallas_call(gradients, out_shape=(pltpu.VMEM((half, 256), F32), pltpu....]
where the time goes in v4:
time: 71.2 us; the launch traced here: 70.7 us
  starting transfers between devices  26.4 us (37%)
  Pallas kernels  19.6 us (28%)
  waiting for transfers between devices  18.1 us (25%)
  local copies, waits for them, and re-layouts  4.88 us (7%)
  between operations  1.06 us (1%)
  other arithmetic  0.75 us (1%)
    ppermute x13, starting transfers between devices, swap(): lax.ppermute(block, axis, [(i, i ^ flip) for i in range(lax.axis_size(axi...  23.1 us
    ppermute x13, waiting for transfers between devices, swap(): lax.ppermute(block, axis, [(i, i ^ flip) for i in range(lax.axis_size(axi...  15.9 us
    pallas_call x1, Pallas kernels, local(): pl.pallas_call(gradients, out_shape=(pltpu.VMEM((half, 256), F32), pltpu....  13.8 us
    pallas_call x1, Pallas kernels, local(): pl.pallas_call(fine_field, out_shape=jax.ShapeDtypeStruct((4 * ROWS, 16,...  3.81 us
    unnamed x16, local copies, waits for them, and re-layouts  2.29 us
    ppermute x2, waiting for transfers between devices, exchange(): one = lax.ppermute(jnp.where(odd, first, last), axis, even_swap)  2.18 us
    pallas_call x1, Pallas kernels, local(): pl.pallas_call(lambda *refs: finish(chans, gx, *refs), out_shape=(out(3,...  2 us
    ppermute x2, starting transfers between devices, exchange(): one = lax.ppermute(jnp.where(odd, first, last), axis, even_swap)  1.98 us
  transfers between devices with their start and end apart: 17, of which 11 were waited for; matrix products, arithmetic and copies ran while one was open for 6% of the time, Pallas kernels for 5%

profile of v4, /device:TPU:0, one launch (start us, length us, event | category | flops | bytes accessed | tf_op | source)
XLA Modules:
  0.0 70.7 jit_solution(5649378703265699647)
XLA Ops:
  0.6 0.8 %pad.27 = bf16[2,16,268]{2,0,1:T(2,128)(2,1)S(1)} pad(bf16[2,12,256]{2,0,1:T(2,128)(2,1)} %bitcast.64, bf16[]{:T(256)} %constant.41.clone.1), padding=0_0x0_4x6_6 | pad | bytes 29442 | tf_op jit(solution)/shard_map/jit(_pad)/pad | solution.py:684
  1.4 0.5 collective-permute-start
  2.0 1.1 %fusion.9 = (bf16[12,64,12]{2,1,0:T(8,128)(2,1)S(1)}, bf16[12,64,12]{2,1,0:T(8,128)(2,1)S(1)}) fusion(bf16[12,64,128]{2,1,0:T(8,128)(2,1)} %param.23), kind=kLoop, calls=%fused_computation.47 | loop fusion | bytes 73728 | tf_op jit(solution)/shard_map/slice | solution.py:715
  3.1 1.1 %copy.37 = bf16[12,64,128]{2,0,1:T(8,128)(2,1)S(1)} copy(bf16[12,64,128]{2,1,0:T(8,128)(2,1)} %param.23) | data formatting | bytes 393216 | tf_op args[11]
  4.2 0.1 maximum_select_fusion.2
  4.3 0.1 slice_bitcast_fusion.3
  4.4 0.1 broadcast_select_fusion.7
  4.5 3.7 %collective-permute-start.1 = (bf16[2,4,16,76]{3,1,2,0:T(4,128)(2,1)S(1)}, bf16[2,4,16,76]{3,1,2,0:T(4,128)(2,1)S(1)}, u32[]{:S(2)}, u32[]{:S(2)}) collective-permute-start(bf16[2,4,16,76]{3,1,2,0:T(4,128)(2,1)S(1)} %get-tuple-element.102), channel_id=1, source_target_pairs={{0,4},{1,5},{2,6},{3,7},{4,0},{5,1},{6,2},{7,3},{8,12},{9,13},{10,... | collective-permute-start | bytes 58376 | tf_op jit(solution)/shard_map/ppermute | solution.py:677
  8.2 0.1 pad.29.refs_13_
  8.3 0.2 copy.35
  8.4 0.2 copy.34
  8.6 1.6 %collective-permute-done.1 = bf16[2,4,16,76]{3,1,2,0:T(4,128)(2,1)S(1)} collective-permute-done((bf16[2,4,16,76]{3,1,2,0:T(4,128)(2,1)S(1)}, bf16[2,4,16,76]{3,1,2,0:T(4,128)(2,1)S(1)}, u32[]{:S(2)}, u32[]{:S(2)}) %collective-permute-start.1) | collective-permute-done | bytes 19488 | tf_op jit(solution)/shard_map/ppermute | solution.py:677
  10.2 0.1 maximum_select_fusion
  10.3 0.0 copy-start.3
  10.4 0.1 collective-permute-start.3
  10.4 0.7 collective-permute-start.4
  11.1 3.4 %collective-permute-start.2 = (bf16[1,8,16,76]{3,1,2,0:T(8,128)(2,1)S(1)}, bf16[1,8,16,76]{3,1,2,0:T(8,128)(2,1)S(1)}, u32[]{:S(2)}, u32[]{:S(2)}) collective-permute-start(bf16[1,8,16,76]{3,1,2,0:T(8,128)(2,1)S(1)} %get-tuple-element.100), channel_id=1, source_target_pairs={{0,2},{1,3},{2,0},{3,1},{4,6},{5,7},{6,4},{7,5},{8,10},{9,11},{10,... | collective-permute-start | bytes 58376 | tf_op jit(solution)/shard_map/ppermute | solution.py:677
  14.6 0.3 copy.32
  14.9 1.9 %collective-permute-done.2 = bf16[1,8,16,76]{3,1,2,0:T(8,128)(2,1)S(1)} collective-permute-done((bf16[1,8,16,76]{3,1,2,0:T(8,128)(2,1)S(1)}, bf16[1,8,16,76]{3,1,2,0:T(8,128)(2,1)S(1)}, u32[]{:S(2)}, u32[]{:S(2)}) %collective-permute-start.2) | collective-permute-done | bytes 19488 | tf_op jit(solution)/shard_map/ppermute | solution.py:677
  16.9 0.1 broadcast_select_fusion.2
  17.0 1.9 %collective-permute-start.5 = (bf16[24,16,128]{2,1,0:T(8,128)(2,1)S(1)}, bf16[24,16,128]{2,1,0:T(8,128)(2,1)S(1)}, u32[]{:S(2)}, u32[]{:S(2)}) collective-permute-start(bf16[24,16,128]{2,1,0:T(8,128)(2,1)S(1)} %get-tuple-element.89), channel_id=1, source_target_pairs={{0,8},{8,0},{16,24},{24,16},{1,9},{9,1},{17,25},{25,17},{2,10},{10... | collective-permute-start | bytes 294920 | tf_op jit(solution)/shard_map/ppermute | solution.py:671
  18.9 0.7 collective-permute-start.6
  19.6 0.1 pad_add_fusion.refs_0_
  19.7 0.1 pad.30
  19.8 0.1 pad.33.refs_14_
  19.8 2.2 %collective-permute-done.5 = bf16[24,16,128]{2,1,0:T(8,128)(2,1)S(1)} collective-permute-done((bf16[24,16,128]{2,1,0:T(8,128)(2,1)S(1)}, bf16[24,16,128]{2,1,0:T(8,128)(2,1)S(1)}, u32[]{:S(2)}, u32[]{:S(2)}) %collective-permute-start.5) | collective-permute-done | bytes 98336 | tf_op jit(solution)/shard_map/ppermute | solution.py:671
  22.1 13.8 %gradients.1 = (f32[704,256]{1,0:T(8,128)S(1)}, bf16[704,256]{1,0:T(8,128)(2,1)S(1)}, bf16[896,1024]{1,0:T(8,128)(2,1)}, bf16[256,256]{1,0:T(8,128)(2,1)S(1)}, bf16[256,256]{1,0:T(8,128)(2,1)S(1)}) custom-call(s32[4]{0:T(128)S(1)} %pad_add_fusion.refs_0_, bf16[16,16,128]{2,1,0:T(8,128)(2,1)S(1)} %pad.28.refs_1_, ...), custom_call_target="tpu_custom_call" | custom-call | tf_op jit(solution)/shard_map/gradients/pallas_call | solution.py:862
  35.9 0.1 collective-permute-start.7
  36.0 1.6 %collective-permute-done.7 = bf16[704,256]{1,0:T(8,128)(2,1)S(1)} collective-permute-done((bf16[704,256]{1,0:T(8,128)(2,1)S(1)}, bf16[704,256]{1,0:T(8,128)(2,1)S(1)}, u32[]{:S(2)}, u32[]{:S(2)}) %collective-permute-start.7) | collective-permute-done | bytes 360480 | tf_op jit(solution)/shard_map/ppermute | solution.py:677
  37.6 0.1 convert_add_fusion
  37.8 3.0 %collective-permute-start.10 = (bf16[176,256]{1,0:T(8,128)(2,1)S(1)}, bf16[176,256]{1,0:T(8,128)(2,1)S(1)}, u32[]{:S(2)}, u32[]{:S(2)}) collective-permute-start(bf16[176,256]{1,0:T(8,128)(2,1)S(1)} %get-tuple-element.81), channel_id=1, source_target_pairs={{0,24},{8,16},{16,8},{24,0},{1,25},{9,17},{17,9},{25,1},{2,26},{10... | collective-permute-start | bytes 270344 | tf_op jit(solution)/shard_map/ppermute | solution.py:677
  40.7 4.4 %collective-permute-start.8 = (bf16[176,256]{1,0:T(8,128)(2,1)S(1)}, bf16[176,256]{1,0:T(8,128)(2,1)S(1)}, u32[]{:S(2)}, u32[]{:S(2)}) collective-permute-start(bf16[176,256]{1,0:T(8,128)(2,1)S(1)} %get-tuple-element.83), channel_id=1, source_target_pairs={{0,8},{8,0},{16,24},{24,16},{1,9},{9,1},{17,25},{25,17},{2,10},{10... | collective-permute-start | bytes 270344 | tf_op jit(solution)/shard_map/ppermute | solution.py:677
  45.2 3.8 %fine.1 = f32[64,16,128]{2,1,0:T(8,128)S(1)} custom-call(bf16[896,1024]{1,0:T(8,128)(2,1)} %get-tuple-element.40.kept_hbm, bf16[3,3,12,64]{3,2,1,0:T(8,128)(2,1)S(1)} %bitcast.48, f32[1,12]{1,0:T(1,128)S(1)} %bitcast.53), custom_call_target="tpu_custom_call" | custom-call | tf_op jit(solution)/shard_map/fine/pallas_call | solution.py:889
  49.0 0.7 %collective-permute-done.8 = bf16[176,256]{1,0:T(8,128)(2,1)S(1)} collective-permute-done((bf16[176,256]{1,0:T(8,128)(2,1)S(1)}, bf16[176,256]{1,0:T(8,128)(2,1)S(1)}, u32[]{:S(2)}, u32[]{:S(2)}) %collective-permute-start.8) | collective-permute-done | bytes 90144 | tf_op jit(solution)/shard_map/ppermute | solution.py:677
  49.8 1.7 %collective-permute-start.11 = (bf16[176,256]{1,0:T(8,128)(2,1)S(1)}, bf16[176,256]{1,0:T(8,128)(2,1)S(1)}, u32[]{:S(2)}, u32[]{:S(2)}) collective-permute-start(bf16[176,256]{1,0:T(8,128)(2,1)S(1)} %add_convert_fusion.2), channel_id=1, source_target_pairs={{0,2},{1,3},{2,0},{3,1},{4,6},{5,7},{6,4},{7,5},{8,10},{9,11},{10,... | collective-permute-start | bytes 270344 | tf_op jit(solution)/shard_map/ppermute | solution.py:677
  51.4 2.9 %collective-permute-done.11 = bf16[176,256]{1,0:T(8,128)(2,1)S(1)} collective-permute-done((bf16[176,256]{1,0:T(8,128)(2,1)S(1)}, bf16[176,256]{1,0:T(8,128)(2,1)S(1)}, u32[]{:S(2)}, u32[]{:S(2)}) %collective-permute-start.11) | collective-permute-done | bytes 90144 | tf_op jit(solution)/shard_map/ppermute | solution.py:677
  54.4 2.8 %collective-permute-start.12 = (bf16[176,256]{1,0:T(8,128)(2,1)S(1)}, bf16[176,256]{1,0:T(8,128)(2,1)S(1)}, u32[]{:S(2)}, u32[]{:S(2)}) collective-permute-start(bf16[176,256]{1,0:T(8,128)(2,1)S(1)} %add_convert_fusion.1), channel_id=1, source_target_pairs={{0,4},{1,5},{2,6},{3,7},{4,0},{5,1},{6,2},{7,3},{8,12},{9,13},{10,... | collective-permute-start | bytes 270344 | tf_op jit(solution)/shard_map/ppermute | solution.py:677
  57.1 2.7 %collective-permute-done.12 = bf16[176,256]{1,0:T(8,128)(2,1)S(1)} collective-permute-done((bf16[176,256]{1,0:T(8,128)(2,1)S(1)}, bf16[176,256]{1,0:T(8,128)(2,1)S(1)}, u32[]{:S(2)}, u32[]{:S(2)}) %collective-permute-start.12) | collective-permute-done | bytes 90144 | tf_op jit(solution)/shard_map/ppermute | solution.py:677
  59.9 0.6 collective-permute-start.13
  60.5 1.0 %collective-permute-start.14 = (bf16[176,256]{1,0:T(8,128)(2,1)S(1)}, bf16[176,256]{1,0:T(8,128)(2,1)S(1)}, u32[]{:S(2)}, u32[]{:S(2)}) collective-permute-start(bf16[176,256]{1,0:T(8,128)(2,1)S(1)} %add_convert_fusion), channel_id=1, source_target_pairs={{0,16},{8,24},{16,0},{24,8},{1,17},{9,25},{17,1},{25,9},{2,18},{10... | collective-permute-start | bytes 270344 | tf_op jit(solution)/shard_map/ppermute | solution.py:677
  61.5 2.0 %collective-permute-start.15 = (bf16[176,256]{1,0:T(8,128)(2,1)S(1)}, bf16[176,256]{1,0:T(8,128)(2,1)S(1)}, u32[]{:S(2)}, u32[]{:S(2)}) collective-permute-start(bf16[176,256]{1,0:T(8,128)(2,1)S(1)} %add_convert_fusion), channel_id=1, source_target_pairs={{0,24},{8,16},{16,8},{24,0},{1,25},{9,17},{17,9},{25,1},{2,26},{10... | collective-permute-start | bytes 270344 | tf_op jit(solution)/shard_map/ppermute | solution.py:677
  63.5 1.0 %collective-permute-done.13 = bf16[176,256]{1,0:T(8,128)(2,1)S(1)} collective-permute-done((bf16[176,256]{1,0:T(8,128)(2,1)S(1)}, bf16[176,256]{1,0:T(8,128)(2,1)S(1)}, u32[]{:S(2)}, u32[]{:S(2)}) %collective-permute-start.13) | collective-permute-done | bytes 90144 | tf_op jit(solution)/shard_map/ppermute | solution.py:677
  64.5 0.5 collective-permute-done.14
  65.0 1.9 %collective-permute-done.15 = bf16[176,256]{1,0:T(8,128)(2,1)S(1)} collective-permute-done((bf16[176,256]{1,0:T(8,128)(2,1)S(1)}, bf16[176,256]{1,0:T(8,128)(2,1)S(1)}, u32[]{:S(2)}, u32[]{:S(2)}) %collective-permute-start.15) | collective-permute-done | bytes 90144 | tf_op jit(solution)/shard_map/ppermute | solution.py:677
  67.0 0.1 collective-permute-start.16
  67.0 0.9 %copy.33 = f32[12,64,128]{2,1,0:T(8,128)} copy(f32[12,64,128]{2,0,1:T(8,128)S(1)} %bitcast.46) | data formatting | bytes 786432
  67.9 0.8 %collective-permute-done.16.refs_2_ = bf16[704,256]{1,0:T(8,128)(2,1)S(1)} collective-permute-done((bf16[704,256]{1,0:T(8,128)(2,1)S(1)}, bf16[704,256]{1,0:T(8,128)(2,1)S(1)}, u32[]{:S(2)}, u32[]{:S(2)}) %collective-permute-start.16) | collective-permute-done | bytes 360480 | tf_op jit(solution)/shard_map/ppermute | solution.py:677
  68.7 2.0 %finish.1 = (f32[3,3,12,64]{3,2,1,0:T(8,128)}, f32[576,64]{1,0:T(8,128)}, f32[576,256]{1,0:T(8,128)}, f32[576,256]{1,0:T(8,128)}, f32[3,3,12,64]{3,2,1,0:T(8,128...) custom-call(s32[4]{0:T(128)S(1)} %pad_add_fusion.refs_0_, ...), custom_call_target="tpu_custom_call" | custom-call | tf_op jit(solution)/shard_map/finish/pallas_call | solution.py:909
  (34 shorter events, 0.4 us)
Async XLA Ops:
  1.4 2.8 %collective-permute-start = (bf16[2,16,268]{2,0,1:T(2,128)(2,1)S(1)}, bf16[2,16,268]{2,0,1:T(2,128)(2,1)S(1)}, u32[]{:S(2)}, u32[]{:S(2)}) collective-permute-start(bf16[2,16,268]{2,0,1:T(2,128)(2,1)S(1)} %pad.27), channel_id=1, source_target_pairs={{0,1},{1,0},{2,3},{3,2},{4,5},{5,4},{6,7},{7,6},{8,9},{9,8},{10,11... | collective-permute-start | bytes 51464 | tf_op jit(solution)/shard_map/ppermute | solution.py:677
  4.5 5.7 %collective-permute-start.1 = (bf16[2,4,16,76]{3,1,2,0:T(4,128)(2,1)S(1)}, bf16[2,4,16,76]{3,1,2,0:T(4,128)(2,1)S(1)}, u32[]{:S(2)}, u32[]{:S(2)}) collective-permute-start(bf16[2,4,16,76]{3,1,2,0:T(4,128)(2,1)S(1)} %get-tuple-element.102), channel_id=1, source_target_pairs={{0,4},{1,5},{2,6},{3,7},{4,0},{5,1},{6,2},{7,3},{8,12},{9,13},{10,... | collective-permute-start | bytes 58376 | tf_op jit(solution)/shard_map/ppermute | solution.py:677
  10.3 11.7 %copy-start.1 = (f32[256]{0:T(256)S(1)}, f32[256]{0:T(256)}, u32[]{:S(2)}) copy-start(f32[256]{0:T(256)} %param.20) | copy-start | bytes 3076
  10.3 11.7 %copy-start.2 = (f32[256]{0:T(256)S(1)}, f32[256]{0:T(256)}, u32[]{:S(2)}) copy-start(f32[256]{0:T(256)} %param.21) | copy-start | bytes 3076
  10.3 11.7 %copy-start.3 = (f32[64]{0:T(128)S(1)}, f32[64]{0:T(128)}, u32[]{:S(2)}) copy-start(f32[64]{0:T(128)} %param.18) | copy-start | bytes 772
  10.4 11.7 %copy-start.4 = (f32[64]{0:T(128)S(1)}, f32[64]{0:T(128)}, u32[]{:S(2)}) copy-start(f32[64]{0:T(128)} %param.19) | copy-start | bytes 772
  10.4 4.2 %collective-permute-start.3 = (bf16[12,12,64]{2,0,1:T(8,128)(2,1)S(1)}, bf16[12,12,64]{2,0,1:T(8,128)(2,1)S(1)}, u32[]{:S(2)}, u32[]{:S(2)}) collective-permute-start(bf16[12,12,64]{2,0,1:T(8,128)(2,1)S(1)} %get-tuple-element.96), channel_id=1, source_target_pairs={{0,1},{1,0},{2,3},{3,2},{4,5},{5,4},{6,7},{7,6},{8,9},{9,8},{10,11... | collective-permute-start | bytes 55304 | tf_op jit(solution)/shard_map/ppermute | solution.py:671
  10.4 4.1 %collective-permute-start.4 = (bf16[12,12,64]{2,0,1:T(8,128)(2,1)S(1)}, bf16[12,12,64]{2,0,1:T(8,128)(2,1)S(1)}, u32[]{:S(2)}, u32[]{:S(2)}) collective-permute-start(bf16[12,12,64]{2,0,1:T(8,128)(2,1)S(1)} %get-tuple-element.97), channel_id=1, source_target_pairs={{1,2},{2,1},{3,4},{4,3},{5,6},{6,5},{9,10},{10,9},{11,12},{12,11},... | collective-permute-start | bytes 55304 | tf_op jit(solution)/shard_map/ppermute | solution.py:672
  11.1 5.7 %collective-permute-start.2 = (bf16[1,8,16,76]{3,1,2,0:T(8,128)(2,1)S(1)}, bf16[1,8,16,76]{3,1,2,0:T(8,128)(2,1)S(1)}, u32[]{:S(2)}, u32[]{:S(2)}) collective-permute-start(bf16[1,8,16,76]{3,1,2,0:T(8,128)(2,1)S(1)} %get-tuple-element.100), channel_id=1, source_target_pairs={{0,2},{1,3},{2,0},{3,1},{4,6},{5,7},{6,4},{7,5},{8,10},{9,11},{10,... | collective-permute-start | bytes 58376 | tf_op jit(solution)/shard_map/ppermute | solution.py:677
  17.0 5.0 %collective-permute-start.5 = (bf16[24,16,128]{2,1,0:T(8,128)(2,1)S(1)}, bf16[24,16,128]{2,1,0:T(8,128)(2,1)S(1)}, u32[]{:S(2)}, u32[]{:S(2)}) collective-permute-start(bf16[24,16,128]{2,1,0:T(8,128)(2,1)S(1)} %get-tuple-element.89), channel_id=1, source_target_pairs={{0,8},{8,0},{16,24},{24,16},{1,9},{9,1},{17,25},{25,17},{2,10},{10... | collective-permute-start | bytes 294920 | tf_op jit(solution)/shard_map/ppermute | solution.py:671
  18.9 3.1 %collective-permute-start.6 = (bf16[24,16,128]{2,1,0:T(8,128)(2,1)S(1)}, bf16[24,16,128]{2,1,0:T(8,128)(2,1)S(1)}, u32[]{:S(2)}, u32[]{:S(2)}) collective-permute-start(bf16[24,16,128]{2,1,0:T(8,128)(2,1)S(1)} %get-tuple-element.88), channel_id=1, source_target_pairs={{8,16},{16,8},{9,17},{17,9},{10,18},{18,10},{11,19},{19,11},{12,20... | collective-permute-start | bytes 294920 | tf_op jit(solution)/shard_map/ppermute | solution.py:672
  22.1 23.1 %copy-start = (bf16[3,3,64,12]{2,3,1,0:T(8,128)(2,1)S(1)}, bf16[3,3,64,12]{2,3,1,0:T(8,128)(2,1)}, u32[]{:S(2)}) copy-start(bf16[3,3,64,12]{2,3,1,0:T(8,128)(2,1)} %param.17) | copy-start | bytes 41476
  22.1 23.1 %copy-start.5 = (f32[12]{0:T(128)S(1)}, f32[12]{0:T(128)}, u32[]{:S(2)}) copy-start(f32[12]{0:T(128)} %param.22) | copy-start | bytes 148
  35.9 1.7 %collective-permute-start.7 = (bf16[704,256]{1,0:T(8,128)(2,1)S(1)}, bf16[704,256]{1,0:T(8,128)(2,1)S(1)}, u32[]{:S(2)}, u32[]{:S(2)}) collective-permute-start(bf16[704,256]{1,0:T(8,128)(2,1)S(1)} %get-tuple-element.39), channel_id=1, source_target_pairs={{0,1},{1,0},{2,3},{3,2},{4,5},{5,4},{6,7},{7,6},{8,9},{9,8},{10,11... | collective-permute-start | bytes 1081352 | tf_op jit(solution)/shard_map/ppermute | solution.py:677
  37.8 11.2 %collective-permute-start.10 = (bf16[176,256]{1,0:T(8,128)(2,1)S(1)}, bf16[176,256]{1,0:T(8,128)(2,1)S(1)}, u32[]{:S(2)}, u32[]{:S(2)}) collective-permute-start(bf16[176,256]{1,0:T(8,128)(2,1)S(1)} %get-tuple-element.81), channel_id=1, source_target_pairs={{0,24},{8,16},{16,8},{24,0},{1,25},{9,17},{17,9},{25,1},{2,26},{10... | collective-permute-start | bytes 270344 | tf_op jit(solution)/shard_map/ppermute | solution.py:677
  40.7 9.0 %collective-permute-start.8 = (bf16[176,256]{1,0:T(8,128)(2,1)S(1)}, bf16[176,256]{1,0:T(8,128)(2,1)S(1)}, u32[]{:S(2)}, u32[]{:S(2)}) collective-permute-start(bf16[176,256]{1,0:T(8,128)(2,1)S(1)} %get-tuple-element.83), channel_id=1, source_target_pairs={{0,8},{8,0},{16,24},{24,16},{1,9},{9,1},{17,25},{25,17},{2,10},{10... | collective-permute-start | bytes 270344 | tf_op jit(solution)/shard_map/ppermute | solution.py:677
  45.1 4.6 %collective-permute-start.9 = (bf16[176,256]{1,0:T(8,128)(2,1)S(1)}, bf16[176,256]{1,0:T(8,128)(2,1)S(1)}, u32[]{:S(2)}, u32[]{:S(2)}) collective-permute-start(bf16[176,256]{1,0:T(8,128)(2,1)S(1)} %get-tuple-element.82), channel_id=1, source_target_pairs={{0,16},{8,24},{16,0},{24,8},{1,17},{9,25},{17,1},{25,9},{2,18},{10... | collective-permute-start | bytes 270344 | tf_op jit(solution)/shard_map/ppermute | solution.py:677
  49.8 4.6 %collective-permute-start.11 = (bf16[176,256]{1,0:T(8,128)(2,1)S(1)}, bf16[176,256]{1,0:T(8,128)(2,1)S(1)}, u32[]{:S(2)}, u32[]{:S(2)}) collective-permute-start(bf16[176,256]{1,0:T(8,128)(2,1)S(1)} %add_convert_fusion.2), channel_id=1, source_target_pairs={{0,2},{1,3},{2,0},{3,1},{4,6},{5,7},{6,4},{7,5},{8,10},{9,11},{10,... | collective-permute-start | bytes 270344 | tf_op jit(solution)/shard_map/ppermute | solution.py:677
  54.4 5.5 %collective-permute-start.12 = (bf16[176,256]{1,0:T(8,128)(2,1)S(1)}, bf16[176,256]{1,0:T(8,128)(2,1)S(1)}, u32[]{:S(2)}, u32[]{:S(2)}) collective-permute-start(bf16[176,256]{1,0:T(8,128)(2,1)S(1)} %add_convert_fusion.1), channel_id=1, source_target_pairs={{0,4},{1,5},{2,6},{3,7},{4,0},{5,1},{6,2},{7,3},{8,12},{9,13},{10,... | collective-permute-start | bytes 270344 | tf_op jit(solution)/shard_map/ppermute | solution.py:677
  59.9 4.6 %collective-permute-start.13 = (bf16[176,256]{1,0:T(8,128)(2,1)S(1)}, bf16[176,256]{1,0:T(8,128)(2,1)S(1)}, u32[]{:S(2)}, u32[]{:S(2)}) collective-permute-start(bf16[176,256]{1,0:T(8,128)(2,1)S(1)} %add_convert_fusion), channel_id=1, source_target_pairs={{0,8},{8,0},{16,24},{24,16},{1,9},{9,1},{17,25},{25,17},{2,10},{10... | collective-permute-start | bytes 270344 | tf_op jit(solution)/shard_map/ppermute | solution.py:677
  60.5 4.5 %collective-permute-start.14 = (bf16[176,256]{1,0:T(8,128)(2,1)S(1)}, bf16[176,256]{1,0:T(8,128)(2,1)S(1)}, u32[]{:S(2)}, u32[]{:S(2)}) collective-permute-start(bf16[176,256]{1,0:T(8,128)(2,1)S(1)} %add_convert_fusion), channel_id=1, source_target_pairs={{0,16},{8,24},{16,0},{24,8},{1,17},{9,25},{17,1},{25,9},{2,18},{10... | collective-permute-start | bytes 270344 | tf_op jit(solution)/shard_map/ppermute | solution.py:677
  61.5 5.4 %collective-permute-start.15 = (bf16[176,256]{1,0:T(8,128)(2,1)S(1)}, bf16[176,256]{1,0:T(8,128)(2,1)S(1)}, u32[]{:S(2)}, u32[]{:S(2)}) collective-permute-start(bf16[176,256]{1,0:T(8,128)(2,1)S(1)} %add_convert_fusion), channel_id=1, source_target_pairs={{0,24},{8,16},{16,8},{24,0},{1,25},{9,17},{17,9},{25,1},{2,26},{10... | collective-permute-start | bytes 270344 | tf_op jit(solution)/shard_map/ppermute | solution.py:677
  67.0 1.7 %collective-permute-start.16 = (bf16[704,256]{1,0:T(8,128)(2,1)S(1)}, bf16[704,256]{1,0:T(8,128)(2,1)S(1)}, u32[]{:S(2)}, u32[]{:S(2)}) collective-permute-start(bf16[704,256]{1,0:T(8,128)(2,1)S(1)} %pad_maximum_fusion.refs_1_), channel_id=1, source_target_pairs={{0,1},{1,0},{2,3},{3,2},{4,5},{5,4},{6,7},{7,6},{8,9},{9,8},{10,11... | collective-permute-start | bytes 1081352 | tf_op jit(solution)/shard_map/ppermute | solution.py:677

commit v5 on v4

--- a/solution.py
+++ b/solution.py
@@ -747,7 +747,7 @@
     def part(place):
         return lax.dynamic_slice_in_dim(value, place * size, size, 0)
 
-    terms = [swap(part(at_x ^ d).astype(BF), "gx", d) for d in range(1, gx)]
+    terms = [swap(part(at_x ^ d).astype(BF), "gx", d) for d in range(gx - 1, 0, -1)][::-1]
     terms, beside = lax.optimization_barrier((terms, beside))
     beside = beside.transpose(1, 0, 2)[:chans]
     block = tree([part(at_x)] + [term.astype(F32) for term in terms])

time: 71.2 us -> 71.2 us (level)
  no operation moved by 1% of the time
where the time goes in v5:
time: 71.2 us; the launch traced here: 70.7 us
  starting transfers between devices  26.4 us (37%)
  Pallas kernels  19.6 us (28%)
  waiting for transfers between devices  18.1 us (25%)
  local copies, waits for them, and re-layouts  4.88 us (7%)
  between operations  1.06 us (1%)
  other arithmetic  0.75 us (1%)
    ppermute x13, starting transfers between devices, swap(): lax.ppermute(block, axis, [(i, i ^ flip) for i in range(lax.axis_size(axi...  23.1 us
    ppermute x13, waiting for transfers between devices, swap(): lax.ppermute(block, axis, [(i, i ^ flip) for i in range(lax.axis_size(axi...  15.9 us
    pallas_call x1, Pallas kernels, local(): pl.pallas_call(gradients, out_shape=(pltpu.VMEM((half, 256), F32), pltpu....  13.8 us
    pallas_call x1, Pallas kernels, local(): pl.pallas_call(fine_field, out_shape=jax.ShapeDtypeStruct((4 * ROWS, 16,...  3.81 us
    unnamed x16, local copies, waits for them, and re-layouts  2.29 us
    ppermute x2, waiting for transfers between devices, exchange(): one = lax.ppermute(jnp.where(odd, first, last), axis, even_swap)  2.18 us
    pallas_call x1, Pallas kernels, local(): pl.pallas_call(lambda *refs: finish(chans, gx, *refs), out_shape=(out(3,...  2 us
    ppermute x2, starting transfers between devices, exchange(): one = lax.ppermute(jnp.where(odd, first, last), axis, even_swap)  1.98 us
  transfers between devices with their start and end apart: 17, of which 11 were waited for; matrix products, arithmetic and copies ran while one was open for 6% of the time, Pallas kernels for 5%

profile of v5, /device:TPU:0, one launch (start us, length us, event | category | flops | bytes accessed | tf_op | source)
XLA Modules:
  0.0 70.7 jit_solution(5649378703265699647)
XLA Ops:
  0.6 0.8 %pad.27 = bf16[2,16,268]{2,0,1:T(2,128)(2,1)S(1)} pad(bf16[2,12,256]{2,0,1:T(2,128)(2,1)} %bitcast.64, bf16[]{:T(256)} %constant.41.clone.1), padding=0_0x0_4x6_6 | pad | bytes 29442 | tf_op jit(solution)/shard_map/jit(_pad)/pad | solution.py:684
  1.4 0.5 collective-permute-start
  2.0 1.1 %fusion.9 = (bf16[12,64,12]{2,1,0:T(8,128)(2,1)S(1)}, bf16[12,64,12]{2,1,0:T(8,128)(2,1)S(1)}) fusion(bf16[12,64,128]{2,1,0:T(8,128)(2,1)} %param.23), kind=kLoop, calls=%fused_computation.47 | loop fusion | bytes 73728 | tf_op jit(solution)/shard_map/slice | solution.py:715
  3.1 1.1 %copy.37 = bf16[12,64,128]{2,0,1:T(8,128)(2,1)S(1)} copy(bf16[12,64,128]{2,1,0:T(8,128)(2,1)} %param.23) | data formatting | bytes 393216 | tf_op args[11]
  4.2 0.1 maximum_select_fusion.2
  4.3 0.1 slice_bitcast_fusion.3
  4.4 0.1 broadcast_select_fusion.7
  4.5 3.7 %collective-permute-start.1 = (bf16[2,4,16,76]{3,1,2,0:T(4,128)(2,1)S(1)}, bf16[2,4,16,76]{3,1,2,0:T(4,128)(2,1)S(1)}, u32[]{:S(2)}, u32[]{:S(2)}) collective-permute-start(bf16[2,4,16,76]{3,1,2,0:T(4,128)(2,1)S(1)} %get-tuple-element.102), channel_id=1, source_target_pairs={{0,4},{1,5},{2,6},{3,7},{4,0},{5,1},{6,2},{7,3},{8,12},{9,13},{10,... | collective-permute-start | bytes 58376 | tf_op jit(solution)/shard_map/ppermute | solution.py:677
  8.2 0.1 pad.29.refs_13_
  8.3 0.2 copy.35
  8.4 0.2 copy.34
  8.6 1.6 %collective-permute-done.1 = bf16[2,4,16,76]{3,1,2,0:T(4,128)(2,1)S(1)} collective-permute-done((bf16[2,4,16,76]{3,1,2,0:T(4,128)(2,1)S(1)}, bf16[2,4,16,76]{3,1,2,0:T(4,128)(2,1)S(1)}, u32[]{:S(2)}, u32[]{:S(2)}) %collective-permute-start.1) | collective-permute-done | bytes 19488 | tf_op jit(solution)/shard_map/ppermute | solution.py:677
  10.2 0.1 maximum_select_fusion
  10.3 0.0 copy-start.3
  10.4 0.1 collective-permute-start.3
  10.4 0.7 collective-permute-start.4
  11.1 3.4 %collective-permute-start.2 = (bf16[1,8,16,76]{3,1,2,0:T(8,128)(2,1)S(1)}, bf16[1,8,16,76]{3,1,2,0:T(8,128)(2,1)S(1)}, u32[]{:S(2)}, u32[]{:S(2)}) collective-permute-start(bf16[1,8,16,76]{3,1,2,0:T(8,128)(2,1)S(1)} %get-tuple-element.100), channel_id=1, source_target_pairs={{0,2},{1,3},{2,0},{3,1},{4,6},{5,7},{6,4},{7,5},{8,10},{9,11},{10,... | collective-permute-start | bytes 58376 | tf_op jit(solution)/shard_map/ppermute | solution.py:677
  14.6 0.3 copy.32
  14.9 1.9 %collective-permute-done.2 = bf16[1,8,16,76]{3,1,2,0:T(8,128)(2,1)S(1)} collective-permute-done((bf16[1,8,16,76]{3,1,2,0:T(8,128)(2,1)S(1)}, bf16[1,8,16,76]{3,1,2,0:T(8,128)(2,1)S(1)}, u32[]{:S(2)}, u32[]{:S(2)}) %collective-permute-start.2) | collective-permute-done | bytes 19488 | tf_op jit(solution)/shard_map/ppermute | solution.py:677
  16.9 0.1 broadcast_select_fusion.2
  17.0 1.9 %collective-permute-start.5 = (bf16[24,16,128]{2,1,0:T(8,128)(2,1)S(1)}, bf16[24,16,128]{2,1,0:T(8,128)(2,1)S(1)}, u32[]{:S(2)}, u32[]{:S(2)}) collective-permute-start(bf16[24,16,128]{2,1,0:T(8,128)(2,1)S(1)} %get-tuple-element.89), channel_id=1, source_target_pairs={{0,8},{8,0},{16,24},{24,16},{1,9},{9,1},{17,25},{25,17},{2,10},{10... | collective-permute-start | bytes 294920 | tf_op jit(solution)/shard_map/ppermute | solution.py:671
  18.9 0.7 collective-permute-start.6
  19.6 0.1 pad_add_fusion.refs_0_
  19.7 0.1 pad.30
  19.8 0.1 pad.33.refs_14_
  19.8 2.2 %collective-permute-done.5 = bf16[24,16,128]{2,1,0:T(8,128)(2,1)S(1)} collective-permute-done((bf16[24,16,128]{2,1,0:T(8,128)(2,1)S(1)}, bf16[24,16,128]{2,1,0:T(8,128)(2,1)S(1)}, u32[]{:S(2)}, u32[]{:S(2)}) %collective-permute-start.5) | collective-permute-done | bytes 98336 | tf_op jit(solution)/shard_map/ppermute | solution.py:671
  22.1 13.8 %gradients.1 = (f32[704,256]{1,0:T(8,128)S(1)}, bf16[704,256]{1,0:T(8,128)(2,1)S(1)}, bf16[896,1024]{1,0:T(8,128)(2,1)}, bf16[256,256]{1,0:T(8,128)(2,1)S(1)}, bf16[256,256]{1,0:T(8,128)(2,1)S(1)}) custom-call(s32[4]{0:T(128)S(1)} %pad_add_fusion.refs_0_, bf16[16,16,128]{2,1,0:T(8,128)(2,1)S(1)} %pad.28.refs_1_, ...), custom_call_target="tpu_custom_call" | custom-call | tf_op jit(solution)/shard_map/gradients/pallas_call | solution.py:862
  35.9 0.1 collective-permute-start.7
  36.0 1.6 %collective-permute-done.7 = bf16[704,256]{1,0:T(8,128)(2,1)S(1)} collective-permute-done((bf16[704,256]{1,0:T(8,128)(2,1)S(1)}, bf16[704,256]{1,0:T(8,128)(2,1)S(1)}, u32[]{:S(2)}, u32[]{:S(2)}) %collective-permute-start.7) | collective-permute-done | bytes 360480 | tf_op jit(solution)/shard_map/ppermute | solution.py:677
  37.6 0.1 convert_add_fusion
  37.8 3.0 %collective-permute-start.10 = (bf16[176,256]{1,0:T(8,128)(2,1)S(1)}, bf16[176,256]{1,0:T(8,128)(2,1)S(1)}, u32[]{:S(2)}, u32[]{:S(2)}) collective-permute-start(bf16[176,256]{1,0:T(8,128)(2,1)S(1)} %get-tuple-element.81), channel_id=1, source_target_pairs={{0,24},{8,16},{16,8},{24,0},{1,25},{9,17},{17,9},{25,1},{2,26},{10... | collective-permute-start | bytes 270344 | tf_op jit(solution)/shard_map/ppermute | solution.py:677
  40.7 4.4 %collective-permute-start.8 = (bf16[176,256]{1,0:T(8,128)(2,1)S(1)}, bf16[176,256]{1,0:T(8,128)(2,1)S(1)}, u32[]{:S(2)}, u32[]{:S(2)}) collective-permute-start(bf16[176,256]{1,0:T(8,128)(2,1)S(1)} %get-tuple-element.83), channel_id=1, source_target_pairs={{0,8},{8,0},{16,24},{24,16},{1,9},{9,1},{17,25},{25,17},{2,10},{10... | collective-permute-start | bytes 270344 | tf_op jit(solution)/shard_map/ppermute | solution.py:677
  45.2 3.8 %fine.1 = f32[64,16,128]{2,1,0:T(8,128)S(1)} custom-call(bf16[896,1024]{1,0:T(8,128)(2,1)} %get-tuple-element.40.kept_hbm, bf16[3,3,12,64]{3,2,1,0:T(8,128)(2,1)S(1)} %bitcast.48, f32[1,12]{1,0:T(1,128)S(1)} %bitcast.53), custom_call_target="tpu_custom_call" | custom-call | tf_op jit(solution)/shard_map/fine/pallas_call | solution.py:889
  49.0 0.7 %collective-permute-done.8 = bf16[176,256]{1,0:T(8,128)(2,1)S(1)} collective-permute-done((bf16[176,256]{1,0:T(8,128)(2,1)S(1)}, bf16[176,256]{1,0:T(8,128)(2,1)S(1)}, u32[]{:S(2)}, u32[]{:S(2)}) %collective-permute-start.8) | collective-permute-done | bytes 90144 | tf_op jit(solution)/shard_map/ppermute | solution.py:677
  49.8 1.7 %collective-permute-start.11 = (bf16[176,256]{1,0:T(8,128)(2,1)S(1)}, bf16[176,256]{1,0:T(8,128)(2,1)S(1)}, u32[]{:S(2)}, u32[]{:S(2)}) collective-permute-start(bf16[176,256]{1,0:T(8,128)(2,1)S(1)} %add_convert_fusion.2), channel_id=1, source_target_pairs={{0,2},{1,3},{2,0},{3,1},{4,6},{5,7},{6,4},{7,5},{8,10},{9,11},{10,... | collective-permute-start | bytes 270344 | tf_op jit(solution)/shard_map/ppermute | solution.py:677
  51.4 2.9 %collective-permute-done.11 = bf16[176,256]{1,0:T(8,128)(2,1)S(1)} collective-permute-done((bf16[176,256]{1,0:T(8,128)(2,1)S(1)}, bf16[176,256]{1,0:T(8,128)(2,1)S(1)}, u32[]{:S(2)}, u32[]{:S(2)}) %collective-permute-start.11) | collective-permute-done | bytes 90144 | tf_op jit(solution)/shard_map/ppermute | solution.py:677
  54.4 2.8 %collective-permute-start.12 = (bf16[176,256]{1,0:T(8,128)(2,1)S(1)}, bf16[176,256]{1,0:T(8,128)(2,1)S(1)}, u32[]{:S(2)}, u32[]{:S(2)}) collective-permute-start(bf16[176,256]{1,0:T(8,128)(2,1)S(1)} %add_convert_fusion.1), channel_id=1, source_target_pairs={{0,4},{1,5},{2,6},{3,7},{4,0},{5,1},{6,2},{7,3},{8,12},{9,13},{10,... | collective-permute-start | bytes 270344 | tf_op jit(solution)/shard_map/ppermute | solution.py:677
  57.1 2.7 %collective-permute-done.12 = bf16[176,256]{1,0:T(8,128)(2,1)S(1)} collective-permute-done((bf16[176,256]{1,0:T(8,128)(2,1)S(1)}, bf16[176,256]{1,0:T(8,128)(2,1)S(1)}, u32[]{:S(2)}, u32[]{:S(2)}) %collective-permute-start.12) | collective-permute-done | bytes 90144 | tf_op jit(solution)/shard_map/ppermute | solution.py:677
  59.9 0.6 collective-permute-start.13
  60.5 1.0 %collective-permute-start.14 = (bf16[176,256]{1,0:T(8,128)(2,1)S(1)}, bf16[176,256]{1,0:T(8,128)(2,1)S(1)}, u32[]{:S(2)}, u32[]{:S(2)}) collective-permute-start(bf16[176,256]{1,0:T(8,128)(2,1)S(1)} %add_convert_fusion), channel_id=1, source_target_pairs={{0,16},{8,24},{16,0},{24,8},{1,17},{9,25},{17,1},{25,9},{2,18},{10... | collective-permute-start | bytes 270344 | tf_op jit(solution)/shard_map/ppermute | solution.py:677
  61.5 2.0 %collective-permute-start.15 = (bf16[176,256]{1,0:T(8,128)(2,1)S(1)}, bf16[176,256]{1,0:T(8,128)(2,1)S(1)}, u32[]{:S(2)}, u32[]{:S(2)}) collective-permute-start(bf16[176,256]{1,0:T(8,128)(2,1)S(1)} %add_convert_fusion), channel_id=1, source_target_pairs={{0,24},{8,16},{16,8},{24,0},{1,25},{9,17},{17,9},{25,1},{2,26},{10... | collective-permute-start | bytes 270344 | tf_op jit(solution)/shard_map/ppermute | solution.py:677
  63.5 1.0 %collective-permute-done.13 = bf16[176,256]{1,0:T(8,128)(2,1)S(1)} collective-permute-done((bf16[176,256]{1,0:T(8,128)(2,1)S(1)}, bf16[176,256]{1,0:T(8,128)(2,1)S(1)}, u32[]{:S(2)}, u32[]{:S(2)}) %collective-permute-start.13) | collective-permute-done | bytes 90144 | tf_op jit(solution)/shard_map/ppermute | solution.py:677
  64.5 0.5 collective-permute-done.14
  65.0 1.9 %collective-permute-done.15 = bf16[176,256]{1,0:T(8,128)(2,1)S(1)} collective-permute-done((bf16[176,256]{1,0:T(8,128)(2,1)S(1)}, bf16[176,256]{1,0:T(8,128)(2,1)S(1)}, u32[]{:S(2)}, u32[]{:S(2)}) %collective-permute-start.15) | collective-permute-done | bytes 90144 | tf_op jit(solution)/shard_map/ppermute | solution.py:677
  67.0 0.1 collective-permute-start.16
  67.0 0.9 %copy.33 = f32[12,64,128]{2,1,0:T(8,128)} copy(f32[12,64,128]{2,0,1:T(8,128)S(1)} %bitcast.46) | data formatting | bytes 786432
  67.9 0.8 %collective-permute-done.16.refs_2_ = bf16[704,256]{1,0:T(8,128)(2,1)S(1)} collective-permute-done((bf16[704,256]{1,0:T(8,128)(2,1)S(1)}, bf16[704,256]{1,0:T(8,128)(2,1)S(1)}, u32[]{:S(2)}, u32[]{:S(2)}) %collective-permute-start.16) | collective-permute-done | bytes 360480 | tf_op jit(solution)/shard_map/ppermute | solution.py:677
  68.7 2.0 %finish.1 = (f32[3,3,12,64]{3,2,1,0:T(8,128)}, f32[576,64]{1,0:T(8,128)}, f32[576,256]{1,0:T(8,128)}, f32[576,256]{1,0:T(8,128)}, f32[3,3,12,64]{3,2,1,0:T(8,128...) custom-call(s32[4]{0:T(128)S(1)} %pad_add_fusion.refs_0_, ...), custom_call_target="tpu_custom_call" | custom-call | tf_op jit(solution)/shard_map/finish/pallas_call | solution.py:909
  (34 shorter events, 0.4 us)
Async XLA Ops:
  1.4 2.8 %collective-permute-start = (bf16[2,16,268]{2,0,1:T(2,128)(2,1)S(1)}, bf16[2,16,268]{2,0,1:T(2,128)(2,1)S(1)}, u32[]{:S(2)}, u32[]{:S(2)}) collective-permute-start(bf16[2,16,268]{2,0,1:T(2,128)(2,1)S(1)} %pad.27), channel_id=1, source_target_pairs={{0,1},{1,0},{2,3},{3,2},{4,5},{5,4},{6,7},{7,6},{8,9},{9,8},{10,11... | collective-permute-start | bytes 51464 | tf_op jit(solution)/shard_map/ppermute | solution.py:677
  4.5 5.7 %collective-permute-start.1 = (bf16[2,4,16,76]{3,1,2,0:T(4,128)(2,1)S(1)}, bf16[2,4,16,76]{3,1,2,0:T(4,128)(2,1)S(1)}, u32[]{:S(2)}, u32[]{:S(2)}) collective-permute-start(bf16[2,4,16,76]{3,1,2,0:T(4,128)(2,1)S(1)} %get-tuple-element.102), channel_id=1, source_target_pairs={{0,4},{1,5},{2,6},{3,7},{4,0},{5,1},{6,2},{7,3},{8,12},{9,13},{10,... | collective-permute-start | bytes 58376 | tf_op jit(solution)/shard_map/ppermute | solution.py:677
  10.3 11.7 %copy-start.1 = (f32[256]{0:T(256)S(1)}, f32[256]{0:T(256)}, u32[]{:S(2)}) copy-start(f32[256]{0:T(256)} %param.20) | copy-start | bytes 3076
  10.3 11.7 %copy-start.2 = (f32[256]{0:T(256)S(1)}, f32[256]{0:T(256)}, u32[]{:S(2)}) copy-start(f32[256]{0:T(256)} %param.21) | copy-start | bytes 3076
  10.3 11.7 %copy-start.3 = (f32[64]{0:T(128)S(1)}, f32[64]{0:T(128)}, u32[]{:S(2)}) copy-start(f32[64]{0:T(128)} %param.18) | copy-start | bytes 772
  10.4 11.7 %copy-start.4 = (f32[64]{0:T(128)S(1)}, f32[64]{0:T(128)}, u32[]{:S(2)}) copy-start(f32[64]{0:T(128)} %param.19) | copy-start | bytes 772
  10.4 4.2 %collective-permute-start.3 = (bf16[12,12,64]{2,0,1:T(8,128)(2,1)S(1)}, bf16[12,12,64]{2,0,1:T(8,128)(2,1)S(1)}, u32[]{:S(2)}, u32[]{:S(2)}) collective-permute-start(bf16[12,12,64]{2,0,1:T(8,128)(2,1)S(1)} %get-tuple-element.96), channel_id=1, source_target_pairs={{0,1},{1,0},{2,3},{3,2},{4,5},{5,4},{6,7},{7,6},{8,9},{9,8},{10,11... | collective-permute-start | bytes 55304 | tf_op jit(solution)/shard_map/ppermute | solution.py:671
  10.4 4.1 %collective-permute-start.4 = (bf16[12,12,64]{2,0,1:T(8,128)(2,1)S(1)}, bf16[12,12,64]{2,0,1:T(8,128)(2,1)S(1)}, u32[]{:S(2)}, u32[]{:S(2)}) collective-permute-start(bf16[12,12,64]{2,0,1:T(8,128)(2,1)S(1)} %get-tuple-element.97), channel_id=1, source_target_pairs={{1,2},{2,1},{3,4},{4,3},{5,6},{6,5},{9,10},{10,9},{11,12},{12,11},... | collective-permute-start | bytes 55304 | tf_op jit(solution)/shard_map/ppermute | solution.py:672
  11.1 5.7 %collective-permute-start.2 = (bf16[1,8,16,76]{3,1,2,0:T(8,128)(2,1)S(1)}, bf16[1,8,16,76]{3,1,2,0:T(8,128)(2,1)S(1)}, u32[]{:S(2)}, u32[]{:S(2)}) collective-permute-start(bf16[1,8,16,76]{3,1,2,0:T(8,128)(2,1)S(1)} %get-tuple-element.100), channel_id=1, source_target_pairs={{0,2},{1,3},{2,0},{3,1},{4,6},{5,7},{6,4},{7,5},{8,10},{9,11},{10,... | collective-permute-start | bytes 58376 | tf_op jit(solution)/shard_map/ppermute | solution.py:677
  17.0 5.0 %collective-permute-start.5 = (bf16[24,16,128]{2,1,0:T(8,128)(2,1)S(1)}, bf16[24,16,128]{2,1,0:T(8,128)(2,1)S(1)}, u32[]{:S(2)}, u32[]{:S(2)}) collective-permute-start(bf16[24,16,128]{2,1,0:T(8,128)(2,1)S(1)} %get-tuple-element.89), channel_id=1, source_target_pairs={{0,8},{8,0},{16,24},{24,16},{1,9},{9,1},{17,25},{25,17},{2,10},{10... | collective-permute-start | bytes 294920 | tf_op jit(solution)/shard_map/ppermute | solution.py:671
  18.9 3.1 %collective-permute-start.6 = (bf16[24,16,128]{2,1,0:T(8,128)(2,1)S(1)}, bf16[24,16,128]{2,1,0:T(8,128)(2,1)S(1)}, u32[]{:S(2)}, u32[]{:S(2)}) collective-permute-start(bf16[24,16,128]{2,1,0:T(8,128)(2,1)S(1)} %get-tuple-element.88), channel_id=1, source_target_pairs={{8,16},{16,8},{9,17},{17,9},{10,18},{18,10},{11,19},{19,11},{12,20... | collective-permute-start | bytes 294920 | tf_op jit(solution)/shard_map/ppermute | solution.py:672
  22.1 23.1 %copy-start = (bf16[3,3,64,12]{2,3,1,0:T(8,128)(2,1)S(1)}, bf16[3,3,64,12]{2,3,1,0:T(8,128)(2,1)}, u32[]{:S(2)}) copy-start(bf16[3,3,64,12]{2,3,1,0:T(8,128)(2,1)} %param.17) | copy-start | bytes 41476
  22.1 23.1 %copy-start.5 = (f32[12]{0:T(128)S(1)}, f32[12]{0:T(128)}, u32[]{:S(2)}) copy-start(f32[12]{0:T(128)} %param.22) | copy-start | bytes 148
  35.9 1.7 %collective-permute-start.7 = (bf16[704,256]{1,0:T(8,128)(2,1)S(1)}, bf16[704,256]{1,0:T(8,128)(2,1)S(1)}, u32[]{:S(2)}, u32[]{:S(2)}) collective-permute-start(bf16[704,256]{1,0:T(8,128)(2,1)S(1)} %get-tuple-element.39), channel_id=1, source_target_pairs={{0,1},{1,0},{2,3},{3,2},{4,5},{5,4},{6,7},{7,6},{8,9},{9,8},{10,11... | collective-permute-start | bytes 1081352 | tf_op jit(solution)/shard_map/ppermute | solution.py:677
  37.8 11.2 %collective-permute-start.10 = (bf16[176,256]{1,0:T(8,128)(2,1)S(1)}, bf16[176,256]{1,0:T(8,128)(2,1)S(1)}, u32[]{:S(2)}, u32[]{:S(2)}) collective-permute-start(bf16[176,256]{1,0:T(8,128)(2,1)S(1)} %get-tuple-element.81), channel_id=1, source_target_pairs={{0,24},{8,16},{16,8},{24,0},{1,25},{9,17},{17,9},{25,1},{2,26},{10... | collective-permute-start | bytes 270344 | tf_op jit(solution)/shard_map/ppermute | solution.py:677
  40.7 9.0 %collective-permute-start.8 = (bf16[176,256]{1,0:T(8,128)(2,1)S(1)}, bf16[176,256]{1,0:T(8,128)(2,1)S(1)}, u32[]{:S(2)}, u32[]{:S(2)}) collective-permute-start(bf16[176,256]{1,0:T(8,128)(2,1)S(1)} %get-tuple-element.83), channel_id=1, source_target_pairs={{0,8},{8,0},{16,24},{24,16},{1,9},{9,1},{17,25},{25,17},{2,10},{10... | collective-permute-start | bytes 270344 | tf_op jit(solution)/shard_map/ppermute | solution.py:677
  45.1 4.6 %collective-permute-start.9 = (bf16[176,256]{1,0:T(8,128)(2,1)S(1)}, bf16[176,256]{1,0:T(8,128)(2,1)S(1)}, u32[]{:S(2)}, u32[]{:S(2)}) collective-permute-start(bf16[176,256]{1,0:T(8,128)(2,1)S(1)} %get-tuple-element.82), channel_id=1, source_target_pairs={{0,16},{8,24},{16,0},{24,8},{1,17},{9,25},{17,1},{25,9},{2,18},{10... | collective-permute-start | bytes 270344 | tf_op jit(solution)/shard_map/ppermute | solution.py:677
  49.8 4.6 %collective-permute-start.11 = (bf16[176,256]{1,0:T(8,128)(2,1)S(1)}, bf16[176,256]{1,0:T(8,128)(2,1)S(1)}, u32[]{:S(2)}, u32[]{:S(2)}) collective-permute-start(bf16[176,256]{1,0:T(8,128)(2,1)S(1)} %add_convert_fusion.2), channel_id=1, source_target_pairs={{0,2},{1,3},{2,0},{3,1},{4,6},{5,7},{6,4},{7,5},{8,10},{9,11},{10,... | collective-permute-start | bytes 270344 | tf_op jit(solution)/shard_map/ppermute | solution.py:677
  54.4 5.5 %collective-permute-start.12 = (bf16[176,256]{1,0:T(8,128)(2,1)S(1)}, bf16[176,256]{1,0:T(8,128)(2,1)S(1)}, u32[]{:S(2)}, u32[]{:S(2)}) collective-permute-start(bf16[176,256]{1,0:T(8,128)(2,1)S(1)} %add_convert_fusion.1), channel_id=1, source_target_pairs={{0,4},{1,5},{2,6},{3,7},{4,0},{5,1},{6,2},{7,3},{8,12},{9,13},{10,... | collective-permute-start | bytes 270344 | tf_op jit(solution)/shard_map/ppermute | solution.py:677
  59.9 4.6 %collective-permute-start.13 = (bf16[176,256]{1,0:T(8,128)(2,1)S(1)}, bf16[176,256]{1,0:T(8,128)(2,1)S(1)}, u32[]{:S(2)}, u32[]{:S(2)}) collective-permute-start(bf16[176,256]{1,0:T(8,128)(2,1)S(1)} %add_convert_fusion), channel_id=1, source_target_pairs={{0,8},{8,0},{16,24},{24,16},{1,9},{9,1},{17,25},{25,17},{2,10},{10... | collective-permute-start | bytes 270344 | tf_op jit(solution)/shard_map/ppermute | solution.py:677
  60.5 4.5 %collective-permute-start.14 = (bf16[176,256]{1,0:T(8,128)(2,1)S(1)}, bf16[176,256]{1,0:T(8,128)(2,1)S(1)}, u32[]{:S(2)}, u32[]{:S(2)}) collective-permute-start(bf16[176,256]{1,0:T(8,128)(2,1)S(1)} %add_convert_fusion), channel_id=1, source_target_pairs={{0,16},{8,24},{16,0},{24,8},{1,17},{9,25},{17,1},{25,9},{2,18},{10... | collective-permute-start | bytes 270344 | tf_op jit(solution)/shard_map/ppermute | solution.py:677
  61.5 5.4 %collective-permute-start.15 = (bf16[176,256]{1,0:T(8,128)(2,1)S(1)}, bf16[176,256]{1,0:T(8,128)(2,1)S(1)}, u32[]{:S(2)}, u32[]{:S(2)}) collective-permute-start(bf16[176,256]{1,0:T(8,128)(2,1)S(1)} %add_convert_fusion), channel_id=1, source_target_pairs={{0,24},{8,16},{16,8},{24,0},{1,25},{9,17},{17,9},{25,1},{2,26},{10... | collective-permute-start | bytes 270344 | tf_op jit(solution)/shard_map/ppermute | solution.py:677
  67.0 1.7 %collective-permute-start.16 = (bf16[704,256]{1,0:T(8,128)(2,1)S(1)}, bf16[704,256]{1,0:T(8,128)(2,1)S(1)}, u32[]{:S(2)}, u32[]{:S(2)}) collective-permute-start(bf16[704,256]{1,0:T(8,128)(2,1)S(1)} %pad_maximum_fusion.refs_1_), channel_id=1, source_target_pairs={{0,1},{1,0},{2,3},{3,2},{4,5},{5,4},{6,7},{7,6},{8,9},{9,8},{10,11... | collective-permute-start | bytes 1081352 | tf_op jit(solution)/shard_map/ppermute | solution.py:677
